TPU v7x, 32 devices: a whole 2x2x4 slice. The times are simulated.
32 devices in a mesh: grp: 2 (over y), row: 4 (over z), mic: 2 (over x), orient: 2 (over core).
Axes of the slice: x: 2, y: 2, z: 4, core: 2. Of those that a mesh axis runs over, the one named last changes fastest.
Arguments:
- spectra: bfloat16 [8, 2, 2048, 2048], P(('grp', 'mic'), None, 'row'), parts along dimension 0, may hold values from -6 to 6
- bank: bfloat16 [8, 384, 384], replicated, as said below
- orient_index: int32 [16], P('grp'), parts along dimension 0, may hold values from 0 to 7, as said below
Outputs:
- peak_map: float32 [8, 4, 512, 128], P(('grp', 'mic'), 'row'), parts along dimension 0
- power_map: float32 [8, 4, 512, 128], P(('grp', 'mic'), 'row'), parts along dimension 0
There are 2 independent parts, one for each index of `grp`. A program takes and returns all parts, laid end to end along the dimension named above; an argument that names none is the same for every part. Nothing has to cross between parts.
Inputs may be any that keep to these rules, and one draw needn't show every extreme that they name: `bank`: projection images of the table. `orient_index`: each entry names one projection of the table; entries may repeat.
All inputs are finite; a program needn't handle non-finite values.
Results may differ from a plain program's by a relative error of at most 0.0051.
Values may be sent and summed in bfloat16 or wider, within the bound.
No kernel may reach another device: no remote copies, remote signals or barrier semaphores. Data moves between devices by JAX's collectives and lax.ppermute only.
A program may use at most 128 MiB of HBM per device.

v0:
```python
import math

import jax
import jax.numpy as jnp
from jax import lax
from jax.sharding import PartitionSpec as P

WCOLS = 128


two_pi = 2.0 * math.pi


def swapped(shard, axis, apart):
    return lax.ppermute(shard, axis, [(i, i ^ 1 << apart) for i in range(lax.axis_size(axis))])


def merged_2(part, axis, combine):
    gathered = jax.tree.map(lambda a: lax.all_gather(a, axis), part)

    def take(source):
        return jax.tree.map(lambda a: lax.dynamic_index_in_dim(a, source, 0, False), gathered)

    return lax.fori_loop(
        1, lax.axis_size(axis), lambda source, state: combine(state, take(source)), take(0)
    )


def phase_table(row_start, row_count, col_start, col_count, period):
    row_ids = row_start + jnp.arange(row_count, dtype=jnp.int32)
    col_ids = col_start + jnp.arange(col_count, dtype=jnp.int32)
    wrapped = row_ids[:, None] * col_ids[None, :] % period
    angles = wrapped.astype(jnp.float32) * (two_pi / period)
    return (jnp.cos(angles), jnp.sin(angles))


def normalize(picture):
    values = picture.astype(jnp.float32)
    centred = values - jnp.mean(values)
    factor = lax.rsqrt(jnp.mean(centred * centred) + 1e-06)
    return (centred * factor).astype(jnp.bfloat16)


def reverse_bits(number, digits):
    result = number * 0
    for digit in range(digits):
        result = result + number // (1 << digit) % 2 * (1 << digits - 1 - digit)
    return result


def combine_maps(first_pair, second_pair):
    return (jnp.maximum(first_pair[0], second_pair[0]), first_pair[1] + second_pair[1])


def shards(spectra, bank, orient_index):
    mic_count = spectra.shape[0]
    band_rows = spectra.shape[2]
    length = spectra.shape[3]
    tsize_px = bank.shape[1]
    row_devices = lax.axis_size("row")
    row_place = lax.axis_index("row")
    mic_devices = lax.axis_size("mic")
    mic_place = lax.axis_index("mic")
    share_count = orient_index.shape[0] // lax.axis_size("orient")
    chosen = lax.dynamic_slice_in_dim(
        orient_index, lax.axis_index("orient") * share_count, share_count
    )
    templates = jax.vmap(normalize)(bank[chosen])
    cos_y, sin_y = phase_table(row_place * band_rows, band_rows, 0, tsize_px, length)
    left_table = jnp.concatenate([cos_y.astype(jnp.bfloat16), -sin_y.astype(jnp.bfloat16)], 0)
    rowpass = jnp.einsum(
        "ay,oyx->oax", left_table, templates, preferred_element_type=jnp.float32
    ).astype(jnp.bfloat16)
    kx_share = length // mic_devices
    cos_x, sin_x = phase_table(0, tsize_px, mic_place * kx_share, kx_share, length)
    right_table = jnp.concatenate([cos_x.astype(jnp.bfloat16), sin_x.astype(jnp.bfloat16)], 1)
    mixed = jnp.einsum("oax,xk->oak", rowpass, right_table, preferred_element_type=jnp.float32)
    upper_rows = mixed[:, :band_rows]
    lower_rows = mixed[:, band_rows:]
    spec_re = upper_rows[:, :, :kx_share] + lower_rows[:, :, kx_share:]
    spec_im = lower_rows[:, :, :kx_share] - upper_rows[:, :, kx_share:]
    own_spectra = jnp.stack([spec_re, spec_im], 1).astype(jnp.bfloat16)
    piece = lax.all_gather(own_spectra, "mic", axis=3, tiled=True)
    width = piece.shape[3]
    cos_e, sin_e = phase_table(jnp.int32(0), width, 0, WCOLS, length)
    row_table = jnp.concatenate([cos_e.astype(jnp.bfloat16), sin_e.astype(jnp.bfloat16)], 1)
    updates = []
    for orient_pos in range(piece.shape[0]):
        tmpl_re = piece[orient_pos, 0].astype(jnp.float32)
        tmpl_im = piece[orient_pos, 1].astype(jnp.float32)
        mic_re = spectra[:, 0].astype(jnp.float32)
        mic_im = spectra[:, 1].astype(jnp.float32)
        prod_re = mic_re * tmpl_re + mic_im * tmpl_im
        prod_im = mic_im * tmpl_re - mic_re * tmpl_im
        product = jnp.stack([prod_re, prod_im], 1).astype(jnp.bfloat16)
        summed = jnp.einsum("mcbk,kw->mcbw", product, row_table, preferred_element_type=jnp.float32)
        part_re = summed[:, 0, :, :WCOLS] - summed[:, 1, :, WCOLS:]
        part_im = summed[:, 0, :, WCOLS:] + summed[:, 1, :, :WCOLS]
        updates.append(jnp.stack([part_re, part_im], 1))
    partial_value = jnp.stack(updates, 1)
    item_total = mic_count * share_count
    flat = partial_value.reshape(item_total, 2, band_rows, WCOLS)
    sections = row_devices.bit_length() - 1
    values = flat
    for bit in reversed(range(sections)):
        half_span = 1 << bit
        partner = swapped(values, "row", bit)
        upper_side = row_place // half_span % 2
        offset = row_place % half_span
        twist = offset.astype(jnp.float32) * (math.pi / half_span)
        twist_re = jnp.cos(twist)
        twist_im = jnp.sin(twist)
        differ = partner - values
        rot_re = differ[:, 0] * twist_re - differ[:, 1] * twist_im
        rot_im = differ[:, 0] * twist_im + differ[:, 1] * twist_re
        rotated = jnp.stack([rot_re, rot_im], 1)
        values = jnp.where(upper_side == 1, rotated, values + partner)
    residue = reverse_bits(row_place, sections)
    pixel_rows = residue + row_devices * jnp.arange(band_rows, dtype=jnp.int32)
    local_rows = jnp.arange(band_rows, dtype=jnp.int32)
    wrapped_col = pixel_rows[:, None] * local_rows[None, :] % length
    col_angles = wrapped_col.astype(jnp.float32) * (two_pi / length)
    column_table = jnp.stack([jnp.cos(col_angles), -jnp.sin(col_angles)], 1)
    corr = jnp.einsum("tcj,icjw->itw", column_table, values, precision=lax.Precision.HIGHEST)
    corr = corr * (1.0 / (length * tsize_px))
    corr = corr.reshape(mic_count, share_count, band_rows, WCOLS)
    peak_part = jnp.max(corr, axis=1)
    power_part = jnp.sum(corr * corr, axis=1)
    merged = merged_2((peak_part, power_part), "orient", combine_maps)
    return (merged[0][:, None], merged[1][:, None])


def solution(mesh):
    return jax.shard_map(
        shards,
        mesh=mesh,
        in_specs=(P(("grp", "mic"), None, "row", None), P(), P("grp")),
        out_specs=(P(("grp", "mic"), "row", None, None), P(("grp", "mic"), "row", None, None)),
        check_vma=False,
    )
```

profile of v0, /device:TPU:0, one launch (start us, length us, event | category | flops | bytes accessed | tf_op | source)
XLA Modules:
  0.0 665.7 jit_solution(2914393372446859276)
XLA Ops:
  7.2 3.8 cosine_convert_fusion.2
  11.0 3.8 fusion.100
  17.3 6.5 cosine_convert_fusion
  23.8 18.0 %fusion.40 = f32[4,1024,2048]{2,1,0:T(8,128)} fusion(bf16[384,1024]{1,0:T(8,128)(2,1)S(1)} %get-tuple-element.59, bf16[384,1024]{1,0:T(8,128)(2,1)S(1)} %get-tuple-element.58, bf16[4,384,384]{2,1,0:T(8,128)(2,1)S(1)} %gather_fusion, f32[4]{0:T(128)S(1)} %add_rsqrt_fusion, f32[4]{0:T(128)S(1)} %broadcast_multiply_fusion, bf16[512,384]{1,0:T(8,128)(2,1)} %fusion.100, ...), kind=kOutput, calls=%fused_computation.63 | convolution fusion | flops 7659061248 | bytes 37093408 | tf_op jit(solution)/shard_map/oax,xk->oak/dot_general | solution.py:77
  41.8 14.6 %fusion.34 = (bf16[4,1,512,1024]{3,2,0,1:T(8,128)(2,1)S(1)}, bf16[4,1,512,1024]{3,2,0,1:T(8,128)(2,1)}) fusion(f32[4,1024,2048]{2,1,0:T(8,128)} %fusion.40), kind=kLoop, calls=%fused_computation.54 | loop fusion | flops 8388608 | bytes 41943040 | tf_op jit(solution)/shard_map/stack | solution.py:82
  56.3 6.2 pad_maximum_fusion
  62.6 5.0 sine_convert_fusion.1
  67.6 196.7 %all-gather.6.cloned.1.call-done = bf16[4,2,512,2048]{3,2,0,1:T(8,128)(2,1)} async-done(((bf16[4,2,512,1024]{3,2,0,1:T(8,128)(2,1)}), bf16[4,2,512,2048]{3,2,0,1:T(8,128)(2,1)}) %all-gather.6.cloned.1.call-update) | async-done | bytes 16777232 | tf_op jit(solution)/shard_map/all_gather | solution.py:83
  264.3 14.2 %fusion.56 = (f32[512,2048]{1,0:T(8,128)S(1)}, f32[512,2048]{1,0:T(8,128)}, f32[512,2048]{1,0:T(8,128)}, f32[512,2048]{1,0:T(8,128)}, f32[512,2048]{1,0:T(8,128)...) fusion(bf16[4,2,512,2048]{3,2,0,1:T(8,128)(2,1)} %all-gather.6.cloned.1.call-done), kind=kLoop, calls=%fused_computation.91 | loop fusion | flops 8388608 | bytes 50331648 | tf_op jit(solution)/shard_map/convert_element_type | solution.py:89
  278.5 19.2 %fusion.1 = (bf16[2,1,512,2048]{3,2,1,0:T(8,128)(2,1)}, bf16[2,1,512,2048]{3,2,1,0:T(8,128)(2,1)}, bf16[2,1,512,2048]{3,2,1,0:T(8,128)(2,1)}, bf16[2,1,512,2048]...) fusion(f32[512,2048]{1,0:T(8,128)} %get-tuple-element.35, ...), kind=kLoop, calls=%fused_computation.18 | loop fusion | flops 54525952 | bytes 58720256 | tf_op jit(solution)/shard_map/convert.14
  297.8 5.2 fusion.18
  304.0 1.2 copy-done.2
  305.2 1.2 copy-done.3
  306.4 5.2 fusion.5
  311.6 5.2 fusion.22
  317.5 2.4 fusion.26
  321.0 2.4 fusion.30
  324.1 2.3 copy.9
  326.4 2.4 collective-permute-start
  329.0 180.8 %collective-permute-done = f32[8,2,512,128]{3,2,1,0:T(8,128)} collective-permute-done((f32[8,2,512,128]{3,2,1,0:T(8,128)}, f32[8,2,512,128]{3,2,1,0:T(8,128)}, u32[]{:S(2)}, u32[]{:S(2)}) %collective-permute-start) | collective-permute-done | bytes 4194336 | tf_op jit(solution)/shard_map/ppermute | solution.py:15
  509.8 3.9 bitcast_subtract_fusion
  514.2 6.2 maximum_select_fusion
  520.9 4.2 fusion.99
  525.1 87.2 %collective-permute-done.1 = f32[8,2,512,128]{3,2,1,0:T(8,128)} collective-permute-done((f32[8,2,512,128]{3,2,1,0:T(8,128)}, f32[8,2,512,128]{3,2,1,0:T(8,128)}, u32[]{:S(2)}, u32[]{:S(2)}) %collective-permute-start.1) | collective-permute-done | bytes 4194336 | tf_op jit(solution)/shard_map/ppermute | solution.py:15
  612.3 4.1 sub.78
  616.8 16.4 %fusion.59 = (f32[2,512,128]{1,2,0:T(8,128)S(1)}, f32[2,512,128]{1,2,0:T(8,128)S(1)}) fusion(f32[512,1,512]{2,0,1:T(8,128)S(1)} %get-tuple-element.61, f32[512,1,512]{2,0,1:T(8,128)S(1)} %get-tuple-element.60, f32[8,1,512,128]{3,2,1,0:T(8,128)S(1)} %get-tuple-element.47, f32[8,1,512,128]{3,2,1,0:T(8,128)S(1)} %get-tuple-element.46, ...), kind=kOutput, calls=%fused_computation.97 | convolution fusion | flops 6447955968 | bytes 15728641 | tf_op jit(solution)/shard_map/tcj,icjw->itw/dot_general | solution.py:124
  633.2 1.0 copy.12
  634.2 1.0 copy.11
  635.3 9.1 %all-gather.10.cloned.1.call-done = f32[4,512,128]{2,1,0:T(8,128)} async-done(((f32[2,512,128]{2,1,0:T(8,128)}), f32[4,512,128]{2,1,0:T(8,128)}) %all-gather.10.cloned.1.call-update) | async-done | bytes 1048592 | tf_op jit(solution)/shard_map/all_gather | solution.py:19
  644.3 2.0 fusion.97
  646.4 10.3 %all-gather.8.cloned.1.call-done = f32[4,512,128]{2,1,0:T(8,128)} async-done(((f32[2,512,128]{2,1,0:T(8,128)}), f32[4,512,128]{2,1,0:T(8,128)}) %all-gather.8.cloned.1.call-update) | async-done | bytes 1048592 | tf_op jit(solution)/shard_map/all_gather | solution.py:19
  656.7 2.0 fusion.98
  (51 shorter events, 7.4 us)
Async XLA Ops:
  7.2 8.5 %copy-start = (bf16[8,384,384]{2,1,0:T(8,128)(2,1)S(1)}, bf16[8,384,384]{2,1,0:T(8,128)(2,1)}, u32[]{:S(2)}) copy-start(bf16[8,384,384]{2,1,0:T(8,128)(2,1)} %param.4) | copy-start | bytes 7077892
  7.2 257.1 %all-gather.6.cloned.1.call-start = ((), (), s32[]{:S(2)}) async-start(), calls=%async_computation | async-start | bytes 25165824 | tf_op jit(solution)/shard_map/all_gather | solution.py:83
  62.6 581.7 %all-gather.10.cloned.1.call-start = ((), (), s32[]{:S(2)}) async-start(), calls=%async_computation.2 | async-start | bytes 1572864 | tf_op jit(solution)/shard_map/all_gather | solution.py:19
  297.7 5.4 slice-start
  297.7 6.2 slice-start.1
  297.8 7.4 %copy-start.2 = (f32[512,2048]{1,0:T(8,128)S(1)}, f32[512,2048]{1,0:T(8,128)}, u32[]{:S(2)}) copy-start(f32[512,2048]{1,0:T(8,128)} %get-tuple-element.33) | copy-start | bytes 12582916
  297.8 8.6 %copy-start.3 = (f32[512,2048]{1,0:T(8,128)S(1)}, f32[512,2048]{1,0:T(8,128)}, u32[]{:S(2)}) copy-start(f32[512,2048]{1,0:T(8,128)} %get-tuple-element.34) | copy-start | bytes 12582916
  306.4 5.2 copy-start.8
  306.4 5.2 copy-start.9
  311.6 5.3 copy-start.6
  311.6 5.9 copy-start.7
  317.5 2.5 copy-start.4
  317.5 3.5 copy-start.5
  326.4 183.4 %collective-permute-start = (f32[8,2,512,128]{3,2,1,0:T(8,128)}, f32[8,2,512,128]{3,2,1,0:T(8,128)}, u32[]{:S(2)}, u32[]{:S(2)}) collective-permute-start(f32[8,2,512,128]{3,2,1,0:T(8,128)} %bitcast.20), channel_id=1, source_target_pairs={{0,8},{4,12},{8,0},{12,4},{1,9},{5,13},{9,1},{13,5},{2,10},{6,14},... | collective-permute-start | bytes 12582920 | tf_op jit(solution)/shard_map/ppermute | solution.py:15
  520.4 91.9 %collective-permute-start.1 = (f32[8,2,512,128]{3,2,1,0:T(8,128)}, f32[8,2,512,128]{3,2,1,0:T(8,128)}, u32[]{:S(2)}, u32[]{:S(2)}) collective-permute-start(f32[8,2,512,128]{3,2,1,0:T(8,128)} %maximum_select_fusion), channel_id=1, source_target_pairs={{0,4},{4,0},{8,12},{12,8},{1,5},{5,1},{9,13},{13,9},{2,6},{6,2},{1... | collective-permute-start | bytes 12582920 | tf_op jit(solution)/shard_map/ppermute | solution.py:15
  616.8 41.9 %copy-start.1 = (bf16[8,384,384]{2,1,0:T(8,128)(2,1)S(1)}, bf16[8,384,384]{2,1,0:T(8,128)(2,1)}, u32[]{:S(2)}) copy-start(bf16[8,384,384]{2,1,0:T(8,128)(2,1)} %param.4) | copy-start | bytes 7077892
  634.2 22.5 %all-gather.8.cloned.1.call-start = ((), (), s32[]{:S(2)}) async-start(), calls=%async_computation.1 | async-start | bytes 1572864 | tf_op jit(solution)/shard_map/all_gather | solution.py:19
Sparse Core Ops, SparseCore 0:
  62.7 201.5 all-gather.5
  634.3 9.9 all-gather.9
  646.4 10.1 all-gather.7
where the time goes:
time: 674 us; the launch traced here: 666 us
  waiting for transfers between devices  484 us (72%)
  other arithmetic  104 us (15%)
  matrix products  49.5 us (7%)
  between operations  14.6 us (2%)
  local copies, waits for them, and re-layouts  9.96 us (1%)
    ppermute x2, waiting for transfers between devices, swapped(): lax.ppermute(shard, axis, [(i, i ^ 1 << apart) for i in range(lax.axis_si...  268 us
    all_gather x1, waiting for transfers between devices, shards(): piece = lax.all_gather(own_spectra, 'mic', axis=3, tiled=True)  197 us
    another operation x2, other arithmetic  24.4 us
    another operation x2, other arithmetic, shards(): own_spectra = jnp.stack([spec_re, spec_im], 1).astype(jnp.bfloat16)  20.8 us
    all_gather x2, waiting for transfers between devices, merged_2(): gathered = jax.tree.map(lambda a: lax.all_gather(a, axis), part)  19.4 us
    dot_general x1, matrix products, shards(): jnp.einsum('oax,xk->oak', rowpass, right_table, preferred_element_type=jn...  18 us
    dot_general x1, matrix products, shards(): jnp.einsum('tcj,icjw->itw', column_table, values, precision=lax.Precision...  16.4 us
    dot_general x4, matrix products, shards(): jnp.einsum('mcbk,kw->mcbw', product, row_table, preferred_element_type=jn...  15.2 us
  transfers between devices with their start and end apart: 5, of which 5 were waited for; matrix products, arithmetic and copies ran while one was open for 2% of the time, Pallas kernels for 0%

commit v1 on v0

v1 whole, which is shorter than its diff:
```python
import functools
import math

import jax
import jax.numpy as jnp
import ml_dtypes
import numpy as np
from jax import lax
from jax.experimental import pallas as pl
from jax.experimental.pallas import tpu as pltpu
from jax.sharding import PartitionSpec as P

WCOLS = 128
PAD = 16

two_pi = 2.0 * math.pi
BF16 = ml_dtypes.bfloat16
PARAMS = pltpu.CompilerParams(vmem_limit_bytes=40 * 1024 * 1024)


def bits(count):
    return count.bit_length() - 1


def reverse_bits(number, digits):
    result = number * 0
    for digit in range(digits):
        result = result + number // (1 << digit) % 2 * (1 << digits - 1 - digit)
    return result


def phases(rows, cols, period):
    angles = np.outer(rows, cols) % period * (two_pi / period)
    return np.cos(angles), np.sin(angles)


def window_table(length, win, mirrored):
    ratio = length // win
    lanes = win // ratio
    sign = 1 if mirrored else -1
    base = np.arange(win)[:, None] + sign * ratio * np.arange(lanes)[None, :]
    d = (length // ratio * np.arange(ratio)[:, None, None] + base[None]) % length
    u = np.arange(win)
    kernel = np.exp(2j * np.pi * (np.outer(np.arange(length), u) % length) / length).sum(1) / win
    val = kernel[d]
    upper = np.concatenate([val.real, -sign * val.imag], 2)
    lower = np.concatenate([-val.imag, -sign * val.real], 2)
    return np.concatenate([upper, lower], 1).astype(BF16)


def tiles_of(re, im, lanes, axis):
    pieces = []
    for start in range(0, re.shape[axis], lanes):
        cut = [slice(None)] * re.ndim
        cut[axis] = slice(start, start + lanes)
        pieces += [re[tuple(cut)], im[tuple(cut)]]
    return np.concatenate(pieces, axis)


def template_table(tsize, win, lanes):
    cos, sin = phases(np.arange(tsize), np.arange(win), win)
    upper = tiles_of(cos, -sin, lanes, 1)
    lower = tiles_of(sin, cos, lanes, 1)
    return np.concatenate([upper, lower], 0).astype(BF16)


def back_table(win, lanes):
    cos, sin = phases(np.arange(win), np.arange(WCOLS), win)
    re_rows = np.concatenate([cos, sin], 1)
    im_rows = np.concatenate([-sin, cos], 1)
    return tiles_of(re_rows, im_rows, lanes, 0).astype(BF16)


def column_table(length, classes, cores, band):
    steps = length // classes
    out = []
    for rho in range(classes):
        per_core = []
        for core in range(cores):
            cos, sin = phases(rho + classes * np.arange(steps), core * band + np.arange(band), length)
            per_core.append(np.concatenate([cos, -sin], 1))
        out.append(np.stack(per_core))
    return np.stack(out).astype(BF16)


def flip_table(band):
    out = np.zeros((band + PAD, band), np.float32)
    out[band - np.arange(band), np.arange(band)] = 1.0
    return out.astype(BF16)


def window_kernel(mirrored, place_ref, spec_ref, table_ref, out_ref, acc_ref):
    ratio = table_ref.shape[0]
    win = table_ref.shape[1] // 2
    width = table_ref.shape[2]
    step = pl.program_id(0)

    @pl.when(step == 0)
    def _():
        acc_ref[...] = jnp.zeros_like(acc_ref)

    for part in range(ratio):
        block = lax.rem(step + (part if mirrored else ratio - part), ratio)
        got = jnp.dot(spec_ref[0, 0], table_ref[block, :win], preferred_element_type=jnp.float32)
        got += jnp.dot(spec_ref[0, 1], table_ref[block, win:], preferred_element_type=jnp.float32)
        acc_ref[:, part * width : (part + 1) * width] += got

    @pl.when(step == ratio - 1)
    def _():
        out_ref[...] = acc_ref[...].astype(out_ref.dtype)


def windowed(spectra, table, place, band, dtype, mirrored):
    ratio, double_win, width = table.shape
    win = double_win // 2
    return pl.pallas_call(
        functools.partial(window_kernel, mirrored),
        out_shape=jax.ShapeDtypeStruct((band, ratio * width), dtype),
        grid_spec=pltpu.PrefetchScalarGridSpec(
            num_scalar_prefetch=1,
            grid=(ratio,),
            in_specs=[
                pl.BlockSpec((1, 2, band, win), lambda a, place: (place[0], 0, place[1], a)),
                pl.BlockSpec(table.shape, lambda a, place: (0, 0, 0)),
            ],
            out_specs=pl.BlockSpec((band, ratio * width), lambda a, place: (0, 0)),
            scratch_shapes=[pltpu.VMEM((band, ratio * width), jnp.float32)],
        ),
        compiler_params=PARAMS,
        cost_estimate=pl.CostEstimate(
            flops=2 * band * 2 * win * ratio * ratio * width,
            bytes_accessed=2 * (2 * band * win * ratio + table.size),
            transcendentals=0,
        ),
        name="windowed",
    )(place, spectra, table)


def partial_kernel(members, place_ref, keep_ref, other_ref, flip_ref, tspec_ref, back_ref, *rest):
    outs = rest[:members]
    held_ref, part_ref = rest[members:]
    orient = pl.program_id(0)
    window = part_ref.shape[0]
    band = keep_ref.shape[0]
    rows, width = held_ref.shape
    lanes = 128
    blocks = width // (2 * lanes)

    @pl.when(orient == 0)
    def _():
        held_ref[...] = jnp.dot(flip_ref[...], other_ref[...], preferred_element_type=jnp.float32)
        held_ref[:band] += keep_ref[...]

    total = jnp.zeros((rows, 2 * WCOLS), jnp.float32)
    for block in range(blocks):
        re_at = slice(2 * block * lanes, (2 * block + 1) * lanes)
        im_at = slice((2 * block + 1) * lanes, (2 * block + 2) * lanes)
        mic_re = held_ref[:, re_at]
        mic_im = held_ref[:, im_at]
        tmpl_re = tspec_ref[0, :, re_at].astype(jnp.float32)
        tmpl_im = tspec_ref[0, :, im_at].astype(jnp.float32)
        prod_re = (mic_re * tmpl_re + mic_im * tmpl_im).astype(jnp.bfloat16)
        prod_im = (mic_im * tmpl_re - mic_re * tmpl_im).astype(jnp.bfloat16)
        total += jnp.dot(
            jnp.concatenate([prod_re, prod_im], 1),
            back_ref[2 * block * lanes : (2 * block + 2) * lanes],
            preferred_element_type=jnp.float32,
        )
    part_ref[orient] = total

    @pl.when(orient == window - 1)
    def _():
        group = WCOLS // members
        lane_group = lax.broadcasted_iota(jnp.int32, (rows, WCOLS), 1) // group
        tiles = max(1, window // members)
        mine = place_ref[0]
        for tile in range(tiles):
            for plane in range(2):
                at = slice(plane * WCOLS, (plane + 1) * WCOLS)
                pieces = []
                for i in range(members):
                    piece = part_ref[(tile * members + i) % window, :, at]
                    pieces.append(pltpu.roll(piece, group * i, 1) if i else piece)
                for s in range(members):
                    target = lax.bitwise_xor(mine, s)
                    packed = pieces[0]
                    for i in range(1, members):
                        inside = (lane_group + (members - i)) % members == target
                        packed = jnp.where(inside, pieces[i], packed)
                    start = (plane * tiles + tile) * WCOLS
                    outs[s][:, start : start + WCOLS] = packed.astype(outs[s].dtype)


def partials(keep, other, flip, tspec, back, place, members):
    window, rows, width = tspec.shape
    tiles = max(1, window // members)
    whole = lambda shape: pl.BlockSpec(shape, lambda o, place: (0,) * len(shape))
    out_shape = (rows, 2 * tiles * WCOLS)
    return pl.pallas_call(
        functools.partial(partial_kernel, members),
        out_shape=[jax.ShapeDtypeStruct(out_shape, jnp.bfloat16)] * members,
        grid_spec=pltpu.PrefetchScalarGridSpec(
            num_scalar_prefetch=1,
            grid=(window,),
            in_specs=[
                whole(keep.shape),
                whole(other.shape),
                whole(flip.shape),
                pl.BlockSpec((1, rows, width), lambda o, place: (o, 0, 0)),
                whole(back.shape),
            ],
            out_specs=[whole(out_shape)] * members,
            scratch_shapes=[
                pltpu.VMEM((rows, width), jnp.float32),
                pltpu.VMEM((window, rows, 2 * WCOLS), jnp.float32),
            ],
        ),
        compiler_params=PARAMS,
        cost_estimate=pl.CostEstimate(
            flops=2 * window * rows * width * 2 * WCOLS,
            bytes_accessed=2 * tspec.size,
            transcendentals=0,
        ),
        name="partials",
    )(place, keep, other, flip, tspec, back)


def column_kernel(members, classes, scale, place_ref, factor_ref, table_ref, *rest):
    parts = rest[:members]
    outs = rest[members:]
    cores = table_ref.shape[1]
    steps = table_ref.shape[2]
    band = table_ref.shape[3] // 2
    wide = parts[0].shape[1] // 2
    step = pl.program_id(0)
    spread = members // cores
    corr = jnp.zeros((steps, wide), jnp.float32)
    for s_core in range(cores):
        z_re = jnp.zeros((band, wide), jnp.float32)
        z_im = jnp.zeros((band, wide), jnp.float32)
        more_re = jnp.zeros((PAD, wide), jnp.float32)
        more_im = jnp.zeros((PAD, wide), jnp.float32)
        for s_row in range(spread):
            s = s_row * cores + s_core
            cos, sin = factor_ref[step, s, 0], factor_ref[step, s, 1]
            re = parts[s][:band, :wide].astype(jnp.float32)
            im = parts[s][:band, wide:].astype(jnp.float32)
            z_re += cos * re - sin * im
            z_im += sin * re + cos * im
            t = s_row * cores + (s_core ^ 1)
            cos, sin = factor_ref[step, t, 2], factor_ref[step, t, 3]
            re = parts[t][band:, :wide].astype(jnp.float32)
            im = parts[t][band:, wide:].astype(jnp.float32)
            more_re += cos * re - sin * im
            more_im += sin * re + cos * im
        stacked = jnp.concatenate(
            [z_re[:PAD] + more_re, z_re[PAD:], z_im[:PAD] + more_im, z_im[PAD:]], 0
        ).astype(jnp.bfloat16)
        core = lax.bitwise_xor(place_ref[1], s_core)
        corr += jnp.dot(table_ref[0, core], stacked, preferred_element_type=jnp.float32)
    corr = corr * (scale * factor_ref[step, members, 0])
    peak = corr[:, :WCOLS]
    power = corr[:, :WCOLS] * corr[:, :WCOLS]
    for start in range(WCOLS, wide, WCOLS):
        more = corr[:, start : start + WCOLS]
        peak = jnp.maximum(peak, more)
        power = power + more * more
    group = WCOLS // members
    shift = group
    while shift < WCOLS:
        peak = jnp.maximum(peak, pltpu.roll(peak, shift, 1))
        power = power + pltpu.roll(power, shift, 1)
        shift *= 2
    power = power * factor_ref[step, members, 1]
    height = steps // (members // 2)
    lane_group = lax.broadcasted_iota(jnp.int32, (height, WCOLS), 1) // group
    kappa = (lane_group + (members - place_ref[0])) % members
    packed = peak[:height]
    for k in range(1, members):
        source = (power if k % 2 else peak)[k // 2 * height : (k // 2 + 1) * height]
        packed = jnp.where(kappa == k, source, packed)
    for s in range(classes):

        @pl.when(step == s)
        def _():
            outs[s][...] = packed.astype(outs[s].dtype)


def columns(parts, table, place, factor, scale, dtype):
    classes, cores, steps, double_band = table.shape
    members = len(parts)
    height = steps // (members // 2)
    whole = lambda shape: pl.BlockSpec(shape, lambda s, place, factor: (0,) * len(shape))
    return pl.pallas_call(
        functools.partial(column_kernel, members, classes, scale),
        out_shape=[jax.ShapeDtypeStruct((height, WCOLS), dtype)] * classes,
        grid_spec=pltpu.PrefetchScalarGridSpec(
            num_scalar_prefetch=2,
            grid=(classes,),
            in_specs=[
                pl.BlockSpec(
                    (1, cores, steps, double_band), lambda s, place, factor: (place[2 + s], 0, 0, 0)
                )
            ]
            + [whole(part.shape) for part in parts],
            out_specs=[whole((height, WCOLS))] * classes,
        ),
        compiler_params=PARAMS,
        name="columns",
    )(place, factor, table, *parts)


def unpack_kernel(members, classes, place_ref, *rest):
    near = rest[:classes]
    far = rest[classes : 2 * classes]
    peak_ref, power_ref = rest[2 * classes :]
    row, core = place_ref[0], place_ref[1]
    half = classes // 2
    height = near[0].shape[0]
    group = WCOLS // members
    lane_group = lax.broadcasted_iota(jnp.int32, (height, WCOLS), 1) // group
    side = row // half
    for delta in range(2):
        mic = lax.bitwise_xor(side, delta)
        for k in range(members):
            wanted = (lane_group + (members - k)) % members
            value = jnp.zeros((height, WCOLS), jnp.float32)
            for low in range(half):
                s = delta * half + low
                base = lax.bitwise_xor(row, s) % half * 2
                for source, at in ((near, core), (far, 1 - core)):
                    value = jnp.where(wanted == base + at, source[s][...].astype(jnp.float32), value)
            if k:
                value = pltpu.roll(value, WCOLS - k * group, 1)
            target = power_ref if k % 2 else peak_ref
            target[mic, 0, k // 2 * height : (k // 2 + 1) * height, :] = value


def unpack(near, far, place, steps, members):
    classes = len(near)
    shape = jax.ShapeDtypeStruct((2, 1, steps, WCOLS), jnp.float32)
    return pl.pallas_call(
        functools.partial(unpack_kernel, members, classes),
        out_shape=[shape, shape],
        in_specs=[pl.BlockSpec(memory_space=pltpu.SMEM)]
        + [pl.BlockSpec(memory_space=pltpu.VMEM)] * (2 * classes),
        out_specs=[pl.BlockSpec(memory_space=pltpu.VMEM)] * 2,
        compiler_params=PARAMS,
        name="unpack",
    )(place, *near, *far)


def normalize(picture):
    values = picture.astype(jnp.float32)
    centred = values - jnp.mean(values)
    factor = lax.rsqrt(jnp.mean(centred * centred) + 1e-06)
    return (centred * factor).astype(jnp.bfloat16)


def template_spectra(bank, orient_index, band_id, band, length, win, lanes):
    tsize = bank.shape[1]
    templates = jax.vmap(normalize)(bank[orient_index])
    cos, sin = phases(np.arange(length + PAD), np.arange(tsize), length)
    rows = jnp.asarray(np.stack([cos, -sin]).astype(BF16))
    left = lax.dynamic_slice_in_dim(rows, band_id * band, band + PAD, 1)
    rowpass = jnp.einsum("cay,oyx->oacx", left, templates, preferred_element_type=jnp.float32)
    rowpass = rowpass.astype(jnp.bfloat16).reshape(templates.shape[0], band + PAD, 2 * tsize)
    right = jnp.asarray(template_table(tsize, win, lanes))
    spectrum = jnp.einsum("oax,xk->oak", rowpass, right, preferred_element_type=jnp.float32)
    return spectrum.astype(jnp.bfloat16)


def shards(spectra, bank, orient_index):
    length = spectra.shape[3]
    tsize = bank.shape[1]
    classes = lax.axis_size("row")
    cores = lax.axis_size("orient")
    row = lax.axis_index("row")
    core = lax.axis_index("orient")
    count = classes * cores
    members = count // 2
    half = classes // 2
    band = length // count
    steps = length // classes
    win = 1 << (tsize + WCOLS - 2).bit_length()
    lanes = win // (length // win)
    device = row * cores + core
    member = device % members
    side = device // members
    line = ("row", "orient")

    send_place = jnp.stack([1 - side, core]).astype(jnp.int32)
    keep_place = jnp.stack([side, core]).astype(jnp.int32)
    mirror_table = jnp.asarray(window_table(length, win, True))
    sent = windowed(spectra, mirror_table, send_place, band, jnp.bfloat16, True)
    other = lax.ppermute(sent, line, [(i, count - 1 - i) for i in range(count)])
    table = jnp.asarray(window_table(length, win, False))
    keep = windowed(spectra, table, keep_place, band, jnp.float32, False)
    tspec = template_spectra(bank, orient_index, device, band, length, win, lanes)
    parts = partials(
        keep,
        other,
        jnp.asarray(flip_table(band)),
        tspec,
        jnp.asarray(back_table(win, lanes)),
        member[None].astype(jnp.int32),
        members,
    )
    got = [parts[0]]
    for s in range(1, members):
        got.append(lax.ppermute(parts[s], line, [(i, i ^ s) for i in range(count)]))

    step_ids = lax.bitwise_xor(row, jnp.arange(classes, dtype=jnp.int32))
    rho = reverse_bits(step_ids, bits(classes))
    sources = lax.bitwise_xor(member, jnp.arange(members, dtype=jnp.int32))
    roots = np.exp(2j * np.pi * np.arange(classes) / classes)
    root_re = jnp.asarray(np.round(roots.real, 15).astype(np.float32))
    root_im = jnp.asarray(np.round(roots.imag, 15).astype(np.float32))
    own = rho[:, None] * (sources // cores)[None, :] % classes
    after = rho[:, None] * ((sources + 1) // cores)[None, :] % classes
    factor = jnp.stack([root_re[own], root_im[own], root_re[after], root_im[after]], 2)
    sign = 1.0 - 2.0 * (side * rho % 2).astype(jnp.float32)
    window = orient_index.shape[0]
    share = jnp.full_like(sign, window / max(window, members))
    zeros = jnp.zeros_like(sign)
    last = jnp.stack([sign, share, zeros, zeros], 1)[:, None]
    factor = jnp.concatenate([factor, last], 1)
    place = jnp.concatenate([jnp.stack([member, core]), rho]).astype(jnp.int32)
    maps = columns(
        got,
        jnp.asarray(column_table(length, classes, cores, band)),
        place,
        factor,
        1.0 / (length * tsize),
        jnp.float32,
    )
    near = [maps[0]]
    for s in range(1, classes):
        near.append(lax.ppermute(maps[s], "row", [(i, i ^ s) for i in range(classes)]))
    far = [lax.ppermute(m, "orient", [(0, 1), (1, 0)]) for m in near]
    peak, power = unpack(near, far, jnp.stack([row, core]).astype(jnp.int32), steps, members)
    return peak, power


def solution(mesh):
    return jax.shard_map(
        shards,
        mesh=mesh,
        in_specs=(P(("grp", "mic"), None, "row", None), P(), P("grp")),
        out_specs=(P(("grp", "mic"), "row", None, None), P(("grp", "mic"), "row", None, None)),
        check_vma=False,
    )
```

time: 674 us -> 82.5 us (0.12); the launches traced: 666 us -> 82.2 us
  waiting for transfers between devices: 484 us -> 20.4 us
  other arithmetic: 104 us -> 3.83 us
  matrix products: 49.5 us -> 7.61 us
  Pallas kernels: 0 us -> 18.5 us
  between operations: 14.6 us -> 0.85 us
  local copies, waits for them, and re-layouts: 9.96 us -> 20 us
  starting transfers between devices: 3.02 us -> 11.1 us
    ppermute x2 -> x11, waiting for transfers between devices: 268 us -> 20.4 us  [the longest x3 9.93 us: shards(): lax.ppermute(maps[s], 'row', [(i, i ^ s) for i in range(classes)])]
    all_gather x3 -> x0, waiting for transfers between devices: 216 us -> none  [the longest x1 197 us: shards(): piece = lax.all_gather(own_spectra, 'mic', axis=3, tiled=True)]
    another operation x9 -> x4, other arithmetic: 45.8 us -> 0.3 us  [the longest x1 0.08 us: shards(): last = jnp.stack([sign, share, zeros, zeros], 1)[:, None]]
    dot_general x6 -> x2, matrix products: 49.5 us -> 7.61 us  [the longest x1 3.85 us: template_spectra(): jnp.einsum('oax,xk->oak', rowpass, right, preferred_element_type=jnp.floa...]
    convert_element_type x4 -> x0, other arithmetic: 29.4 us -> none  [the longest x1 14.2 us: shards(): tmpl_re = piece[orient_pos, 0].astype(jnp.float32)]
    pallas_call x0 -> x5, Pallas kernels: none -> 18.5 us  [the longest x2 7.58 us: windowed(): pl.pallas_call(functools.partial(window_kernel, mirrored), out_shape=jax....]
    sub x8 -> x1, other arithmetic: 9.3 us -> 0.03 us  [shards(): sign = 1.0 - 2.0 * (side * rho % 2).astype(jnp.float32)]
    ppermute x2 -> x11, starting transfers between devices: 2.9 us -> 11.1 us  [the longest x1 4.55 us: shards(): other = lax.ppermute(sent, line, [(i, count - 1 - i) for i in range(count)])]
  transfers between devices with their start and end apart: 5 -> 11, of which waited for: 5 -> 6; matrix products, arithmetic and copies ran while one was open for 2% -> 23% of each run, Pallas kernels for 0% -> 5%
where the time goes in v1:
time: 82.5 us; the launch traced here: 82.2 us
  waiting for transfers between devices  20.4 us (25%)
  local copies, waits for them, and re-layouts  20 us (24%)
  Pallas kernels  18.5 us (22%)
  starting transfers between devices  11.1 us (13%)
  matrix products  7.61 us (9%)
  other arithmetic  3.83 us (5%)
  between operations  0.85 us (1%)
    unnamed x28, local copies, waits for them, and re-layouts  12.4 us
    ppermute x3, waiting for transfers between devices, shards(): lax.ppermute(maps[s], 'row', [(i, i ^ s) for i in range(classes)])  9.93 us
    ppermute x3, waiting for transfers between devices, shards(): got.append(lax.ppermute(parts[s], line, [(i, i ^ s) for i in range(count)]))  9.18 us
    pallas_call x2, Pallas kernels, windowed(): pl.pallas_call(functools.partial(window_kernel, mirrored), out_shape=jax....  7.58 us
    pallas_call x1, Pallas kernels, partials(): pl.pallas_call(functools.partial(partial_kernel, members), out_shape=[jax...  4.61 us
    ppermute x1, starting transfers between devices, shards(): other = lax.ppermute(sent, line, [(i, count - 1 - i) for i in range(count)])  4.55 us
    pallas_call x1, Pallas kernels, columns(): pl.pallas_call(functools.partial(column_kernel, members, classes, scale),...  4.53 us
    ppermute x3, starting transfers between devices, shards(): lax.ppermute(maps[s], 'row', [(i, i ^ s) for i in range(classes)])  4.45 us
  transfers between devices with their start and end apart: 11, of which 6 were waited for; matrix products, arithmetic and copies ran while one was open for 23% of the time, Pallas kernels for 5%

profile of v1, /device:TPU:0, one launch (start us, length us, event | category | flops | bytes accessed | tf_op | source)
XLA Modules:
  0.0 82.2 jit_solution(14947257226314961367)
XLA Ops:
  0.7 3.5 %copy-done.1 = bf16[2,2,512,2048]{3,2,1,0:T(8,128)(2,1)S(1)} copy-done((bf16[2,2,512,2048]{3,2,1,0:T(8,128)(2,1)S(1)}, bf16[2,2,512,2048]{3,2,1,0:T(8,128)(2,1)}, u32[]{:S(2)}) %copy-start.1) | copy-done | bytes 8388632
  4.3 1.6 %copy-done.5 = bf16[4,1024,256]{2,1,0:T(8,128)(2,1)S(1)} copy-done((bf16[4,1024,256]{2,1,0:T(8,128)(2,1)S(1)}, bf16[4,1024,256]{2,1,0:T(8,128)(2,1)}, u32[]{:S(2)}) %copy-start.5) | copy-done | bytes 2097176
  5.9 3.8 %windowed.3 = bf16[256,1024]{1,0:T(8,128)(2,1)S(1)} custom-call(s32[2]{0:T(128)S(1)} %pad_add_fusion.3.place_ref, bf16[2,2,512,2048]{3,2,1,0:T(8,128)(2,1)S(1)} %copy-done.1, bf16[4,1024,256]{2,1,0:T(8,128)(2,1)S(1)} %copy-done.5), custom_call_target="tpu_custom_call" | custom-call | flops 2147483648 | bytes 4194304 | tf_op jit(solution)/shard_map/windowed/pallas_call | solution.py:116
  9.6 4.6 %collective-permute-start = (bf16[256,1024]{1,0:T(8,128)(2,1)S(1)}, bf16[256,1024]{1,0:T(8,128)(2,1)S(1)}, u32[]{:S(2)}, u32[]{:S(2)}) collective-permute-start(bf16[256,1024]{1,0:T(8,128)(2,1)S(1)} %windowed.3), channel_id=1, source_target_pairs={{0,13},{1,12},{4,9},{5,8},{8,5},{9,4},{12,1},{13,0},{2,15},{3,14},... | collective-permute-start | bytes 1572872 | tf_op jit(solution)/shard_map/ppermute | solution.py:396
  14.4 2.3 %gather_fusion.4 = bf16[8,384,384]{2,1,0:T(8,128)(2,1)} fusion(bf16[8,384,384]{2,1,0:T(8,128)(2,1)S(1)} %copy-done, s32[1024]{0:T(1024)S(1)} %pad_clamp_fusion), kind=kCustom, calls=%fused_computation.4 | custom fusion | bytes 4718624 | tf_op jit(solution)/shard_map/gather | solution.py:362
  16.7 2.3 %convert_reduce_fusion = f32[8]{0:T(128)S(1)} fusion(bf16[8,384,384]{2,1,0:T(8,128)(2,1)} %gather_fusion.4), kind=kLoop, calls=%fused_computation.6 | loop fusion | flops 2359288 | bytes 2359328 | tf_op jit(solution)/shard_map/vmap()/reduce_sum | solution.py:355
  19.1 0.9 %fusion.2 = f32[8]{0:T(128)S(1)} fusion(bf16[8,384,384]{2,1,0:T(8,128)(2,1)S(1)} %copy-done.10, f32[8]{0:T(128)S(1)} %broadcast_multiply_fusion), kind=kLoop, calls=%fused_computation.9 | loop fusion | flops 4718584 | bytes 2359360 | tf_op jit(solution)/shard_map/vmap()/reduce_sum | solution.py:356
  19.9 3.8 %convert_bitcast_fusion = bf16[8,2,34,8,384]{4,3,2,1,0:T(8,128)(2,1)S(1)} fusion(bf16[8,384,384]{2,1,0:T(8,128)(2,1)} %gather_fusion.4, f32[8]{0:T(128)S(1)} %add_rsqrt_fusion, f32[8]{0:T(128)S(1)} %broadcast_multiply_fusion, bf16[2,2064,384]{2,1,0:T(8,128)(2,1)} %constant.156.clone, s32[]{:T(128)S(6)} %select_n.158), kind=kOutput, calls=%fused_computation.11 | convolution fusion | flops 1289846784 | bytes 6119492 | tf_op jit(solution)/shard_map/cay,oyx->oacx/dot_general | solution.py:366
  23.7 2.0 %copy.26 = bf16[8,2,34,8,384]{4,3,1,2,0:T(8,128)(2,1)} copy(bf16[8,2,34,8,384]{4,3,2,1,0:T(8,128)(2,1)S(1)} %convert_bitcast_fusion) | data formatting | bytes 6684672 | tf_op jit(solution)/shard_map/reshape | solution.py:367
  26.0 3.4 %copy-done.2 = bf16[2,2,512,2048]{3,2,1,0:T(8,128)(2,1)S(1)} copy-done((bf16[2,2,512,2048]{3,2,1,0:T(8,128)(2,1)S(1)}, bf16[2,2,512,2048]{3,2,1,0:T(8,128)(2,1)}, u32[]{:S(2)}) %copy-start.2) | copy-done | bytes 8388632
  29.4 1.6 %copy-done.4 = bf16[4,1024,256]{2,1,0:T(8,128)(2,1)S(1)} copy-done((bf16[4,1024,256]{2,1,0:T(8,128)(2,1)S(1)}, bf16[4,1024,256]{2,1,0:T(8,128)(2,1)}, u32[]{:S(2)}) %copy-start.4) | copy-done | bytes 2097176
  31.0 3.8 %windowed.2.keep_ref = f32[256,1024]{1,0:T(8,128)S(1)} custom-call(s32[2]{0:T(128)S(1)} %pad_add_fusion.2.place_ref, bf16[2,2,512,2048]{3,2,1,0:T(8,128)(2,1)S(1)} %copy-done.2, bf16[4,1024,256]{2,1,0:T(8,128)(2,1)S(1)} %copy-done.4), custom_call_target="tpu_custom_call" | custom-call | flops 2147483648 | bytes 4194304 | tf_op jit(solution)/shard_map/windowed/pallas_call | solution.py:116
  35.0 3.8 %convolution_convert_fusion.tspec_ref = bf16[8,272,1024]{2,1,0:T(8,128)(2,1)S(1)} fusion(bf16[8,272,768]{2,1,0:T(8,128)(2,1)S(1)} %bitcast.29, bf16[768,1024,1]{1,0,2:T(8,128)(2,1)S(1)} %copy-done.13), kind=kOutput, calls=%fused_computation.12 | convolution fusion | flops 3424780288 | bytes 9371648 | tf_op jit(solution)/shard_map/oax,xk->oak/dot_general | solution.py:369
  38.9 4.6 %partials.1 = (bf16[272,512]{1,0:T(8,128)(2,1)S(1)}, bf16[272,512]{1,0:T(8,128)(2,1)}, bf16[272,512]{1,0:T(8,128)(2,1)}, bf16[272,512]{1,0:T(8,128)(2,1)}) custom-call(s32[1]{0:T(128)} %bitcast.2.place_ref, f32[256,1024]{1,0:T(8,128)S(1)} %windowed.2.keep_ref, bf16[256,1024]{1,0:T(8,128)(2,1)S(1)} %collective-permute-done.other_ref, ...), custom_call_target="tpu_custom_call" | custom-call | flops 1140850688 | bytes 4456448 | tf_op jit(solution)/shard_map/partials/pallas_call | solution.py:199
  43.5 0.7 collective-permute-start.1
  44.2 1.4 %collective-permute-start.3 = (bf16[272,512]{1,0:T(8,128)(2,1)}, bf16[272,512]{1,0:T(8,128)(2,1)S(1)}, u32[]{:S(2)}, u32[]{:S(2)}) collective-permute-start(bf16[272,512]{1,0:T(8,128)(2,1)} %get-tuple-element.13), channel_id=1, source_target_pairs={{0,5},{1,4},{4,1},{5,0},{8,13},{9,12},{12,9},{13,8},{2,7},{3,6},{6... | collective-permute-start | bytes 835592 | tf_op jit(solution)/shard_map/ppermute | solution.py:411
  45.5 0.7 gather_fusion
  46.2 0.7 gather_fusion.1
  46.9 0.7 gather_fusion.2
  47.5 0.7 gather_fusion.3
  48.8 5.1 %collective-permute-done.2.rest_2_ = bf16[272,512]{1,0:T(8,128)(2,1)S(1)} collective-permute-done((bf16[272,512]{1,0:T(8,128)(2,1)}, bf16[272,512]{1,0:T(8,128)(2,1)S(1)}, u32[]{:S(2)}, u32[]{:S(2)}) %collective-permute-start.2) | collective-permute-done | bytes 278560 | tf_op jit(solution)/shard_map/ppermute | solution.py:411
  53.9 4.0 %collective-permute-done.3.rest_3_ = bf16[272,512]{1,0:T(8,128)(2,1)S(1)} collective-permute-done((bf16[272,512]{1,0:T(8,128)(2,1)}, bf16[272,512]{1,0:T(8,128)(2,1)S(1)}, u32[]{:S(2)}, u32[]{:S(2)}) %collective-permute-start.3) | collective-permute-done | bytes 278560 | tf_op jit(solution)/shard_map/ppermute | solution.py:411
  58.0 2.2 %copy-done.3 = bf16[4,2,512,512]{3,2,1,0:T(8,128)(2,1)S(1)} copy-done((bf16[4,2,512,512]{3,2,1,0:T(8,128)(2,1)S(1)}, bf16[4,2,512,512]{3,2,1,0:T(8,128)(2,1)}, u32[]{:S(2)}) %copy-start.3) | copy-done | bytes 4194328
  60.1 4.5 %columns.1 = (f32[256,128]{1,0:T(8,128)S(1)}, f32[256,128]{1,0:T(8,128)S(1)}, f32[256,128]{1,0:T(8,128)S(1)}, f32[256,128]{1,0:T(8,128)S(1)}) custom-call(s32[6]{0:T(128)S(1)} %pad_add_fusion.1.place_ref, f32[4,5,4]{2,1,0:T(8,128)S(1)} %pad_maximum_fusion.factor_ref, bf16[4,2,512,512]{3,2,1,0:T(8,128)(2,1)S(1)} %copy-done.3, ...), custom_call_target="tpu_custom_call" | custom-call | tf_op jit(solution)/shard_map/columns/pallas_call | solution.py:294
  64.7 1.0 %collective-permute-start.6 = (f32[256,128]{1,0:T(8,128)S(1)}, f32[256,128]{1,0:T(8,128)S(1)}, u32[]{:S(2)}, u32[]{:S(2)}) collective-permute-start(f32[256,128]{1,0:T(8,128)S(1)} %get-tuple-element.17), channel_id=1, source_target_pairs={{0,12},{4,8},{8,4},{12,0},{1,13},{5,9},{9,5},{13,1},{2,14},{6,10},... | collective-permute-start | bytes 393224 | tf_op jit(solution)/shard_map/ppermute | solution.py:439
  65.7 0.3 collective-permute-start.4
  66.0 3.1 %collective-permute-start.5 = (f32[256,128]{1,0:T(8,128)S(1)}, f32[256,128]{1,0:T(8,128)S(1)}, u32[]{:S(2)}, u32[]{:S(2)}) collective-permute-start(f32[256,128]{1,0:T(8,128)S(1)} %get-tuple-element.16), channel_id=1, source_target_pairs={{0,8},{4,12},{8,0},{12,4},{1,9},{5,13},{9,1},{13,5},{2,10},{6,14},... | collective-permute-start | bytes 393224 | tf_op jit(solution)/shard_map/ppermute | solution.py:439
  69.1 3.8 %collective-permute-done.6.rest_3_ = f32[256,128]{1,0:T(8,128)S(1)} collective-permute-done((f32[256,128]{1,0:T(8,128)S(1)}, f32[256,128]{1,0:T(8,128)S(1)}, u32[]{:S(2)}, u32[]{:S(2)}) %collective-permute-start.6) | collective-permute-done | bytes 131104 | tf_op jit(solution)/shard_map/ppermute | solution.py:439
  73.0 3.1 %collective-permute-done.4.rest_1_ = f32[256,128]{1,0:T(8,128)S(1)} collective-permute-done((f32[256,128]{1,0:T(8,128)S(1)}, f32[256,128]{1,0:T(8,128)S(1)}, u32[]{:S(2)}, u32[]{:S(2)}) %collective-permute-start.4) | collective-permute-done | bytes 131104 | tf_op jit(solution)/shard_map/ppermute | solution.py:439
  76.1 3.0 %collective-permute-done.5.rest_2_ = f32[256,128]{1,0:T(8,128)S(1)} collective-permute-done((f32[256,128]{1,0:T(8,128)S(1)}, f32[256,128]{1,0:T(8,128)S(1)}, u32[]{:S(2)}, u32[]{:S(2)}) %collective-permute-start.5) | collective-permute-done | bytes 131104 | tf_op jit(solution)/shard_map/ppermute | solution.py:439
  79.2 1.3 %collective-permute-done.9.rest_6_ = f32[256,128]{1,0:T(8,128)S(1)} collective-permute-done((f32[256,128]{1,0:T(8,128)S(1)}, f32[256,128]{1,0:T(8,128)S(1)}, u32[]{:S(2)}, u32[]{:S(2)}) %collective-permute-start.9) | collective-permute-done | bytes 131104 | tf_op jit(solution)/shard_map/ppermute | solution.py:440
  80.4 1.8 %unpack.1 = (f32[2,1,512,128]{3,2,1,0:T(8,128)}, f32[2,1,512,128]{3,2,1,0:T(8,128)}) custom-call(s32[2]{0:T(128)S(1)} %pad_add_fusion.place_ref, f32[256,128]{1,0:T(8,128)S(1)} %get-tuple-element.14.rest_0_, f32[256,128]{1,0:T(8,128)S(1)} %collective-permute-done.4.rest_1_, f32[256,128]{1,0:T(8,128)S(1)} %collective-permute-done.5.rest_2_, ...), custom_call_target="tpu_custom_call" | custom-call | tf_op jit(solution)/shard_map/unpack/pallas_call | solution.py:342
  (58 shorter events, 1.4 us)
Async XLA Ops:
  0.6 13.7 %copy-start = (bf16[8,384,384]{2,1,0:T(8,128)(2,1)S(1)}, bf16[8,384,384]{2,1,0:T(8,128)(2,1)}, u32[]{:S(2)}) copy-start(bf16[8,384,384]{2,1,0:T(8,128)(2,1)} %param.13) | copy-start | bytes 7077892
  0.7 3.5 %copy-start.1 = (bf16[2,2,512,2048]{3,2,1,0:T(8,128)(2,1)S(1)}, bf16[2,2,512,2048]{3,2,1,0:T(8,128)(2,1)}, u32[]{:S(2)}) copy-start(bf16[2,2,512,2048]{3,2,1,0:T(8,128)(2,1)} %spec_ref.3) | copy-start | bytes 25165828
  4.3 1.6 %copy-start.5 = (bf16[4,1024,256]{2,1,0:T(8,128)(2,1)S(1)}, bf16[4,1024,256]{2,1,0:T(8,128)(2,1)}, u32[]{:S(2)}) copy-start(bf16[4,1024,256]{2,1,0:T(8,128)(2,1)} %constant.154.clone.table_ref) | copy-start | bytes 6291460
  5.9 8.5 %copy-start.12 = (s32[8]{0:T(128)S(1)}, s32[8]{0:T(128)}, u32[]{:S(2)}) copy-start(s32[8]{0:T(128)} %param.14) | copy-start | bytes 100
  9.6 29.2 %collective-permute-start = (bf16[256,1024]{1,0:T(8,128)(2,1)S(1)}, bf16[256,1024]{1,0:T(8,128)(2,1)S(1)}, u32[]{:S(2)}, u32[]{:S(2)}) collective-permute-start(bf16[256,1024]{1,0:T(8,128)(2,1)S(1)} %windowed.3), channel_id=1, source_target_pairs={{0,13},{1,12},{4,9},{5,8},{8,5},{9,4},{12,1},{13,0},{2,15},{3,14},... | collective-permute-start | bytes 1572872 | tf_op jit(solution)/shard_map/ppermute | solution.py:396
  16.7 2.4 %copy-start.10 = (bf16[8,384,384]{2,1,0:T(8,128)(2,1)S(1)}, bf16[8,384,384]{2,1,0:T(8,128)(2,1)}, u32[]{:S(2)}) copy-start(bf16[8,384,384]{2,1,0:T(8,128)(2,1)} %gather_fusion.4) | copy-start | bytes 7077892
  26.0 3.4 %copy-start.2 = (bf16[2,2,512,2048]{3,2,1,0:T(8,128)(2,1)S(1)}, bf16[2,2,512,2048]{3,2,1,0:T(8,128)(2,1)}, u32[]{:S(2)}) copy-start(bf16[2,2,512,2048]{3,2,1,0:T(8,128)(2,1)} %spec_ref.3) | copy-start | bytes 25165828
  29.4 1.6 %copy-start.4 = (bf16[4,1024,256]{2,1,0:T(8,128)(2,1)S(1)}, bf16[4,1024,256]{2,1,0:T(8,128)(2,1)}, u32[]{:S(2)}) copy-start(bf16[4,1024,256]{2,1,0:T(8,128)(2,1)} %constant.155.clone.table_ref) | copy-start | bytes 6291460
  31.0 4.0 %copy-start.11 = (bf16[8,2,34,8,384]{4,3,1,2,0:T(8,128)(2,1)S(1)}, bf16[8,2,34,8,384]{4,3,1,2,0:T(8,128)(2,1)}, u32[]{:S(2)}) copy-start(bf16[8,2,34,8,384]{4,3,1,2,0:T(8,128)(2,1)} %copy.26) | copy-start | bytes 10027012
  31.0 4.0 %copy-start.13 = (bf16[768,1024,1]{1,0,2:T(8,128)(2,1)S(1)}, bf16[768,1024,1]{1,0,2:T(8,128)(2,1)}, u32[]{:S(2)}) copy-start(bf16[768,1024,1]{1,0,2:T(8,128)(2,1)} %constant.164) | copy-start | bytes 4718596
  35.0 3.9 %copy-start.6 = (bf16[1024,256]{1,0:T(8,128)(2,1)S(1)}, bf16[1024,256]{1,0:T(8,128)(2,1)}, u32[]{:S(2)}) copy-start(bf16[1024,256]{1,0:T(8,128)(2,1)} %constant.159.clone.back_ref) | copy-start | bytes 1572868
  35.0 3.9 %copy-start.7 = (bf16[272,256]{1,0:T(8,128)(2,1)S(1)}, bf16[272,256]{1,0:T(8,128)(2,1)}, u32[]{:S(2)}) copy-start(bf16[272,256]{1,0:T(8,128)(2,1)} %constant.158.clone.flip_ref) | copy-start | bytes 417796
  38.8 6.7 %copy-start.9 = (f32[4]{0:T(128)S(1)}, f32[4]{0:T(128)}, u32[]{:S(2)}) copy-start(f32[4]{0:T(128)} %constant.160.clone) | copy-start | bytes 52
  38.9 7.3 %copy-start.8 = (f32[4]{0:T(128)S(1)}, f32[4]{0:T(128)}, u32[]{:S(2)}) copy-start(f32[4]{0:T(128)} %constant.161.clone) | copy-start | bytes 52
  43.5 5.3 %collective-permute-start.1 = (bf16[272,512]{1,0:T(8,128)(2,1)}, bf16[272,512]{1,0:T(8,128)(2,1)S(1)}, u32[]{:S(2)}, u32[]{:S(2)}) collective-permute-start(bf16[272,512]{1,0:T(8,128)(2,1)} %get-tuple-element.11), channel_id=1, source_target_pairs={{0,1},{1,0},{4,5},{5,4},{8,9},{9,8},{12,13},{13,12},{2,3},{3,2},{6... | collective-permute-start | bytes 835592 | tf_op jit(solution)/shard_map/ppermute | solution.py:411
  44.2 9.7 %collective-permute-start.2 = (bf16[272,512]{1,0:T(8,128)(2,1)}, bf16[272,512]{1,0:T(8,128)(2,1)S(1)}, u32[]{:S(2)}, u32[]{:S(2)}) collective-permute-start(bf16[272,512]{1,0:T(8,128)(2,1)} %get-tuple-element.12), channel_id=1, source_target_pairs={{0,4},{1,5},{4,0},{5,1},{8,12},{9,13},{12,8},{13,9},{2,6},{3,7},{6... | collective-permute-start | bytes 835592 | tf_op jit(solution)/shard_map/ppermute | solution.py:411
  44.2 13.8 %collective-permute-start.3 = (bf16[272,512]{1,0:T(8,128)(2,1)}, bf16[272,512]{1,0:T(8,128)(2,1)S(1)}, u32[]{:S(2)}, u32[]{:S(2)}) collective-permute-start(bf16[272,512]{1,0:T(8,128)(2,1)} %get-tuple-element.13), channel_id=1, source_target_pairs={{0,5},{1,4},{4,1},{5,0},{8,13},{9,12},{12,9},{13,8},{2,7},{3,6},{6... | collective-permute-start | bytes 835592 | tf_op jit(solution)/shard_map/ppermute | solution.py:411
  57.9 2.2 %copy-start.3 = (bf16[4,2,512,512]{3,2,1,0:T(8,128)(2,1)S(1)}, bf16[4,2,512,512]{3,2,1,0:T(8,128)(2,1)}, u32[]{:S(2)}) copy-start(bf16[4,2,512,512]{3,2,1,0:T(8,128)(2,1)} %constant.162.clone.table_ref) | copy-start | bytes 12582916
  64.7 8.3 %collective-permute-start.6 = (f32[256,128]{1,0:T(8,128)S(1)}, f32[256,128]{1,0:T(8,128)S(1)}, u32[]{:S(2)}, u32[]{:S(2)}) collective-permute-start(f32[256,128]{1,0:T(8,128)S(1)} %get-tuple-element.17), channel_id=1, source_target_pairs={{0,12},{4,8},{8,4},{12,0},{1,13},{5,9},{9,5},{13,1},{2,14},{6,10},... | collective-permute-start | bytes 393224 | tf_op jit(solution)/shard_map/ppermute | solution.py:439
  65.7 10.4 %collective-permute-start.4 = (f32[256,128]{1,0:T(8,128)S(1)}, f32[256,128]{1,0:T(8,128)S(1)}, u32[]{:S(2)}, u32[]{:S(2)}) collective-permute-start(f32[256,128]{1,0:T(8,128)S(1)} %get-tuple-element.15), channel_id=1, source_target_pairs={{0,4},{4,0},{8,12},{12,8},{1,5},{5,1},{9,13},{13,9},{2,6},{6,2},{1... | collective-permute-start | bytes 393224 | tf_op jit(solution)/shard_map/ppermute | solution.py:439
  66.0 13.1 %collective-permute-start.5 = (f32[256,128]{1,0:T(8,128)S(1)}, f32[256,128]{1,0:T(8,128)S(1)}, u32[]{:S(2)}, u32[]{:S(2)}) collective-permute-start(f32[256,128]{1,0:T(8,128)S(1)} %get-tuple-element.16), channel_id=1, source_target_pairs={{0,8},{4,12},{8,0},{12,4},{1,9},{5,13},{9,1},{13,5},{2,10},{6,14},... | collective-permute-start | bytes 393224 | tf_op jit(solution)/shard_map/ppermute | solution.py:439
  69.1 10.0 %collective-permute-start.7 = (f32[256,128]{1,0:T(8,128)S(1)}, f32[256,128]{1,0:T(8,128)S(1)}, u32[]{:S(2)}, u32[]{:S(2)}) collective-permute-start(f32[256,128]{1,0:T(8,128)S(1)} %get-tuple-element.14.rest_0_), channel_id=1, source_target_pairs={{0,1},{1,0},{2,3},{3,2},{4,5},{5,4},{6,7},{7,6},{8,9},{9,8},{10,11... | collective-permute-start | bytes 393224 | tf_op jit(solution)/shard_map/ppermute | solution.py:440
  73.0 6.2 %collective-permute-start.10 = (f32[256,128]{1,0:T(8,128)S(1)}, f32[256,128]{1,0:T(8,128)S(1)}, u32[]{:S(2)}, u32[]{:S(2)}) collective-permute-start(f32[256,128]{1,0:T(8,128)S(1)} %collective-permute-done.6.rest_3_), channel_id=1, source_target_pairs={{0,1},{1,0},{2,3},{3,2},{4,5},{5,4},{6,7},{7,6},{8,9},{9,8},{10,11... | collective-permute-start | bytes 393224 | tf_op jit(solution)/shard_map/ppermute | solution.py:440
  76.1 3.1 %collective-permute-start.8 = (f32[256,128]{1,0:T(8,128)S(1)}, f32[256,128]{1,0:T(8,128)S(1)}, u32[]{:S(2)}, u32[]{:S(2)}) collective-permute-start(f32[256,128]{1,0:T(8,128)S(1)} %collective-permute-done.4.rest_1_), channel_id=1, source_target_pairs={{0,1},{1,0},{2,3},{3,2},{4,5},{5,4},{6,7},{7,6},{8,9},{9,8},{10,11... | collective-permute-start | bytes 393224 | tf_op jit(solution)/shard_map/ppermute | solution.py:440
  79.1 1.3 %collective-permute-start.9 = (f32[256,128]{1,0:T(8,128)S(1)}, f32[256,128]{1,0:T(8,128)S(1)}, u32[]{:S(2)}, u32[]{:S(2)}) collective-permute-start(f32[256,128]{1,0:T(8,128)S(1)} %collective-permute-done.5.rest_2_), channel_id=1, source_target_pairs={{0,1},{1,0},{2,3},{3,2},{4,5},{5,4},{6,7},{7,6},{8,9},{9,8},{10,11... | collective-permute-start | bytes 393224 | tf_op jit(solution)/shard_map/ppermute | solution.py:440

commit v2 on v0

v2 whole, which is shorter than its diff:
```python
import functools
import math

import jax
import jax.numpy as jnp
import ml_dtypes
import numpy as np
from jax import lax
from jax.experimental import pallas as pl
from jax.experimental.pallas import tpu as pltpu
from jax.sharding import PartitionSpec as P

WCOLS = 128
WINDOW_MB = 57
TEMPLATE_MB = 16
PARTIAL_MB = 16
COLUMN_MB = 12
PAD = 16

two_pi = 2.0 * math.pi
BF16 = ml_dtypes.bfloat16


def params(mebibytes):
    return pltpu.CompilerParams(vmem_limit_bytes=mebibytes * 1024 * 1024)


def bits(count):
    return count.bit_length() - 1


def reverse_bits(number, digits):
    result = number * 0
    for digit in range(digits):
        result = result + number // (1 << digit) % 2 * (1 << digits - 1 - digit)
    return result


def phases(rows, cols, period):
    angles = np.outer(rows, cols) % period * (two_pi / period)
    return np.cos(angles), np.sin(angles)


def window_table(length, win, mirrored):
    ratio = length // win
    lanes = win // ratio
    sign = 1 if mirrored else -1
    base = np.arange(win)[:, None] + sign * ratio * np.arange(lanes)[None, :]
    d = (length // ratio * np.arange(ratio)[:, None, None] + base[None]) % length
    u = np.arange(win)
    kernel = np.exp(2j * np.pi * (np.outer(np.arange(length), u) % length) / length).sum(1) / win
    val = kernel[d]
    return np.concatenate([val.real, val.imag], 2).astype(BF16)


def tiles_of(re, im, lanes, axis):
    pieces = []
    for start in range(0, re.shape[axis], lanes):
        cut = [slice(None)] * re.ndim
        cut[axis] = slice(start, start + lanes)
        pieces += [re[tuple(cut)], im[tuple(cut)]]
    return np.concatenate(pieces, axis)


def template_table(tsize, win, lanes):
    cos, sin = phases(np.arange(tsize), np.arange(win), win)
    upper = tiles_of(cos, -sin, lanes, 1)
    lower = tiles_of(sin, cos, lanes, 1)
    return np.concatenate([upper, lower], 0).astype(BF16)


def split(table):
    upper = table.astype(BF16)
    return np.stack([upper, (table - upper.astype(np.float64)).astype(BF16)])


def back_table(win, lanes):
    cos, sin = phases(np.arange(win), np.arange(WCOLS), win)
    re_rows = np.concatenate([cos, sin], 1)
    im_rows = np.concatenate([-sin, cos], 1)
    table = tiles_of(re_rows, im_rows, lanes, 0)
    return split(table.reshape(win // lanes, 2 * lanes, 2 * WCOLS))


def column_table(length, classes, cores, band):
    steps = length // classes
    freqs = np.arange(cores * band)
    out = []
    for rho in range(classes):
        cos, sin = phases(rho + classes * np.arange(steps), freqs, length)
        out.append(tiles_of(cos, -sin, band, 1))
    return np.stack(out).astype(BF16)


def flip_table(band):
    out = np.zeros((band + PAD, band), np.float32)
    out[band - np.arange(band), np.arange(band)] = 1.0
    return out.astype(BF16)


def vmem(count):
    return [pl.BlockSpec(memory_space=pltpu.VMEM)] * count


def hbm(count):
    return [pl.BlockSpec(memory_space=pltpu.HBM)] * count


SMEM = pl.BlockSpec(memory_space=pltpu.SMEM)


def place():
    row, core = lax.axis_index("row"), lax.axis_index("orient")
    cores = lax.axis_size("orient")
    members = lax.axis_size("row") * cores // 2
    device = row * cores + core
    return row, core, members, device % members, device // members


def window_kernel(mirrored, place_ref, spec_ref, table_ref, out_ref):
    ratio, win, width = table_ref.shape
    lanes = width // 2
    rows = out_ref.shape[0]
    pieces = []
    for step in range(ratio):
        at = slice(step * win, (step + 1) * win)
        pieces += [spec_ref[0, part, :, at] for part in range(2)]
    stacked = jnp.concatenate(pieces, 0)
    got = [
        jnp.dot(stacked, table_ref[which], preferred_element_type=jnp.float32)
        for which in range(ratio)
    ]
    for part in range(ratio):
        re, im = 0.0, 0.0
        for which in range(ratio):
            step = (which - part if mirrored else which + part) % ratio
            re = re + got[which][2 * step * rows : (2 * step + 1) * rows]
            im = im + got[which][(2 * step + 1) * rows : (2 * step + 2) * rows]
        out_re = re[:, :lanes] - im[:, lanes:]
        out_im = re[:, lanes:] + im[:, :lanes]
        if mirrored:
            out_im = -out_im
        start = part * width
        out_ref[:, start : start + lanes] = out_re.astype(out_ref.dtype)
        out_ref[:, start + lanes : start + width] = out_im.astype(out_ref.dtype)


def windowed(spectra, table, place, rows, dtype, mirrored):
    ratio, win, width = table.shape
    length = ratio * win
    return pl.pallas_call(
        functools.partial(window_kernel, mirrored),
        out_shape=jax.ShapeDtypeStruct((rows, ratio * width), dtype),
        grid_spec=pltpu.PrefetchScalarGridSpec(
            num_scalar_prefetch=1,
            grid=(1,),
            in_specs=[
                pl.BlockSpec((1, 2, rows, length), lambda a, place: (place[0], 0, place[1], 0)),
                pl.BlockSpec(table.shape, lambda a, place: (0, 0, 0)),
            ],
            out_specs=pl.BlockSpec((rows, ratio * width), lambda a, place: (0, 0)),
        ),
        compiler_params=params(WINDOW_MB),
        cost_estimate=pl.CostEstimate(
            flops=4 * rows * length * ratio * width,
            bytes_accessed=2 * (2 * rows * length + length * width),
            transcendentals=0,
        ),
        name="windowed",
    )(place, spectra, table)


def template_kernel(index_ref, bank_ref, left_ref, right_ref, low_ref, high_ref, hold_low, hold_high):
    ratio, depth, width = right_ref.shape
    window, low = hold_low.shape[0], hold_low.shape[1]
    rows = left_ref.shape[1]
    left = jnp.concatenate([left_ref[0], left_ref[1]], 0)
    for o in range(window):
        values = bank_ref[index_ref[o]].astype(jnp.float32)
        centred = values - jnp.mean(values)
        factor = lax.rsqrt(jnp.mean(centred * centred) + 1e-06)
        template = (centred * factor).astype(jnp.bfloat16)
        rowpass = jnp.dot(left, template, preferred_element_type=jnp.float32).astype(jnp.bfloat16)
        both = jnp.concatenate([rowpass[:rows], rowpass[rows:]], 1)
        hold_low[o] = both[:low]
        hold_high[o] = both[low:]
    for hold, out in ((hold_low, low_ref), (hold_high, high_ref)):
        flat = hold[...].reshape(window * hold.shape[1], depth)
        for part in range(ratio):
            got = jnp.dot(flat, right_ref[part], preferred_element_type=jnp.float32)
            out[part] = got.astype(out.dtype)


def template_spectra(bank, orient_index, left, band, win, lanes, dtype):
    tsize = bank.shape[1]
    window = orient_index.shape[0]
    ratio = win // lanes
    right = template_table(tsize, win, lanes).reshape(2 * tsize, ratio, 2 * lanes)
    right = jnp.asarray(np.ascontiguousarray(right.transpose(1, 0, 2)))
    low, high = band // 2, band // 2 + PAD
    return pl.pallas_call(
        template_kernel,
        out_shape=[
            jax.ShapeDtypeStruct((ratio, window * low, 2 * lanes), dtype),
            jax.ShapeDtypeStruct((ratio, window * high, 2 * lanes), dtype),
        ],
        in_specs=[SMEM] + vmem(3),
        out_specs=vmem(2),
        scratch_shapes=[
            pltpu.VMEM((window, low, 2 * tsize), jnp.bfloat16),
            pltpu.VMEM((window, high, 2 * tsize), jnp.bfloat16),
        ],
        compiler_params=params(TEMPLATE_MB),
        cost_estimate=pl.CostEstimate(
            flops=2 * window * (band + PAD) * tsize * (2 * tsize + 4 * win),
            bytes_accessed=2 * (bank.size + window * (band + PAD) * 2 * win),
            transcendentals=0,
        ),
        name="templates",
    )(orient_index, bank, left, right)


def partial_kernel(count, first, keep_ref, flip_ref, tspec_ref, back_ref, *rest):
    other_refs, rest = rest[:count], rest[count:]
    part_ref, outs = rest[-1], rest[:-1]
    _, _, members, mine, _ = place()
    window = part_ref.shape[0]
    band = keep_ref.shape[0] // 2
    rows = flip_ref.shape[0]
    ratio, _, width = tspec_ref.shape
    lanes = width // 2
    received = jnp.concatenate([other[...] for other in other_refs], 0)
    held = jnp.dot(flip_ref[...], received, preferred_element_type=jnp.float32)
    head = held[:band] + keep_ref[first : first + band]
    held = head if rows == band else jnp.concatenate([head, held[band:]], 0)
    total = None
    for part in range(ratio):
        mic_re = held[:, part * width : part * width + lanes]
        mic_im = held[:, part * width + lanes : (part + 1) * width]
        upper, lower = [], []
        for o in range(window):
            tmpl_re = tspec_ref[part, o * rows : (o + 1) * rows, :lanes].astype(jnp.float32)
            tmpl_im = tspec_ref[part, o * rows : (o + 1) * rows, lanes:].astype(jnp.float32)
            prod_re = mic_re * tmpl_re + mic_im * tmpl_im
            prod_im = mic_im * tmpl_re - mic_re * tmpl_im
            product = jnp.concatenate([prod_re, prod_im], 1)
            rounded = product.astype(jnp.bfloat16)
            upper.append(rounded)
            lower.append((product - rounded.astype(jnp.float32)).astype(jnp.bfloat16))
        upper = jnp.concatenate(upper, 0)
        lower = jnp.concatenate(lower, 0)
        got = jnp.dot(upper, back_ref[0, part], preferred_element_type=jnp.float32)
        got += jnp.dot(lower, back_ref[0, part], preferred_element_type=jnp.float32)
        got += jnp.dot(upper, back_ref[1, part], preferred_element_type=jnp.float32)
        total = got if total is None else total + got
    for o in range(window):
        part_ref[o] = total[o * rows : (o + 1) * rows]

    group = WCOLS // members
    lane_group = lax.broadcasted_iota(jnp.int32, (rows, WCOLS), 1) // group
    tiles = max(1, window // members)
    for tile in range(tiles):
        for plane in range(2):
            at = slice(plane * WCOLS, (plane + 1) * WCOLS)
            pieces = []
            for i in range(members):
                piece = part_ref[(tile * members + i) % window, :, at]
                pieces.append(pltpu.roll(piece, group * i, 1) if i else piece)
            for s in range(members):
                target = lax.bitwise_xor(mine, s)
                packed = pieces[0]
                for i in range(1, members):
                    inside = (lane_group + (members - i)) % members == target
                    packed = jnp.where(inside, pieces[i], packed)
                start = (plane * tiles + tile) * WCOLS
                outs[s][:, start : start + WCOLS] = packed.astype(outs[s].dtype)


def partials(keep, others, first, flip, tspec, back, members, window):
    rows = flip.shape[0]
    ratio, _, width = tspec.shape
    tiles = max(1, window // members)
    out_shape = (rows, 2 * tiles * WCOLS)
    return pl.pallas_call(
        functools.partial(partial_kernel, len(others), first),
        out_shape=[jax.ShapeDtypeStruct(out_shape, jnp.bfloat16)] * members,
        in_specs=vmem(4 + len(others)),
        out_specs=vmem(members),
        scratch_shapes=[
            pltpu.VMEM((window, rows, 2 * WCOLS), jnp.float32),
        ],
        compiler_params=params(PARTIAL_MB),
        cost_estimate=pl.CostEstimate(
            flops=12 * tspec.size * WCOLS,
            bytes_accessed=2 * tspec.size,
            transcendentals=0,
        ),
        name="partials",
    )(keep, flip, tspec, back, *others)


def column_kernel(group_of, scale, share, roots_ref, *rest):
    row, core, members, mine, side = place()
    cores, classes = lax.axis_size("orient"), lax.axis_size("row")
    many = len(group_of)
    tables, rest = rest[:many], rest[many:]
    low_parts, high_parts = rest[:members], rest[members : 2 * members]
    outs = rest[2 * members : 2 * members + many]
    held_ref, last_ref = rest[2 * members + many :]
    steps = tables[0].shape[0]
    low, width = low_parts[0].shape
    band = held_ref.shape[1]
    wide = width // 2
    for s in range(members):
        member = lax.bitwise_xor(mine, s)
        held_ref[member, :low] = low_parts[s][...]
        held_ref[member, low:] = high_parts[s][: band - low]
        last_ref[member] = high_parts[s][band - low :]
    planes = []
    for member in range(members):
        block = held_ref[member]
        if member:
            head = block[:PAD].astype(jnp.float32) + last_ref[member - 1].astype(jnp.float32)
            block = jnp.concatenate([head.astype(jnp.bfloat16), block[PAD:]], 0)
        planes.append((block[:, :wide], block[:, wide:]))
    top = last_ref[members - 1][:1, :wide].astype(jnp.float32)
    group = WCOLS // members
    height = steps // (members // 2)
    lane_group = lax.broadcasted_iota(jnp.int32, (height, WCOLS), 1) // group
    kappa = (lane_group + (members - mine)) % members
    for which in range(many):
        rho = reverse_bits(lax.bitwise_xor(row, group_of[which]), bits(classes))
        corr = (1 - 2 * (rho % 2)).astype(jnp.float32) * top
        for turn in range(members // cores):
            angle = rho * turn % classes
            cos = roots_ref[0, angle].astype(jnp.bfloat16)
            sin = roots_ref[1, angle].astype(jnp.bfloat16)
            blocks = []
            for re, im in planes[turn * cores : (turn + 1) * cores]:
                blocks += [cos * re - sin * im, sin * re + cos * im] if turn else [re, im]
            stacked = jnp.concatenate(blocks, 0)
            corr = corr + jnp.dot(tables[which][...], stacked, preferred_element_type=jnp.float32)
        corr = corr * (scale * (1 - 2 * (side * rho % 2)).astype(jnp.float32))
        peak = corr[:, :WCOLS]
        power = corr[:, :WCOLS] * corr[:, :WCOLS]
        for start in range(WCOLS, wide, WCOLS):
            more = corr[:, start : start + WCOLS]
            peak = jnp.maximum(peak, more)
            power = power + more * more
        shift = group
        while shift < WCOLS:
            peak = jnp.maximum(peak, pltpu.roll(peak, shift, 1))
            power = power + pltpu.roll(power, shift, 1)
            shift *= 2
        if share != 1.0:
            power = power * share
        packed = peak[:height]
        for k in range(1, members):
            source = (power if k % 2 else peak)[k // 2 * height : (k // 2 + 1) * height]
            packed = jnp.where(kappa == k, source, packed)
        outs[which][...] = packed.astype(outs[which].dtype)


def columns(parts, tables, group_of, classes, band, scale, share, dtype):
    members = len(parts) // 2
    many = len(group_of)
    steps = tables[0].shape[0]
    height = steps // (members // 2)
    width = parts[0].shape[1]
    roots = np.round(np.exp(2j * np.pi * np.arange(classes) / classes), 12)
    roots = jnp.asarray(np.stack([roots.real, roots.imag]).astype(np.float32))
    return pl.pallas_call(
        functools.partial(column_kernel, group_of, scale, share),
        out_shape=[jax.ShapeDtypeStruct((height, WCOLS), dtype)] * many,
        in_specs=[SMEM] + vmem(many + 2 * members),
        out_specs=vmem(many),
        scratch_shapes=[
            pltpu.VMEM((members, band, width), jnp.bfloat16),
            pltpu.VMEM((members, PAD, width), jnp.bfloat16),
        ],
        compiler_params=params(COLUMN_MB),
        cost_estimate=pl.CostEstimate(
            flops=many * 2 * tables[0].size * width // 2,
            bytes_accessed=2 * many * tables[0].size,
            transcendentals=0,
        ),
        name="columns",
    )(roots, *tables, *parts)


def unpack_kernel(classes, *rest):
    near = rest[:classes]
    far = rest[classes : 2 * classes]
    peak_ref, power_ref = rest[2 * classes :]
    row, core, members, _, side = place()
    half = classes // 2
    height = near[0].shape[0]
    group = WCOLS // members
    lane_group = lax.broadcasted_iota(jnp.int32, (height, WCOLS), 1) // group
    for delta in range(2):
        mic = lax.bitwise_xor(side, delta)
        for k in range(members):
            wanted = (lane_group + (members - k)) % members
            value = jnp.zeros((height, WCOLS), jnp.float32)
            for low in range(half):
                s = delta * half + low
                base = lax.bitwise_xor(row, s) % half * 2
                for source, at in ((near, core), (far, 1 - core)):
                    value = jnp.where(wanted == base + at, source[s][...].astype(jnp.float32), value)
            if k:
                value = pltpu.roll(value, WCOLS - k * group, 1)
            target = power_ref if k % 2 else peak_ref
            target[mic, 0, k // 2 * height : (k // 2 + 1) * height, :] = value


def unpack(near, far, steps):
    classes = len(near)
    shape = jax.ShapeDtypeStruct((2, 1, steps, WCOLS), jnp.float32)
    return pl.pallas_call(
        functools.partial(unpack_kernel, classes),
        out_shape=[shape, shape],
        in_specs=vmem(2 * classes),
        out_specs=vmem(2),
        compiler_params=params(8),
        name="unpack",
    )(*near, *far)


def shards(spectra, bank, orient_index):
    length = spectra.shape[3]
    tsize = bank.shape[1]
    classes = lax.axis_size("row")
    cores = lax.axis_size("orient")
    count = classes * cores
    members = count // 2
    band = length // count
    steps = length // classes
    win = 1 << (tsize + WCOLS - 2).bit_length()
    lanes = win // (length // win)
    line = ("row", "orient")
    window = orient_index.shape[0]
    rows = band // 2

    row, core, _, _, side = place()
    device = row * cores + core
    mirror_table = jnp.asarray(window_table(length, win, True))
    table = jnp.asarray(window_table(length, win, False))
    back = jnp.asarray(back_table(win, lanes))
    flip = flip_table(band)

    opposite = [(i, count - 1 - i) for i in range(count)]
    others = []
    for block in (1, 0):
        at = jnp.stack([1 - side, 2 * core + block]).astype(jnp.int32)
        sent = windowed(spectra, mirror_table, at, rows, jnp.bfloat16, True)
        others.insert(0, lax.ppermute(sent, line, opposite))
    cos, sin = phases(np.arange(length + PAD), np.arange(tsize), length)
    left = jnp.asarray(np.stack([cos, -sin]).astype(BF16))
    left = lax.dynamic_slice_in_dim(left, device * band, band + PAD, 1)
    spectra, bank, left, _ = lax.optimization_barrier((spectra, bank, left, sent))
    at = jnp.stack([side, core]).astype(jnp.int32)
    keep = windowed(spectra, table, at, band, jnp.float32, False)
    bank, left, keep = lax.optimization_barrier((bank, left, keep))
    tspec = template_spectra(bank, orient_index, left, band, win, lanes, jnp.float32)
    lows, highs = [], []
    for block, got in ((0, lows), (1, highs)):
        parts = partials(
            keep,
            others[1 - block :],
            block * rows,
            jnp.asarray(flip[:rows, rows:] if block == 0 else flip[rows:]),
            tspec[block],
            back,
            members,
            window,
        )
        got.append(parts[0])
        for s in range(1, members):
            got.append(lax.ppermute(parts[s], line, [(i, i ^ s) for i in range(count)]))

    all_tables = jnp.asarray(column_table(length, classes, cores, band))
    row, _ = lax.optimization_barrier((row, parts[0]))
    maps = [None] * classes
    for group in (range(classes // 2, classes), range(classes // 2)):
        rhos = [reverse_bits(lax.bitwise_xor(row, s), bits(classes)) for s in group]
        made = columns(
            lows + highs,
            [lax.dynamic_index_in_dim(all_tables, rho, 0, False) for rho in rhos],
            tuple(group),
            classes,
            band,
            1.0 / (length * tsize),
            window / max(window, members),
            jnp.float32,
        )
        for s, one in zip(group, made):
            maps[s] = one
    near = [maps[0]]
    for s in range(1, classes):
        near.append(lax.ppermute(maps[s], "row", [(i, i ^ s) for i in range(classes)]))
    far = [lax.ppermute(m, "orient", [(0, 1), (1, 0)]) for m in near]
    peak, power = unpack(near, far, steps)
    return peak, power


def solution(mesh):
    return jax.shard_map(
        shards,
        mesh=mesh,
        in_specs=(P(("grp", "mic"), None, "row", None), P(), P("grp")),
        out_specs=(P(("grp", "mic"), "row", None, None), P(("grp", "mic"), "row", None, None)),
        check_vma=False,
    )
```

time: 674 us -> 70.7 us (0.10); the launches traced: 666 us -> 70.4 us
  waiting for transfers between devices: 484 us -> 16.5 us
  other arithmetic: 104 us -> 1.17 us
  matrix products: 49.5 us -> 0 us
  Pallas kernels: 0 us -> 33.6 us
  between operations: 14.6 us -> 0.98 us
  starting transfers between devices: 3.02 us -> 14.5 us
    ppermute x2 -> x15, waiting for transfers between devices: 268 us -> 16.5 us  [the longest x3 7.68 us: shards(): lax.ppermute(maps[s], 'row', [(i, i ^ s) for i in range(classes)])]
    all_gather x3 -> x0, waiting for transfers between devices: 216 us -> none  [the longest x1 197 us: shards(): piece = lax.all_gather(own_spectra, 'mic', axis=3, tiled=True)]
    dot_general x6 -> x0, matrix products: 49.5 us -> none  [the longest x1 18 us: shards(): jnp.einsum('oax,xk->oak', rowpass, right_table, preferred_element_type=jn...]
    another operation x9 -> x2, other arithmetic: 45.8 us -> 1.17 us  [shards(): at = jnp.stack([1 - side, 2 * core + block]).astype(jnp.int32)]
    pallas_call x0 -> x9, Pallas kernels: none -> 33.6 us  [the longest x3 14.7 us: windowed(): pl.pallas_call(functools.partial(window_kernel, mirrored), out_shape=jax....]
    convert_element_type x4 -> x0, other arithmetic: 29.4 us -> none  [the longest x1 14.2 us: shards(): tmpl_re = piece[orient_pos, 0].astype(jnp.float32)]
    ppermute x2 -> x15, starting transfers between devices: 2.9 us -> 14.5 us  [the longest x3 5.16 us: shards(): lax.ppermute(maps[s], 'row', [(i, i ^ s) for i in range(classes)])]
    sub x8 -> x0, other arithmetic: 9.3 us -> none  [the longest x2 8.04 us: shards(): differ = partner - values]
  transfers between devices with their start and end apart: 5 -> 15, of which waited for: 5 -> 7; matrix products, arithmetic and copies ran while one was open for 2% -> 6% of each run, Pallas kernels for 0% -> 37%
where the time goes in v2:
time: 70.7 us; the launch traced here: 70.4 us
  Pallas kernels  33.6 us (48%)
  waiting for transfers between devices  16.5 us (23%)
  starting transfers between devices  14.5 us (21%)
  local copies, waits for them, and re-layouts  3.71 us (5%)
  other arithmetic  1.17 us (2%)
  between operations  0.98 us (1%)
    pallas_call x3, Pallas kernels, windowed(): pl.pallas_call(functools.partial(window_kernel, mirrored), out_shape=jax....  14.7 us
    pallas_call x1, Pallas kernels, template_spectra(): pl.pallas_call(template_kernel, out_shape=[jax.ShapeDtypeStruct((ratio, w...  7.9 us
    ppermute x3, waiting for transfers between devices, shards(): lax.ppermute(maps[s], 'row', [(i, i ^ s) for i in range(classes)])  7.68 us
    ppermute x6, waiting for transfers between devices, shards(): got.append(lax.ppermute(parts[s], line, [(i, i ^ s) for i in range(count)]))  7.51 us
    ppermute x3, starting transfers between devices, shards(): lax.ppermute(maps[s], 'row', [(i, i ^ s) for i in range(classes)])  5.16 us
    pallas_call x2, Pallas kernels, partials(): pl.pallas_call(functools.partial(partial_kernel, len(others), first), out...  4.99 us
    pallas_call x2, Pallas kernels, columns(): pl.pallas_call(functools.partial(column_kernel, group_of, scale, share),...  4.73 us
    ppermute x2, starting transfers between devices, shards(): others.insert(0, lax.ppermute(sent, line, opposite))  4.49 us
  transfers between devices with their start and end apart: 15, of which 7 were waited for; matrix products, arithmetic and copies ran while one was open for 6% of the time, Pallas kernels for 37%

profile of v2, /device:TPU:0, one launch (start us, length us, event | category | flops | bytes accessed | tf_op | source)
XLA Modules:
  0.0 70.4 jit_solution(18419723397754045594)
XLA Ops:
  0.7 0.6 pad_add_fusion.2.place_ref
  1.2 4.2 %windowed.5 = bf16[128,1024]{1,0:T(8,128)(2,1)} custom-call(s32[2]{0:T(128)} %pad_add_fusion.2.place_ref, bf16[2,2,512,2048]{3,2,1,0:T(8,128)(2,1)} %spec_ref.4, bf16[4,512,256]{2,1,0:T(8,128)(2,1)} %constant.157.clone.table_ref), custom_call_target="tpu_custom_call" | custom-call | flops 1073741824 | bytes 2097152 | tf_op jit(solution)/shard_map/windowed/pallas_call | solution.py:151
  5.4 4.5 %collective-permute-start.1 = (bf16[128,1024]{1,0:T(8,128)(2,1)}, bf16[128,1024]{1,0:T(8,128)(2,1)S(1)}, u32[]{:S(2)}, u32[]{:S(2)}) collective-permute-start(bf16[128,1024]{1,0:T(8,128)(2,1)} %windowed.5), channel_id=1, source_target_pairs={{0,13},{1,12},{4,9},{5,8},{8,5},{9,4},{12,1},{13,0},{2,15},{3,14},... | collective-permute-start | bytes 786440 | tf_op jit(solution)/shard_map/ppermute | solution.py:456
  9.9 0.6 pad_add_fusion
  10.5 4.2 %windowed.3 = bf16[128,1024]{1,0:T(8,128)(2,1)} custom-call(s32[2]{0:T(128)} %get-tuple-element.48.place_ref, bf16[2,2,512,2048]{3,2,1,0:T(8,128)(2,1)} %spec_ref.4, bf16[4,512,256]{2,1,0:T(8,128)(2,1)} %constant.157.clone.table_ref), custom_call_target="tpu_custom_call" | custom-call | flops 1073741824 | bytes 2097152 | tf_op jit(solution)/shard_map/windowed/pallas_call | solution.py:151
  14.6 1.0 %constant_dynamic-slice_fusion.left_ref = bf16[2,272,384]{2,1,0:T(8,128)(2,1)S(1)} fusion(bf16[2,2064,384]{2,1,0:T(8,128)(2,1)} %constant.160.clone, s32[]{:T(128)S(6)} %select_n.71), kind=kLoop, calls=%fused_computation.4 | loop fusion | bytes 835588 | tf_op jit(solution)/shard_map/dynamic_slice | solution.py:459
  15.7 6.4 %windowed.4.keep_ref = f32[256,1024]{1,0:T(8,128)} custom-call(s32[2]{0:T(128)} %get-tuple-element.49.place_ref, bf16[2,2,512,2048]{3,2,1,0:T(8,128)(2,1)} %spec_ref.4, bf16[4,512,256]{2,1,0:T(8,128)(2,1)} %constant.158.clone.table_ref), custom_call_target="tpu_custom_call" | custom-call | flops 2147483648 | bytes 3145728 | tf_op jit(solution)/shard_map/windowed/pallas_call | solution.py:151
  22.1 7.9 %templates.1 = (f32[4,1024,256]{2,1,0:T(8,128)S(1)}, f32[4,1152,256]{2,1,0:T(8,128)S(1)}) custom-call(s32[8]{0:T(128)S(1)} %copy-done.6, bf16[8,384,384]{2,1,0:T(8,128)(2,1)S(1)} %copy-done.5, bf16[2,272,384]{2,1,0:T(8,128)(2,1)S(1)} %constant_dynamic-slice_fusion.left_ref, bf16[4,768,256]{2,1,0:T(8,128)(2,1)S(1)} %copy-done.7), custom_call_target="tpu_custom_call" | custom-call | flops 4706009088 | bytes 6815744 | tf_op jit(solution)/shard_map/templates/pallas_call | solution.py:201
  30.1 2.3 %partials.3 = (bf16[128,512]{1,0:T(8,128)(2,1)S(1)}, bf16[128,512]{1,0:T(8,128)(2,1)S(1)}, bf16[128,512]{1,0:T(8,128)(2,1)S(1)}, bf16[128,512]{1,0:T(8,128)(2,1)S(1)}) custom-call(f32[256,1024]{1,0:T(8,128)S(1)} %copy-done, bf16[128,128]{1,0:T(8,128)(2,1)S(1)} %copy-done.3, f32[4,1024,256]{2,1,0:T(8,128)S(1)} %get-tuple-element.32.tspec_ref, ...), custom_call_target="tpu_custom_call" | custom-call | flops 1610612736 | bytes 2097152 | tf_op jit(solution)/shard_map/partials/pallas_call | solution.py:284
  32.4 0.7 %collective-permute-start.2 = (bf16[128,512]{1,0:T(8,128)(2,1)S(1)}, bf16[128,512]{1,0:T(8,128)(2,1)S(1)}, u32[]{:S(2)}, u32[]{:S(2)}) collective-permute-start(bf16[128,512]{1,0:T(8,128)(2,1)S(1)} %get-tuple-element.34), channel_id=1, source_target_pairs={{0,1},{1,0},{4,5},{5,4},{8,9},{9,8},{12,13},{13,12},{2,3},{3,2},{6... | collective-permute-start | bytes 393224 | tf_op jit(solution)/shard_map/ppermute | solution.py:479
  33.2 2.7 %partials.2 = (bf16[144,512]{1,0:T(8,128)(2,1)S(1)}, bf16[144,512]{1,0:T(8,128)(2,1)S(1)}, bf16[144,512]{1,0:T(8,128)(2,1)S(1)}, bf16[144,512]{1,0:T(8,128)(2,1)S(1)}) custom-call(f32[256,1024]{1,0:T(8,128)S(1)} %copy-done, bf16[144,256]{1,0:T(8,128)(2,1)S(1)} %copy-done.2, f32[4,1152,256]{2,1,0:T(8,128)S(1)} %get-tuple-element.29.tspec_ref, ...), custom_call_target="tpu_custom_call" | custom-call | flops 1811939328 | bytes 2359296 | tf_op jit(solution)/shard_map/partials/pallas_call | solution.py:284
  36.0 0.9 %collective-permute-start.3 = (bf16[128,512]{1,0:T(8,128)(2,1)S(1)}, bf16[128,512]{1,0:T(8,128)(2,1)S(1)}, u32[]{:S(2)}, u32[]{:S(2)}) collective-permute-start(bf16[128,512]{1,0:T(8,128)(2,1)S(1)} %get-tuple-element.35), channel_id=1, source_target_pairs={{0,4},{1,5},{4,0},{5,1},{8,12},{9,13},{12,8},{13,9},{2,6},{3,7},{6... | collective-permute-start | bytes 393224 | tf_op jit(solution)/shard_map/ppermute | solution.py:479
  36.9 0.6 collective-permute-start.4
  37.5 0.8 %collective-permute-start.5 = (bf16[144,512]{1,0:T(8,128)(2,1)S(1)}, bf16[144,512]{1,0:T(8,128)(2,1)S(1)}, u32[]{:S(2)}, u32[]{:S(2)}) collective-permute-start(bf16[144,512]{1,0:T(8,128)(2,1)S(1)} %get-tuple-element.37), channel_id=1, source_target_pairs={{0,1},{1,0},{4,5},{5,4},{8,9},{9,8},{12,13},{13,12},{2,3},{3,2},{6... | collective-permute-start | bytes 442376 | tf_op jit(solution)/shard_map/ppermute | solution.py:479
  38.2 0.8 %collective-permute-start.6 = (bf16[144,512]{1,0:T(8,128)(2,1)S(1)}, bf16[144,512]{1,0:T(8,128)(2,1)S(1)}, u32[]{:S(2)}, u32[]{:S(2)}) collective-permute-start(bf16[144,512]{1,0:T(8,128)(2,1)S(1)} %get-tuple-element.38), channel_id=1, source_target_pairs={{0,4},{1,5},{4,0},{5,1},{8,12},{9,13},{12,8},{13,9},{2,6},{3,7},{6... | collective-permute-start | bytes 442376 | tf_op jit(solution)/shard_map/ppermute | solution.py:479
  39.0 0.6 collective-permute-start.7
  39.6 2.6 %dynamic-slice_bitcast_fusion = (bf16[512,1024]{1,0:T(8,128)(2,1)S(1)}, bf16[512,1024]{1,0:T(8,128)(2,1)S(1)}, bf16[512,1024]{1,0:T(8,128)(2,1)S(1)}, bf16[512,1024]{1,0:T(8,128)(2,1)S(1)}) fusion(bf16[4,512,1024]{2,1,0:T(8,128)(2,1)} %constant.164.clone, s32[]{:T(128)S(6)} %select_n.88, s32[]{:T(128)S(6)} %select_n.80, s32[]{:T(128)S(6)} %select_n.76, ...), kind=kLoop, calls=%fused_computation | loop fusion | bytes 8388624 | tf_op jit(solution)/shard_map/jit(dynamic_index_in_dim)/squeeze | solution.py:488
  42.2 0.2 collective-permute-done.3.rest_4_
  42.4 1.1 %collective-permute-done.4.rest_5_ = bf16[128,512]{1,0:T(8,128)(2,1)S(1)} collective-permute-done((bf16[128,512]{1,0:T(8,128)(2,1)S(1)}, bf16[128,512]{1,0:T(8,128)(2,1)S(1)}, u32[]{:S(2)}, u32[]{:S(2)}) %collective-permute-start.4) | collective-permute-done | bytes 131104 | tf_op jit(solution)/shard_map/ppermute | solution.py:479
  43.6 4.8 %collective-permute-done.6.rest_8_ = bf16[144,512]{1,0:T(8,128)(2,1)S(1)} collective-permute-done((bf16[144,512]{1,0:T(8,128)(2,1)S(1)}, bf16[144,512]{1,0:T(8,128)(2,1)S(1)}, u32[]{:S(2)}, u32[]{:S(2)}) %collective-permute-start.6) | collective-permute-done | bytes 147488 | tf_op jit(solution)/shard_map/ppermute | solution.py:479
  48.4 1.3 %collective-permute-done.7.rest_9_ = bf16[144,512]{1,0:T(8,128)(2,1)S(1)} collective-permute-done((bf16[144,512]{1,0:T(8,128)(2,1)S(1)}, bf16[144,512]{1,0:T(8,128)(2,1)S(1)}, u32[]{:S(2)}, u32[]{:S(2)}) %collective-permute-start.7) | collective-permute-done | bytes 147488 | tf_op jit(solution)/shard_map/ppermute | solution.py:479
  49.7 2.4 %columns.3 = (f32[256,128]{1,0:T(8,128)S(1)}, f32[256,128]{1,0:T(8,128)S(1)}) custom-call(f32[2,4]{1,0:T(2,128)S(1)} %copy-done.4, bf16[512,1024]{1,0:T(8,128)(2,1)S(1)} %get-tuple-element.47.rest_0_, bf16[512,1024]{1,0:T(8,128)(2,1)S(1)} %get-tuple-element.44.rest_1_, bf16[128,512]{1,0:T(8,128)(2,1)S(1)} %get-tuple-element.33.rest_2_, ...), custom_call_target="tpu_custom_call" | custom-call | flops 536870912 | bytes 2097152 | tf_op jit(solution)/shard_map/columns/pallas_call | solution.py:372
  52.1 3.5 %collective-permute-start.9 = (f32[256,128]{1,0:T(8,128)S(1)}, f32[256,128]{1,0:T(8,128)S(1)}, u32[]{:S(2)}, u32[]{:S(2)}) collective-permute-start(f32[256,128]{1,0:T(8,128)S(1)} %get-tuple-element.42), channel_id=1, source_target_pairs={{0,8},{4,12},{8,0},{12,4},{1,9},{5,13},{9,1},{13,5},{2,10},{6,14},... | collective-permute-start | bytes 393224 | tf_op jit(solution)/shard_map/ppermute | solution.py:500
  55.6 1.1 %collective-permute-start.10 = (f32[256,128]{1,0:T(8,128)S(1)}, f32[256,128]{1,0:T(8,128)S(1)}, u32[]{:S(2)}, u32[]{:S(2)}) collective-permute-start(f32[256,128]{1,0:T(8,128)S(1)} %get-tuple-element.43), channel_id=1, source_target_pairs={{0,12},{4,8},{8,4},{12,0},{1,13},{5,9},{9,5},{13,1},{2,14},{6,10},... | collective-permute-start | bytes 393224 | tf_op jit(solution)/shard_map/ppermute | solution.py:500
  56.7 2.4 %columns.2 = (f32[256,128]{1,0:T(8,128)S(1)}, f32[256,128]{1,0:T(8,128)S(1)}) custom-call(f32[2,4]{1,0:T(2,128)S(1)} %copy-done.4, bf16[512,1024]{1,0:T(8,128)(2,1)S(1)} %get-tuple-element.46.rest_0_, bf16[512,1024]{1,0:T(8,128)(2,1)S(1)} %get-tuple-element.45.rest_1_, bf16[128,512]{1,0:T(8,128)(2,1)S(1)} %get-tuple-element.33.rest_2_, ...), custom_call_target="tpu_custom_call" | custom-call | flops 536870912 | bytes 2097152 | tf_op jit(solution)/shard_map/columns/pallas_call | solution.py:372
  59.1 0.5 collective-permute-start.8
  59.6 5.9 %collective-permute-done.9.rest_2_ = f32[256,128]{1,0:T(8,128)S(1)} collective-permute-done((f32[256,128]{1,0:T(8,128)S(1)}, f32[256,128]{1,0:T(8,128)S(1)}, u32[]{:S(2)}, u32[]{:S(2)}) %collective-permute-start.9) | collective-permute-done | bytes 131104 | tf_op jit(solution)/shard_map/ppermute | solution.py:500
  65.6 0.5 collective-permute-start.14
  66.1 1.7 %collective-permute-done.8.rest_1_ = f32[256,128]{1,0:T(8,128)S(1)} collective-permute-done((f32[256,128]{1,0:T(8,128)S(1)}, f32[256,128]{1,0:T(8,128)S(1)}, u32[]{:S(2)}, u32[]{:S(2)}) %collective-permute-start.8) | collective-permute-done | bytes 131104 | tf_op jit(solution)/shard_map/ppermute | solution.py:500
  67.8 0.0 collective-permute-start.12
  67.8 1.3 %collective-permute-done.12.rest_5_ = f32[256,128]{1,0:T(8,128)S(1)} collective-permute-done((f32[256,128]{1,0:T(8,128)S(1)}, f32[256,128]{1,0:T(8,128)S(1)}, u32[]{:S(2)}, u32[]{:S(2)}) %collective-permute-start.12) | collective-permute-done | bytes 131104 | tf_op jit(solution)/shard_map/ppermute | solution.py:501
  69.2 1.2 %unpack.1 = (f32[2,1,512,128]{3,2,1,0:T(8,128)}, f32[2,1,512,128]{3,2,1,0:T(8,128)}) custom-call(f32[256,128]{1,0:T(8,128)S(1)} %get-tuple-element.40.rest_0_, f32[256,128]{1,0:T(8,128)S(1)} %collective-permute-done.8.rest_1_, f32[256,128]{1,0:T(8,128)S(1)} %collective-permute-done.9.rest_2_, f32[256,128]{1,0:T(8,128)S(1)} %collective-permute-done.10.rest_3_, ...), custom_call_target="tpu_custom_call" | custom-call | tf_op jit(solution)/shard_map/unpack/pallas_call | solution.py:419
  (27 shorter events, 0.1 us)
Async XLA Ops:
  5.4 24.7 %collective-permute-start.1 = (bf16[128,1024]{1,0:T(8,128)(2,1)}, bf16[128,1024]{1,0:T(8,128)(2,1)S(1)}, u32[]{:S(2)}, u32[]{:S(2)}) collective-permute-start(bf16[128,1024]{1,0:T(8,128)(2,1)} %windowed.5), channel_id=1, source_target_pairs={{0,13},{1,12},{4,9},{5,8},{8,5},{9,4},{12,1},{13,0},{2,15},{3,14},... | collective-permute-start | bytes 786440 | tf_op jit(solution)/shard_map/ppermute | solution.py:456
  14.6 18.5 %collective-permute-start = (bf16[128,1024]{1,0:T(8,128)(2,1)}, bf16[128,1024]{1,0:T(8,128)(2,1)S(1)}, u32[]{:S(2)}, u32[]{:S(2)}) collective-permute-start(bf16[128,1024]{1,0:T(8,128)(2,1)} %windowed.3), channel_id=1, source_target_pairs={{0,13},{1,12},{4,9},{5,8},{8,5},{9,4},{12,1},{13,0},{2,15},{3,14},... | collective-permute-start | bytes 786440 | tf_op jit(solution)/shard_map/ppermute | solution.py:456
  15.7 6.4 %copy-start.5 = (bf16[8,384,384]{2,1,0:T(8,128)(2,1)S(1)}, bf16[8,384,384]{2,1,0:T(8,128)(2,1)}, u32[]{:S(2)}) copy-start(bf16[8,384,384]{2,1,0:T(8,128)(2,1)} %bank_ref) | copy-start | bytes 7077892
  15.7 6.4 %copy-start.6 = (s32[8]{0:T(128)S(1)}, s32[8]{0:T(128)}, u32[]{:S(2)}) copy-start(s32[8]{0:T(128)} %index_ref.1) | copy-start | bytes 100
  15.7 6.4 %copy-start.7 = (bf16[4,768,256]{2,1,0:T(8,128)(2,1)S(1)}, bf16[4,768,256]{2,1,0:T(8,128)(2,1)}, u32[]{:S(2)}) copy-start(bf16[4,768,256]{2,1,0:T(8,128)(2,1)} %constant.161.clone.right_ref) | copy-start | bytes 4718596
  22.1 8.0 %copy-start = (f32[256,1024]{1,0:T(8,128)S(1)}, f32[256,1024]{1,0:T(8,128)}, u32[]{:S(2)}) copy-start(f32[256,1024]{1,0:T(8,128)} %windowed.4.keep_ref) | copy-start | bytes 3145732
  22.1 8.0 %copy-start.1 = (bf16[2,4,256,256]{3,2,1,0:T(8,128)(2,1)S(1)}, bf16[2,4,256,256]{3,2,1,0:T(8,128)(2,1)}, u32[]{:S(2)}) copy-start(bf16[2,4,256,256]{3,2,1,0:T(8,128)(2,1)} %constant.159.clone.back_ref) | copy-start | bytes 3145732
  22.1 8.0 %copy-start.3 = (bf16[128,128]{1,0:T(8,128)(2,1)S(1)}, bf16[128,128]{1,0:T(8,128)(2,1)}, u32[]{:S(2)}) copy-start(bf16[128,128]{1,0:T(8,128)(2,1)} %constant.162.clone.flip_ref) | copy-start | bytes 98308
  30.0 3.1 %copy-start.2 = (bf16[144,256]{1,0:T(8,128)(2,1)S(1)}, bf16[144,256]{1,0:T(8,128)(2,1)}, u32[]{:S(2)}) copy-start(bf16[144,256]{1,0:T(8,128)(2,1)} %constant.163.clone.flip_ref) | copy-start | bytes 221188
  32.4 6.6 %collective-permute-start.2 = (bf16[128,512]{1,0:T(8,128)(2,1)S(1)}, bf16[128,512]{1,0:T(8,128)(2,1)S(1)}, u32[]{:S(2)}, u32[]{:S(2)}) collective-permute-start(bf16[128,512]{1,0:T(8,128)(2,1)S(1)} %get-tuple-element.34), channel_id=1, source_target_pairs={{0,1},{1,0},{4,5},{5,4},{8,9},{9,8},{12,13},{13,12},{2,3},{3,2},{6... | collective-permute-start | bytes 393224 | tf_op jit(solution)/shard_map/ppermute | solution.py:479
  36.0 6.4 %collective-permute-start.3 = (bf16[128,512]{1,0:T(8,128)(2,1)S(1)}, bf16[128,512]{1,0:T(8,128)(2,1)S(1)}, u32[]{:S(2)}, u32[]{:S(2)}) collective-permute-start(bf16[128,512]{1,0:T(8,128)(2,1)S(1)} %get-tuple-element.35), channel_id=1, source_target_pairs={{0,4},{1,5},{4,0},{5,1},{8,12},{9,13},{12,8},{13,9},{2,6},{3,7},{6... | collective-permute-start | bytes 393224 | tf_op jit(solution)/shard_map/ppermute | solution.py:479
  36.9 6.7 %collective-permute-start.4 = (bf16[128,512]{1,0:T(8,128)(2,1)S(1)}, bf16[128,512]{1,0:T(8,128)(2,1)S(1)}, u32[]{:S(2)}, u32[]{:S(2)}) collective-permute-start(bf16[128,512]{1,0:T(8,128)(2,1)S(1)} %get-tuple-element.36), channel_id=1, source_target_pairs={{0,5},{1,4},{4,1},{5,0},{8,13},{9,12},{12,9},{13,8},{2,7},{3,6},{6... | collective-permute-start | bytes 393224 | tf_op jit(solution)/shard_map/ppermute | solution.py:479
  37.5 6.1 %collective-permute-start.5 = (bf16[144,512]{1,0:T(8,128)(2,1)S(1)}, bf16[144,512]{1,0:T(8,128)(2,1)S(1)}, u32[]{:S(2)}, u32[]{:S(2)}) collective-permute-start(bf16[144,512]{1,0:T(8,128)(2,1)S(1)} %get-tuple-element.37), channel_id=1, source_target_pairs={{0,1},{1,0},{4,5},{5,4},{8,9},{9,8},{12,13},{13,12},{2,3},{3,2},{6... | collective-permute-start | bytes 442376 | tf_op jit(solution)/shard_map/ppermute | solution.py:479
  38.2 10.2 %collective-permute-start.6 = (bf16[144,512]{1,0:T(8,128)(2,1)S(1)}, bf16[144,512]{1,0:T(8,128)(2,1)S(1)}, u32[]{:S(2)}, u32[]{:S(2)}) collective-permute-start(bf16[144,512]{1,0:T(8,128)(2,1)S(1)} %get-tuple-element.38), channel_id=1, source_target_pairs={{0,4},{1,5},{4,0},{5,1},{8,12},{9,13},{12,8},{13,9},{2,6},{3,7},{6... | collective-permute-start | bytes 442376 | tf_op jit(solution)/shard_map/ppermute | solution.py:479
  39.0 10.7 %copy-start.4 = (f32[2,4]{1,0:T(2,128)S(1)}, f32[2,4]{1,0:T(2,128)}, u32[]{:S(2)}) copy-start(f32[2,4]{1,0:T(2,128)} %constant.165.clone.roots_ref) | copy-start | bytes 100
  39.0 10.7 %collective-permute-start.7 = (bf16[144,512]{1,0:T(8,128)(2,1)S(1)}, bf16[144,512]{1,0:T(8,128)(2,1)S(1)}, u32[]{:S(2)}, u32[]{:S(2)}) collective-permute-start(bf16[144,512]{1,0:T(8,128)(2,1)S(1)} %get-tuple-element.39), channel_id=1, source_target_pairs={{0,5},{1,4},{4,1},{5,0},{8,13},{9,12},{12,9},{13,8},{2,7},{3,6},{6... | collective-permute-start | bytes 442376 | tf_op jit(solution)/shard_map/ppermute | solution.py:479
  52.1 13.5 %collective-permute-start.9 = (f32[256,128]{1,0:T(8,128)S(1)}, f32[256,128]{1,0:T(8,128)S(1)}, u32[]{:S(2)}, u32[]{:S(2)}) collective-permute-start(f32[256,128]{1,0:T(8,128)S(1)} %get-tuple-element.42), channel_id=1, source_target_pairs={{0,8},{4,12},{8,0},{12,4},{1,9},{5,13},{9,1},{13,5},{2,10},{6,14},... | collective-permute-start | bytes 393224 | tf_op jit(solution)/shard_map/ppermute | solution.py:500
  55.6 10.0 %collective-permute-start.10 = (f32[256,128]{1,0:T(8,128)S(1)}, f32[256,128]{1,0:T(8,128)S(1)}, u32[]{:S(2)}, u32[]{:S(2)}) collective-permute-start(f32[256,128]{1,0:T(8,128)S(1)} %get-tuple-element.43), channel_id=1, source_target_pairs={{0,12},{4,8},{8,4},{12,0},{1,13},{5,9},{9,5},{13,1},{2,14},{6,10},... | collective-permute-start | bytes 393224 | tf_op jit(solution)/shard_map/ppermute | solution.py:500
  59.1 8.7 %collective-permute-start.8 = (f32[256,128]{1,0:T(8,128)S(1)}, f32[256,128]{1,0:T(8,128)S(1)}, u32[]{:S(2)}, u32[]{:S(2)}) collective-permute-start(f32[256,128]{1,0:T(8,128)S(1)} %get-tuple-element.41), channel_id=1, source_target_pairs={{0,4},{4,0},{8,12},{12,8},{1,5},{5,1},{9,13},{13,9},{2,6},{6,2},{1... | collective-permute-start | bytes 393224 | tf_op jit(solution)/shard_map/ppermute | solution.py:500
  59.6 8.2 %collective-permute-start.11 = (f32[256,128]{1,0:T(8,128)S(1)}, f32[256,128]{1,0:T(8,128)S(1)}, u32[]{:S(2)}, u32[]{:S(2)}) collective-permute-start(f32[256,128]{1,0:T(8,128)S(1)} %get-tuple-element.40.rest_0_), channel_id=1, source_target_pairs={{0,1},{1,0},{2,3},{3,2},{4,5},{5,4},{6,7},{7,6},{8,9},{9,8},{10,11... | collective-permute-start | bytes 393224 | tf_op jit(solution)/shard_map/ppermute | solution.py:501
  65.6 2.3 %collective-permute-start.13 = (f32[256,128]{1,0:T(8,128)S(1)}, f32[256,128]{1,0:T(8,128)S(1)}, u32[]{:S(2)}, u32[]{:S(2)}) collective-permute-start(f32[256,128]{1,0:T(8,128)S(1)} %collective-permute-done.9.rest_2_), channel_id=1, source_target_pairs={{0,1},{1,0},{2,3},{3,2},{4,5},{5,4},{6,7},{7,6},{8,9},{9,8},{10,11... | collective-permute-start | bytes 393224 | tf_op jit(solution)/shard_map/ppermute | solution.py:501
  65.6 2.3 %collective-permute-start.14 = (f32[256,128]{1,0:T(8,128)S(1)}, f32[256,128]{1,0:T(8,128)S(1)}, u32[]{:S(2)}, u32[]{:S(2)}) collective-permute-start(f32[256,128]{1,0:T(8,128)S(1)} %collective-permute-done.10.rest_3_), channel_id=1, source_target_pairs={{0,1},{1,0},{2,3},{3,2},{4,5},{5,4},{6,7},{7,6},{8,9},{9,8},{10,11... | collective-permute-start | bytes 393224 | tf_op jit(solution)/shard_map/ppermute | solution.py:501
  67.8 1.3 %collective-permute-start.12 = (f32[256,128]{1,0:T(8,128)S(1)}, f32[256,128]{1,0:T(8,128)S(1)}, u32[]{:S(2)}, u32[]{:S(2)}) collective-permute-start(f32[256,128]{1,0:T(8,128)S(1)} %collective-permute-done.8.rest_1_), channel_id=1, source_target_pairs={{0,1},{1,0},{2,3},{3,2},{4,5},{5,4},{6,7},{7,6},{8,9},{9,8},{10,11... | collective-permute-start | bytes 393224 | tf_op jit(solution)/shard_map/ppermute | solution.py:501

commit v3 on v2

--- a/solution.py
+++ b/solution.py
@@ -117,17 +117,19 @@
     return row, core, members, device % members, device // members
 
 
-def window_kernel(mirrored, place_ref, spec_ref, table_ref, out_ref):
-    ratio, win, width = table_ref.shape
+def window_block(mirrored, spec, table, out_ref):
+    rows, total = out_ref.shape
+    ratio = table(None)
+    width = total // ratio
     lanes = width // 2
-    rows = out_ref.shape[0]
+    win = ratio * lanes
     pieces = []
     for step in range(ratio):
         at = slice(step * win, (step + 1) * win)
-        pieces += [spec_ref[0, part, :, at] for part in range(2)]
+        pieces += [spec(part, at) for part in range(2)]
     stacked = jnp.concatenate(pieces, 0)
     got = [
-        jnp.dot(stacked, table_ref[which], preferred_element_type=jnp.float32)
+        jnp.dot(stacked, table(which), preferred_element_type=jnp.float32)
         for which in range(ratio)
     ]
     for part in range(ratio):
@@ -145,75 +147,160 @@
         out_ref[:, start + lanes : start + width] = out_im.astype(out_ref.dtype)
 
 
-def windowed(spectra, table, place, rows, dtype, mirrored):
-    ratio, win, width = table.shape
-    length = ratio * win
+def first_kernel(spec_ref, tables_ref, out_ref, held_ref, table_ref, sem):
+    rows = out_ref.shape[0]
+    _, core, _, _, side = place()
+    start = pl.multiple_of((2 * core + 1) * rows, rows)
+    copies = [
+        pltpu.make_async_copy(
+            spec_ref.at[1 - side, :, pl.ds(start, rows)], held_ref, sem.at[0]
+        ),
+        pltpu.make_async_copy(tables_ref.at[0], table_ref, sem.at[1]),
+    ]
+    for copy in copies:
+        copy.start()
+    for copy in copies:
+        copy.wait()
+    window_block(
+        True,
+        lambda part, at: held_ref[part, :, at],
+        lambda k: table_ref.shape[0] if k is None else table_ref[k],
+        out_ref,
+    )
+
+
+def window_first(spectra, tables, rows):
+    _, ratio, win, width = tables.shape
     return pl.pallas_call(
-        functools.partial(window_kernel, mirrored),
-        out_shape=jax.ShapeDtypeStruct((rows, ratio * width), dtype),
+        first_kernel,
+        out_shape=jax.ShapeDtypeStruct((rows, ratio * width), jnp.bfloat16),
+        in_specs=hbm(2),
+        out_specs=vmem(1)[0],
+        scratch_shapes=[
+            pltpu.VMEM((2, rows, ratio * win), jnp.bfloat16),
+            pltpu.VMEM((ratio, win, width), jnp.bfloat16),
+            pltpu.SemaphoreType.DMA((2,)),
+        ],
+        compiler_params=params(WINDOW_MB),
+        cost_estimate=pl.CostEstimate(
+            flops=4 * rows * ratio * win * ratio * width,
+            bytes_accessed=8 * rows * ratio * win,
+            transcendentals=0,
+        ),
+        name="window_first",
+    )(spectra, tables)
+
+
+def rest_kernel(place_ref, spec_ref, table_ref, main_ref, more_ref, *outs):
+    sent_ref, keep_ref, low_ref, high_ref = outs
+    step = pl.program_id(0)
+    spec = lambda part, at: spec_ref[0, part, :, at]
+    table = lambda k: table_ref.shape[1] if k is None else table_ref[0, k]
+
+    @pl.when(step == 0)
+    def _():
+        window_block(True, spec, table, sent_ref)
+        low, band = low_ref.shape[1], main_ref.shape[1]
+        low_ref[...] = main_ref[:, :low]
+        high_ref[:, : band - low] = main_ref[:, low:]
+        high_ref[:, band - low :] = more_ref[...]
+
+    @pl.when(step > 0)
+    def _():
+        window_block(False, spec, table, keep_ref)
+
+
+def window_rest(spectra, tables, left, rows):
+    _, ratio, win, width = tables.shape
+    row, core, members, _, side = place()
+    device = row * lax.axis_size("orient") + core
+    band = 2 * rows
+    tsize = left.shape[2]
+    at = jnp.stack([side, core, device]).astype(jnp.int32)
+
+    def spec_index(i, at):
+        first = jnp.where(i == 0, 1, 0)
+        return at[0] + first * (1 - 2 * at[0]), 0, 2 * at[1] + jnp.maximum(i - 1, 0), 0
+
+    return pl.pallas_call(
+        rest_kernel,
+        out_shape=[
+            jax.ShapeDtypeStruct((rows, ratio * width), jnp.bfloat16),
+            jax.ShapeDtypeStruct((band, ratio * width), jnp.float32),
+            jax.ShapeDtypeStruct((2, rows, tsize), jnp.bfloat16),
+            jax.ShapeDtypeStruct((2, rows + PAD, tsize), jnp.bfloat16),
+        ],
         grid_spec=pltpu.PrefetchScalarGridSpec(
             num_scalar_prefetch=1,
-            grid=(1,),
+            grid=(3,),
             in_specs=[
-                pl.BlockSpec((1, 2, rows, length), lambda a, place: (place[0], 0, place[1], 0)),
-                pl.BlockSpec(table.shape, lambda a, place: (0, 0, 0)),
+                pl.BlockSpec((1, 2, rows, ratio * win), spec_index),
+                pl.BlockSpec((1, ratio, win, width), lambda i, at: (jnp.minimum(i, 1), 0, 0, 0)),
+                pl.BlockSpec((2, band, tsize), lambda i, at: (0, at[2], 0)),
+                pl.BlockSpec((2, PAD, tsize), lambda i, at: (0, (at[2] + 1) * (band // PAD), 0)),
             ],
-            out_specs=pl.BlockSpec((rows, ratio * width), lambda a, place: (0, 0)),
+            out_specs=[
+                pl.BlockSpec((rows, ratio * width), lambda i, at: (0, 0)),
+                pl.BlockSpec((rows, ratio * width), lambda i, at: (jnp.maximum(i - 1, 0), 0)),
+                pl.BlockSpec((2, rows, tsize), lambda i, at: (0, 0, 0)),
+                pl.BlockSpec((2, rows + PAD, tsize), lambda i, at: (0, 0, 0)),
+            ],
         ),
         compiler_params=params(WINDOW_MB),
         cost_estimate=pl.CostEstimate(
-            flops=4 * rows * length * ratio * width,
-            bytes_accessed=2 * (2 * rows * length + length * width),
+            flops=12 * rows * ratio * win * ratio * width,
+            bytes_accessed=20 * rows * ratio * win,
             transcendentals=0,
         ),
-        name="windowed",
-    )(place, spectra, table)
-
-
-def template_kernel(index_ref, bank_ref, left_ref, right_ref, low_ref, high_ref, hold_low, hold_high):
+        name="window_rest",
+    )(at, spectra, tables, left, left)
+
+
+def template_kernel(fresh, index_ref, bank_ref, left_ref, right_ref, out_ref, *rest):
+    hold_ref = rest[-1]
     ratio, depth, width = right_ref.shape
-    window, low = hold_low.shape[0], hold_low.shape[1]
-    rows = left_ref.shape[1]
+    window, rows = hold_ref.shape[0], hold_ref.shape[1]
     left = jnp.concatenate([left_ref[0], left_ref[1]], 0)
     for o in range(window):
-        values = bank_ref[index_ref[o]].astype(jnp.float32)
-        centred = values - jnp.mean(values)
-        factor = lax.rsqrt(jnp.mean(centred * centred) + 1e-06)
-        template = (centred * factor).astype(jnp.bfloat16)
+        if fresh:
+            values = bank_ref[index_ref[o]].astype(jnp.float32)
+            share = 1.0 / values.size
+            total = jnp.sum(jnp.sum(values, 0, keepdims=True), 1, keepdims=True)
+            centred = values - total * share
+            square = jnp.sum(jnp.sum(centred * centred, 0, keepdims=True), 1, keepdims=True)
+            factor = lax.rsqrt(square * share + 1e-06)
+            template = (centred * factor).astype(jnp.bfloat16)
+            rest[0][o] = template
+        else:
+            template = bank_ref[o]
         rowpass = jnp.dot(left, template, preferred_element_type=jnp.float32).astype(jnp.bfloat16)
-        both = jnp.concatenate([rowpass[:rows], rowpass[rows:]], 1)
-        hold_low[o] = both[:low]
-        hold_high[o] = both[low:]
-    for hold, out in ((hold_low, low_ref), (hold_high, high_ref)):
-        flat = hold[...].reshape(window * hold.shape[1], depth)
-        for part in range(ratio):
-            got = jnp.dot(flat, right_ref[part], preferred_element_type=jnp.float32)
-            out[part] = got.astype(out.dtype)
-
-
-def template_spectra(bank, orient_index, left, band, win, lanes, dtype):
+        hold_ref[o] = jnp.concatenate([rowpass[:rows], rowpass[rows:]], 1)
+    flat = hold_ref[...].reshape(window * rows, depth)
+    for part in range(ratio):
+        got = jnp.dot(flat, right_ref[part], preferred_element_type=jnp.float32)
+        out_ref[part] = got.astype(out_ref.dtype)
+
+
+def template_spectra(bank, orient_index, left, win, lanes, dtype, fresh):
     tsize = bank.shape[1]
     window = orient_index.shape[0]
     ratio = win // lanes
+    rows = left.shape[1]
     right = template_table(tsize, win, lanes).reshape(2 * tsize, ratio, 2 * lanes)
     right = jnp.asarray(np.ascontiguousarray(right.transpose(1, 0, 2)))
-    low, high = band // 2, band // 2 + PAD
+    out_shape = [jax.ShapeDtypeStruct((ratio, window * rows, 2 * lanes), dtype)]
+    if fresh:
+        out_shape.append(jax.ShapeDtypeStruct((window, tsize, tsize), jnp.bfloat16))
     return pl.pallas_call(
-        template_kernel,
-        out_shape=[
-            jax.ShapeDtypeStruct((ratio, window * low, 2 * lanes), dtype),
-            jax.ShapeDtypeStruct((ratio, window * high, 2 * lanes), dtype),
-        ],
+        functools.partial(template_kernel, fresh),
+        out_shape=out_shape,
         in_specs=[SMEM] + vmem(3),
-        out_specs=vmem(2),
-        scratch_shapes=[
-            pltpu.VMEM((window, low, 2 * tsize), jnp.bfloat16),
-            pltpu.VMEM((window, high, 2 * tsize), jnp.bfloat16),
-        ],
+        out_specs=vmem(len(out_shape)),
+        scratch_shapes=[pltpu.VMEM((window, rows, 2 * tsize), jnp.bfloat16)],
         compiler_params=params(TEMPLATE_MB),
         cost_estimate=pl.CostEstimate(
-            flops=2 * window * (band + PAD) * tsize * (2 * tsize + 4 * win),
-            bytes_accessed=2 * (bank.size + window * (band + PAD) * 2 * win),
+            flops=2 * window * rows * tsize * (2 * tsize + 4 * win),
+            bytes_accessed=2 * bank.size + 4 * window * rows * 2 * win,
             transcendentals=0,
         ),
         name="templates",
@@ -441,35 +528,33 @@
     window = orient_index.shape[0]
     rows = band // 2
 
-    row, core, _, _, side = place()
-    device = row * cores + core
-    mirror_table = jnp.asarray(window_table(length, win, True))
-    table = jnp.asarray(window_table(length, win, False))
+    row = lax.axis_index("row")
+    window_tables = jnp.asarray(
+        np.stack([window_table(length, win, True), window_table(length, win, False)])
+    )
     back = jnp.asarray(back_table(win, lanes))
     flip = flip_table(band)
 
     opposite = [(i, count - 1 - i) for i in range(count)]
-    others = []
-    for block in (1, 0):
-        at = jnp.stack([1 - side, 2 * core + block]).astype(jnp.int32)
-        sent = windowed(spectra, mirror_table, at, rows, jnp.bfloat16, True)
-        others.insert(0, lax.ppermute(sent, line, opposite))
     cos, sin = phases(np.arange(length + PAD), np.arange(tsize), length)
     left = jnp.asarray(np.stack([cos, -sin]).astype(BF16))
-    left = lax.dynamic_slice_in_dim(left, device * band, band + PAD, 1)
-    spectra, bank, left, _ = lax.optimization_barrier((spectra, bank, left, sent))
-    at = jnp.stack([side, core]).astype(jnp.int32)
-    keep = windowed(spectra, table, at, band, jnp.float32, False)
-    bank, left, keep = lax.optimization_barrier((bank, left, keep))
-    tspec = template_spectra(bank, orient_index, left, band, win, lanes, jnp.float32)
+    sent = window_first(spectra, window_tables, rows)
+    others = [lax.ppermute(sent, line, opposite)]
+    spectra, bank, _ = lax.optimization_barrier((spectra, bank, sent))
+    sent, keep, *left = window_rest(spectra, window_tables, left, rows)
+    others.insert(0, lax.ppermute(sent, line, opposite))
+    bank, keep, *left = lax.optimization_barrier((bank, keep, *left))
     lows, highs = [], []
     for block, got in ((0, lows), (1, highs)):
+        tspec, *fresh = template_spectra(
+            bank, orient_index, left[block], win, lanes, jnp.float32, block == 0
+        )
         parts = partials(
             keep,
             others[1 - block :],
             block * rows,
             jnp.asarray(flip[:rows, rows:] if block == 0 else flip[rows:]),
-            tspec[block],
+            tspec,
             back,
             members,
             window,
@@ -477,6 +562,11 @@
         got.append(parts[0])
         for s in range(1, members):
             got.append(lax.ppermute(parts[s], line, [(i, i ^ s) for i in range(count)]))
+        if block == 0:
+            bank, left[1], _ = lax.optimization_barrier((fresh[0], left[1], parts[0]))
+            early = lows[1 : members // 2 + 1]
+            others[0], *early = lax.optimization_barrier((others[0], *early))
+            lows[1 : members // 2 + 1] = early
 
     all_tables = jnp.asarray(column_table(length, classes, cores, band))
     row, _ = lax.optimization_barrier((row, parts[0]))

time: 70.7 us -> 66.8 us (0.945)
  Pallas kernels: 33.6 us -> 30.5 us
  waiting for transfers between devices: 16.5 us -> 15.3 us
  starting transfers between devices: 14.5 us -> 15.6 us
    ppermute x0 -> x1, starting transfers between devices: none -> 4.55 us  [shards(): others = [lax.ppermute(sent, line, opposite)]]
    ppermute x2 -> x1, starting transfers between devices: 4.49 us -> 0.1 us  [shards(): others.insert(0, lax.ppermute(sent, line, opposite))]
    pallas_call x4, Pallas kernels: 22.6 us -> 19.4 us  [the longest x2 8.07 us: template_spectra(): pl.pallas_call(functools.partial(template_kernel, fresh), out_shape=out_s...]
    ppermute x6, waiting for transfers between devices: 7.51 us -> 5.17 us  [shards(): got.append(lax.ppermute(parts[s], line, [(i, i ^ s) for i in range(count)]))]
    ppermute x6, starting transfers between devices: 4.3 us -> 6.08 us  [shards(): got.append(lax.ppermute(parts[s], line, [(i, i ^ s) for i in range(count)]))]
    ppermute x3, waiting for transfers between devices: 7.68 us -> 8.76 us  [shards(): lax.ppermute(maps[s], 'row', [(i, i ^ s) for i in range(classes)])]
    dynamic_slice x1 -> x0, local copies, waits for them, and re-layouts: 1.05 us -> none  [shards(): left = lax.dynamic_slice_in_dim(left, device * band, band + PAD, 1)]
    unnamed x16 -> x20, local copies, waits for them, and re-layouts: 0.05 us -> 1.08 us
  transfers between devices with their start and end apart: 15 -> 15, of which waited for: 7 -> 6; matrix products, arithmetic and copies ran while one was open for 6% -> 5% of each run, Pallas kernels for 37% -> 35%
where the time goes in v3:
time: 66.8 us; the launch traced here: 66.6 us
  Pallas kernels  30.5 us (46%)
  starting transfers between devices  15.6 us (23%)
  waiting for transfers between devices  15.3 us (23%)
  local copies, waits for them, and re-layouts  3.71 us (6%)
  between operations  0.99 us (1%)
    ppermute x3, waiting for transfers between devices, shards(): lax.ppermute(maps[s], 'row', [(i, i ^ s) for i in range(classes)])  8.76 us
    pallas_call x2, Pallas kernels, template_spectra(): pl.pallas_call(functools.partial(template_kernel, fresh), out_shape=out_s...  8.07 us
    pallas_call x1, Pallas kernels, window_rest(): pl.pallas_call(rest_kernel, out_shape=[jax.ShapeDtypeStruct((rows, ratio...  7.78 us
    ppermute x6, starting transfers between devices, shards(): got.append(lax.ppermute(parts[s], line, [(i, i ^ s) for i in range(count)]))  6.08 us
    ppermute x6, waiting for transfers between devices, shards(): got.append(lax.ppermute(parts[s], line, [(i, i ^ s) for i in range(count)]))  5.17 us
    pallas_call x2, Pallas kernels, columns(): pl.pallas_call(functools.partial(column_kernel, group_of, scale, share),...  4.96 us
    pallas_call x2, Pallas kernels, partials(): pl.pallas_call(functools.partial(partial_kernel, len(others), first), out...  4.89 us
    ppermute x1, starting transfers between devices, shards(): others = [lax.ppermute(sent, line, opposite)]  4.55 us
  transfers between devices with their start and end apart: 15, of which 6 were waited for; matrix products, arithmetic and copies ran while one was open for 5% of the time, Pallas kernels for 35%

profile of v3, /device:TPU:0, one launch (start us, length us, event | category | flops | bytes accessed | tf_op | source)
XLA Modules:
  0.0 66.6 jit_solution(689841157821172003)
XLA Ops:
  0.6 3.5 %window_first.1 = bf16[128,1024]{1,0:T(8,128)(2,1)} custom-call(bf16[2,2,512,2048]{3,2,1,0:T(8,128)(2,1)} %spec_ref.2, bf16[2,4,512,256]{3,2,1,0:T(8,128)(2,1)} %constant.150.clone.tables_ref.table_ref), custom_call_target="tpu_custom_call" | custom-call | flops 1073741824 | bytes 2097152 | tf_op jit(solution)/shard_map/window_first/pallas_call | solution.py:174
  4.2 4.6 %collective-permute-start = (bf16[128,1024]{1,0:T(8,128)(2,1)}, bf16[128,1024]{1,0:T(8,128)(2,1)S(1)}, u32[]{:S(2)}, u32[]{:S(2)}) collective-permute-start(bf16[128,1024]{1,0:T(8,128)(2,1)} %window_first.1), channel_id=1, source_target_pairs={{0,13},{1,12},{4,9},{5,8},{8,5},{9,4},{12,1},{13,0},{2,15},{3,14},... | collective-permute-start | bytes 786440 | tf_op jit(solution)/shard_map/ppermute | solution.py:542
  8.7 0.6 pad_add_fusion.place_ref
  9.3 7.8 %window_rest.1 = (bf16[128,1024]{1,0:T(8,128)(2,1)}, f32[256,1024]{1,0:T(8,128)}, bf16[2,128,384]{2,1,0:T(8,128)(2,1)}, bf16[2,144,384]{2,1,0:T(8,128)(2,1)}) custom-call(s32[3]{0:T(128)} %pad_add_fusion.place_ref, bf16[2,2,512,2048]{3,2,1,0:T(8,128)(2,1)} %spec_ref.2, bf16[2,4,512,256]{3,2,1,0:T(8,128)(2,1)} %constant.150.clone.tables_ref.table_ref, ...), custom_call_target="tpu_custom_call" | custom-call | flops 3221225472 | bytes 5242880 | tf_op jit(solution)/shard_map/window_rest/pallas_call | solution.py:225
  17.1 0.0 copy-start.3
  17.2 0.1 collective-permute-start.1
  17.3 1.0 %copy-done.7 = bf16[2,128,384]{2,1,0:T(8,128)(2,1)S(1)} copy-done((bf16[2,128,384]{2,1,0:T(8,128)(2,1)S(1)}, bf16[2,128,384]{2,1,0:T(8,128)(2,1)}, u32[]{:S(2)}) %copy-start.7) | copy-done | bytes 196632
  18.3 4.4 %templates.2 = (f32[4,1024,256]{2,1,0:T(8,128)S(1)}, bf16[8,384,384]{2,1,0:T(8,128)(2,1)S(1)}) custom-call(s32[8]{0:T(128)S(1)} %copy-done.8, bf16[8,384,384]{2,1,0:T(8,128)(2,1)S(1)} %copy-done.5, bf16[2,128,384]{2,1,0:T(8,128)(2,1)S(1)} %copy-done.7, bf16[4,768,256]{2,1,0:T(8,128)(2,1)S(1)} %copy-done.9), custom_call_target="tpu_custom_call" | custom-call | flops 2214592512 | bytes 6553600 | tf_op jit(solution)/shard_map/templates/pallas_call | solution.py:294
  22.8 2.3 %partials.2 = (bf16[128,512]{1,0:T(8,128)(2,1)S(1)}, bf16[128,512]{1,0:T(8,128)(2,1)S(1)}, bf16[128,512]{1,0:T(8,128)(2,1)S(1)}, bf16[128,512]{1,0:T(8,128)(2,1)S(1)}) custom-call(f32[256,1024]{1,0:T(8,128)S(1)} %copy-done.1, bf16[128,128]{1,0:T(8,128)(2,1)S(1)} %copy-done.3, f32[4,1024,256]{2,1,0:T(8,128)S(1)} %get-tuple-element.42.tspec_ref, ...), custom_call_target="tpu_custom_call" | custom-call | flops 1610612736 | bytes 2097152 | tf_op jit(solution)/shard_map/partials/pallas_call | solution.py:371
  25.1 0.7 %collective-permute-start.2 = (bf16[128,512]{1,0:T(8,128)(2,1)S(1)}, bf16[128,512]{1,0:T(8,128)(2,1)S(1)}, u32[]{:S(2)}, u32[]{:S(2)}) collective-permute-start(bf16[128,512]{1,0:T(8,128)(2,1)S(1)} %get-tuple-element.47), channel_id=1, source_target_pairs={{0,1},{1,0},{4,5},{5,4},{8,9},{9,8},{12,13},{13,12},{2,3},{3,2},{6... | collective-permute-start | bytes 393224 | tf_op jit(solution)/shard_map/ppermute | solution.py:564
  25.9 3.1 %collective-permute-start.3 = (bf16[128,512]{1,0:T(8,128)(2,1)S(1)}, bf16[128,512]{1,0:T(8,128)(2,1)S(1)}, u32[]{:S(2)}, u32[]{:S(2)}) collective-permute-start(bf16[128,512]{1,0:T(8,128)(2,1)S(1)} %get-tuple-element.48), channel_id=1, source_target_pairs={{0,4},{1,5},{4,0},{5,1},{8,12},{9,13},{12,8},{13,9},{2,6},{3,7},{6... | collective-permute-start | bytes 393224 | tf_op jit(solution)/shard_map/ppermute | solution.py:564
  29.0 0.1 collective-permute-start.4
  29.1 3.6 %templates.3.tspec_ref = f32[4,1152,256]{2,1,0:T(8,128)S(1)} custom-call(s32[8]{0:T(128)S(1)} %copy-done.8, bf16[8,384,384]{2,1,0:T(8,128)(2,1)S(1)} %get-tuple-element.44.bank_ref, bf16[2,144,384]{2,1,0:T(8,128)(2,1)S(1)} %copy-done.6, bf16[4,768,256]{2,1,0:T(8,128)(2,1)S(1)} %copy-done.9), custom_call_target="tpu_custom_call" | custom-call | flops 2491416576 | bytes 7077888 | tf_op jit(solution)/shard_map/templates/pallas_call | solution.py:294
  32.7 0.6 collective-permute-done.3.rest_4_
  33.3 2.6 %partials.3 = (bf16[144,512]{1,0:T(8,128)(2,1)S(1)}, bf16[144,512]{1,0:T(8,128)(2,1)S(1)}, bf16[144,512]{1,0:T(8,128)(2,1)S(1)}, bf16[144,512]{1,0:T(8,128)(2,1)S(1)}) custom-call(f32[256,1024]{1,0:T(8,128)S(1)} %copy-done.1, bf16[144,256]{1,0:T(8,128)(2,1)S(1)} %copy-done.2, f32[4,1152,256]{2,1,0:T(8,128)S(1)} %templates.3.tspec_ref, ...), custom_call_target="tpu_custom_call" | custom-call | flops 1811939328 | bytes 2359296 | tf_op jit(solution)/shard_map/partials/pallas_call | solution.py:371
  36.1 0.1 collective-permute-start.5
  36.2 2.0 %collective-permute-start.6 = (bf16[144,512]{1,0:T(8,128)(2,1)S(1)}, bf16[144,512]{1,0:T(8,128)(2,1)S(1)}, u32[]{:S(2)}, u32[]{:S(2)}) collective-permute-start(bf16[144,512]{1,0:T(8,128)(2,1)S(1)} %get-tuple-element.56), channel_id=1, source_target_pairs={{0,4},{1,5},{4,0},{5,1},{8,12},{9,13},{12,8},{13,9},{2,6},{3,7},{6... | collective-permute-start | bytes 442376 | tf_op jit(solution)/shard_map/ppermute | solution.py:564
  38.2 0.1 collective-permute-start.7
  38.3 2.6 %dynamic-slice_bitcast_fusion = (bf16[512,1024]{1,0:T(8,128)(2,1)S(1)}, bf16[512,1024]{1,0:T(8,128)(2,1)S(1)}, bf16[512,1024]{1,0:T(8,128)(2,1)S(1)}, bf16[512,1024]{1,0:T(8,128)(2,1)S(1)}) fusion(bf16[4,512,1024]{2,1,0:T(8,128)(2,1)} %constant.156.clone, s32[]{:T(128)S(6)} %select_n.84, s32[]{:T(128)S(6)} %select_n.76, s32[]{:T(128)S(6)} %select_n.72, ...), kind=kLoop, calls=%fused_computation | loop fusion | bytes 8388624 | tf_op jit(solution)/shard_map/jit(dynamic_index_in_dim)/squeeze | solution.py:578
  40.9 2.0 %collective-permute-done.6.rest_8_ = bf16[144,512]{1,0:T(8,128)(2,1)S(1)} collective-permute-done((bf16[144,512]{1,0:T(8,128)(2,1)S(1)}, bf16[144,512]{1,0:T(8,128)(2,1)S(1)}, u32[]{:S(2)}, u32[]{:S(2)}) %collective-permute-start.6) | collective-permute-done | bytes 147488 | tf_op jit(solution)/shard_map/ppermute | solution.py:564
  43.0 2.5 %collective-permute-done.7.rest_9_ = bf16[144,512]{1,0:T(8,128)(2,1)S(1)} collective-permute-done((bf16[144,512]{1,0:T(8,128)(2,1)S(1)}, bf16[144,512]{1,0:T(8,128)(2,1)S(1)}, u32[]{:S(2)}, u32[]{:S(2)}) %collective-permute-start.7) | collective-permute-done | bytes 147488 | tf_op jit(solution)/shard_map/ppermute | solution.py:564
  45.5 2.6 %columns.3 = (f32[256,128]{1,0:T(8,128)S(1)}, f32[256,128]{1,0:T(8,128)S(1)}) custom-call(f32[2,4]{1,0:T(2,128)S(1)} %copy-done.4, bf16[512,1024]{1,0:T(8,128)(2,1)S(1)} %get-tuple-element.65.rest_0_, bf16[512,1024]{1,0:T(8,128)(2,1)S(1)} %get-tuple-element.62.rest_1_, bf16[128,512]{1,0:T(8,128)(2,1)S(1)} %get-tuple-element.43.rest_2_, ...), custom_call_target="tpu_custom_call" | custom-call | flops 536870912 | bytes 2097152 | tf_op jit(solution)/shard_map/columns/pallas_call | solution.py:459
  48.1 3.6 %collective-permute-start.9 = (f32[256,128]{1,0:T(8,128)S(1)}, f32[256,128]{1,0:T(8,128)S(1)}, u32[]{:S(2)}, u32[]{:S(2)}) collective-permute-start(f32[256,128]{1,0:T(8,128)S(1)} %get-tuple-element.60), channel_id=1, source_target_pairs={{0,8},{4,12},{8,0},{12,4},{1,9},{5,13},{9,1},{13,5},{2,10},{6,14},... | collective-permute-start | bytes 393224 | tf_op jit(solution)/shard_map/ppermute | solution.py:590
  51.7 0.5 collective-permute-start.10
  52.1 2.4 %columns.2 = (f32[256,128]{1,0:T(8,128)S(1)}, f32[256,128]{1,0:T(8,128)S(1)}) custom-call(f32[2,4]{1,0:T(2,128)S(1)} %copy-done.4, bf16[512,1024]{1,0:T(8,128)(2,1)S(1)} %get-tuple-element.64.rest_0_, bf16[512,1024]{1,0:T(8,128)(2,1)S(1)} %get-tuple-element.63.rest_1_, bf16[128,512]{1,0:T(8,128)(2,1)S(1)} %get-tuple-element.43.rest_2_, ...), custom_call_target="tpu_custom_call" | custom-call | flops 536870912 | bytes 2097152 | tf_op jit(solution)/shard_map/columns/pallas_call | solution.py:459
  54.5 0.2 collective-permute-start.8
  54.7 6.8 %collective-permute-done.9.rest_2_ = f32[256,128]{1,0:T(8,128)S(1)} collective-permute-done((f32[256,128]{1,0:T(8,128)S(1)}, f32[256,128]{1,0:T(8,128)S(1)}, u32[]{:S(2)}, u32[]{:S(2)}) %collective-permute-start.9) | collective-permute-done | bytes 131104 | tf_op jit(solution)/shard_map/ppermute | solution.py:590
  61.5 0.5 collective-permute-start.14
  62.1 2.0 %collective-permute-done.8.rest_1_ = f32[256,128]{1,0:T(8,128)S(1)} collective-permute-done((f32[256,128]{1,0:T(8,128)S(1)}, f32[256,128]{1,0:T(8,128)S(1)}, u32[]{:S(2)}, u32[]{:S(2)}) %collective-permute-start.8) | collective-permute-done | bytes 131104 | tf_op jit(solution)/shard_map/ppermute | solution.py:590
  64.0 0.0 collective-permute-start.12
  64.1 1.3 %collective-permute-done.12.rest_5_ = f32[256,128]{1,0:T(8,128)S(1)} collective-permute-done((f32[256,128]{1,0:T(8,128)S(1)}, f32[256,128]{1,0:T(8,128)S(1)}, u32[]{:S(2)}, u32[]{:S(2)}) %collective-permute-start.12) | collective-permute-done | bytes 131104 | tf_op jit(solution)/shard_map/ppermute | solution.py:591
  65.4 1.3 %unpack.1 = (f32[2,1,512,128]{3,2,1,0:T(8,128)}, f32[2,1,512,128]{3,2,1,0:T(8,128)}) custom-call(f32[256,128]{1,0:T(8,128)S(1)} %get-tuple-element.58.rest_0_, f32[256,128]{1,0:T(8,128)S(1)} %collective-permute-done.8.rest_1_, f32[256,128]{1,0:T(8,128)S(1)} %collective-permute-done.9.rest_2_, f32[256,128]{1,0:T(8,128)S(1)} %collective-permute-done.10.rest_3_, ...), custom_call_target="tpu_custom_call" | custom-call | tf_op jit(solution)/shard_map/unpack/pallas_call | solution.py:506
  (29 shorter events, 0.1 us)
Async XLA Ops:
  4.2 18.6 %collective-permute-start = (bf16[128,1024]{1,0:T(8,128)(2,1)}, bf16[128,1024]{1,0:T(8,128)(2,1)S(1)}, u32[]{:S(2)}, u32[]{:S(2)}) collective-permute-start(bf16[128,1024]{1,0:T(8,128)(2,1)} %window_first.1), channel_id=1, source_target_pairs={{0,13},{1,12},{4,9},{5,8},{8,5},{9,4},{12,1},{13,0},{2,15},{3,14},... | collective-permute-start | bytes 786440 | tf_op jit(solution)/shard_map/ppermute | solution.py:542
  9.3 7.9 %copy-start.5 = (bf16[8,384,384]{2,1,0:T(8,128)(2,1)S(1)}, bf16[8,384,384]{2,1,0:T(8,128)(2,1)}, u32[]{:S(2)}) copy-start(bf16[8,384,384]{2,1,0:T(8,128)(2,1)} %bank_ref) | copy-start | bytes 7077892
  9.3 7.9 %copy-start.8 = (s32[8]{0:T(128)S(1)}, s32[8]{0:T(128)}, u32[]{:S(2)}) copy-start(s32[8]{0:T(128)} %index_ref.3) | copy-start | bytes 100
  9.3 7.9 %copy-start.9 = (bf16[4,768,256]{2,1,0:T(8,128)(2,1)S(1)}, bf16[4,768,256]{2,1,0:T(8,128)(2,1)}, u32[]{:S(2)}) copy-start(bf16[4,768,256]{2,1,0:T(8,128)(2,1)} %constant.153.clone.right_ref) | copy-start | bytes 4718596
  17.1 5.7 %copy-start = (bf16[2,4,256,256]{3,2,1,0:T(8,128)(2,1)S(1)}, bf16[2,4,256,256]{3,2,1,0:T(8,128)(2,1)}, u32[]{:S(2)}) copy-start(bf16[2,4,256,256]{3,2,1,0:T(8,128)(2,1)} %constant.151.clone.back_ref) | copy-start | bytes 3145732
  17.1 5.7 %copy-start.1 = (f32[256,1024]{1,0:T(8,128)S(1)}, f32[256,1024]{1,0:T(8,128)}, u32[]{:S(2)}) copy-start(f32[256,1024]{1,0:T(8,128)} %get-tuple-element.37.keep_ref) | copy-start | bytes 3145732
  17.1 5.7 %copy-start.3 = (bf16[128,128]{1,0:T(8,128)(2,1)S(1)}, bf16[128,128]{1,0:T(8,128)(2,1)}, u32[]{:S(2)}) copy-start(bf16[128,128]{1,0:T(8,128)(2,1)} %constant.154.clone.flip_ref) | copy-start | bytes 98308
  17.2 15.5 %collective-permute-start.1 = (bf16[128,1024]{1,0:T(8,128)(2,1)}, bf16[128,1024]{1,0:T(8,128)(2,1)S(1)}, u32[]{:S(2)}, u32[]{:S(2)}) collective-permute-start(bf16[128,1024]{1,0:T(8,128)(2,1)} %get-tuple-element.46), channel_id=1, source_target_pairs={{0,13},{1,12},{4,9},{5,8},{8,5},{9,4},{12,1},{13,0},{2,15},{3,14},... | collective-permute-start | bytes 786440 | tf_op jit(solution)/shard_map/ppermute | solution.py:545
  17.3 1.1 %copy-start.7 = (bf16[2,128,384]{2,1,0:T(8,128)(2,1)S(1)}, bf16[2,128,384]{2,1,0:T(8,128)(2,1)}, u32[]{:S(2)}) copy-start(bf16[2,128,384]{2,1,0:T(8,128)(2,1)} %get-tuple-element.39.left_ref) | copy-start | bytes 589828
  22.8 6.3 %copy-start.6 = (bf16[2,144,384]{2,1,0:T(8,128)(2,1)S(1)}, bf16[2,144,384]{2,1,0:T(8,128)(2,1)}, u32[]{:S(2)}) copy-start(bf16[2,144,384]{2,1,0:T(8,128)(2,1)} %get-tuple-element.45.left_ref) | copy-start | bytes 663556
  25.1 7.6 %collective-permute-start.2 = (bf16[128,512]{1,0:T(8,128)(2,1)S(1)}, bf16[128,512]{1,0:T(8,128)(2,1)S(1)}, u32[]{:S(2)}, u32[]{:S(2)}) collective-permute-start(bf16[128,512]{1,0:T(8,128)(2,1)S(1)} %get-tuple-element.47), channel_id=1, source_target_pairs={{0,1},{1,0},{4,5},{5,4},{8,9},{9,8},{12,13},{13,12},{2,3},{3,2},{6... | collective-permute-start | bytes 393224 | tf_op jit(solution)/shard_map/ppermute | solution.py:564
  25.9 7.5 %collective-permute-start.3 = (bf16[128,512]{1,0:T(8,128)(2,1)S(1)}, bf16[128,512]{1,0:T(8,128)(2,1)S(1)}, u32[]{:S(2)}, u32[]{:S(2)}) collective-permute-start(bf16[128,512]{1,0:T(8,128)(2,1)S(1)} %get-tuple-element.48), channel_id=1, source_target_pairs={{0,4},{1,5},{4,0},{5,1},{8,12},{9,13},{12,8},{13,9},{2,6},{3,7},{6... | collective-permute-start | bytes 393224 | tf_op jit(solution)/shard_map/ppermute | solution.py:564
  29.0 4.4 %copy-start.2 = (bf16[144,256]{1,0:T(8,128)(2,1)S(1)}, bf16[144,256]{1,0:T(8,128)(2,1)}, u32[]{:S(2)}) copy-start(bf16[144,256]{1,0:T(8,128)(2,1)} %constant.155.clone.flip_ref) | copy-start | bytes 221188
  29.0 11.9 %collective-permute-start.4 = (bf16[128,512]{1,0:T(8,128)(2,1)S(1)}, bf16[128,512]{1,0:T(8,128)(2,1)S(1)}, u32[]{:S(2)}, u32[]{:S(2)}) collective-permute-start(bf16[128,512]{1,0:T(8,128)(2,1)S(1)} %get-tuple-element.54), channel_id=1, source_target_pairs={{0,5},{1,4},{4,1},{5,0},{8,13},{9,12},{12,9},{13,8},{2,7},{3,6},{6... | collective-permute-start | bytes 393224 | tf_op jit(solution)/shard_map/ppermute | solution.py:564
  36.1 4.8 %collective-permute-start.5 = (bf16[144,512]{1,0:T(8,128)(2,1)S(1)}, bf16[144,512]{1,0:T(8,128)(2,1)S(1)}, u32[]{:S(2)}, u32[]{:S(2)}) collective-permute-start(bf16[144,512]{1,0:T(8,128)(2,1)S(1)} %get-tuple-element.55), channel_id=1, source_target_pairs={{0,1},{1,0},{4,5},{5,4},{8,9},{9,8},{12,13},{13,12},{2,3},{3,2},{6... | collective-permute-start | bytes 442376 | tf_op jit(solution)/shard_map/ppermute | solution.py:564
  36.2 6.8 %collective-permute-start.6 = (bf16[144,512]{1,0:T(8,128)(2,1)S(1)}, bf16[144,512]{1,0:T(8,128)(2,1)S(1)}, u32[]{:S(2)}, u32[]{:S(2)}) collective-permute-start(bf16[144,512]{1,0:T(8,128)(2,1)S(1)} %get-tuple-element.56), channel_id=1, source_target_pairs={{0,4},{1,5},{4,0},{5,1},{8,12},{9,13},{12,8},{13,9},{2,6},{3,7},{6... | collective-permute-start | bytes 442376 | tf_op jit(solution)/shard_map/ppermute | solution.py:564
  38.2 7.3 %collective-permute-start.7 = (bf16[144,512]{1,0:T(8,128)(2,1)S(1)}, bf16[144,512]{1,0:T(8,128)(2,1)S(1)}, u32[]{:S(2)}, u32[]{:S(2)}) collective-permute-start(bf16[144,512]{1,0:T(8,128)(2,1)S(1)} %get-tuple-element.57), channel_id=1, source_target_pairs={{0,5},{1,4},{4,1},{5,0},{8,13},{9,12},{12,9},{13,8},{2,7},{3,6},{6... | collective-permute-start | bytes 442376 | tf_op jit(solution)/shard_map/ppermute | solution.py:564
  38.3 7.2 %copy-start.4 = (f32[2,4]{1,0:T(2,128)S(1)}, f32[2,4]{1,0:T(2,128)}, u32[]{:S(2)}) copy-start(f32[2,4]{1,0:T(2,128)} %constant.157.clone.roots_ref) | copy-start | bytes 100
  48.1 13.5 %collective-permute-start.9 = (f32[256,128]{1,0:T(8,128)S(1)}, f32[256,128]{1,0:T(8,128)S(1)}, u32[]{:S(2)}, u32[]{:S(2)}) collective-permute-start(f32[256,128]{1,0:T(8,128)S(1)} %get-tuple-element.60), channel_id=1, source_target_pairs={{0,8},{4,12},{8,0},{12,4},{1,9},{5,13},{9,1},{13,5},{2,10},{6,14},... | collective-permute-start | bytes 393224 | tf_op jit(solution)/shard_map/ppermute | solution.py:590
  51.7 9.9 %collective-permute-start.10 = (f32[256,128]{1,0:T(8,128)S(1)}, f32[256,128]{1,0:T(8,128)S(1)}, u32[]{:S(2)}, u32[]{:S(2)}) collective-permute-start(f32[256,128]{1,0:T(8,128)S(1)} %get-tuple-element.61), channel_id=1, source_target_pairs={{0,12},{4,8},{8,4},{12,0},{1,13},{5,9},{9,5},{13,1},{2,14},{6,10},... | collective-permute-start | bytes 393224 | tf_op jit(solution)/shard_map/ppermute | solution.py:590
  54.5 9.5 %collective-permute-start.8 = (f32[256,128]{1,0:T(8,128)S(1)}, f32[256,128]{1,0:T(8,128)S(1)}, u32[]{:S(2)}, u32[]{:S(2)}) collective-permute-start(f32[256,128]{1,0:T(8,128)S(1)} %get-tuple-element.59), channel_id=1, source_target_pairs={{0,4},{4,0},{8,12},{12,8},{1,5},{5,1},{9,13},{13,9},{2,6},{6,2},{1... | collective-permute-start | bytes 393224 | tf_op jit(solution)/shard_map/ppermute | solution.py:590
  54.7 9.3 %collective-permute-start.11 = (f32[256,128]{1,0:T(8,128)S(1)}, f32[256,128]{1,0:T(8,128)S(1)}, u32[]{:S(2)}, u32[]{:S(2)}) collective-permute-start(f32[256,128]{1,0:T(8,128)S(1)} %get-tuple-element.58.rest_0_), channel_id=1, source_target_pairs={{0,1},{1,0},{2,3},{3,2},{4,5},{5,4},{6,7},{7,6},{8,9},{9,8},{10,11... | collective-permute-start | bytes 393224 | tf_op jit(solution)/shard_map/ppermute | solution.py:591
  61.5 2.5 %collective-permute-start.13 = (f32[256,128]{1,0:T(8,128)S(1)}, f32[256,128]{1,0:T(8,128)S(1)}, u32[]{:S(2)}, u32[]{:S(2)}) collective-permute-start(f32[256,128]{1,0:T(8,128)S(1)} %collective-permute-done.9.rest_2_), channel_id=1, source_target_pairs={{0,1},{1,0},{2,3},{3,2},{4,5},{5,4},{6,7},{7,6},{8,9},{9,8},{10,11... | collective-permute-start | bytes 393224 | tf_op jit(solution)/shard_map/ppermute | solution.py:591
  61.5 2.5 %collective-permute-start.14 = (f32[256,128]{1,0:T(8,128)S(1)}, f32[256,128]{1,0:T(8,128)S(1)}, u32[]{:S(2)}, u32[]{:S(2)}) collective-permute-start(f32[256,128]{1,0:T(8,128)S(1)} %collective-permute-done.10.rest_3_), channel_id=1, source_target_pairs={{0,1},{1,0},{2,3},{3,2},{4,5},{5,4},{6,7},{7,6},{8,9},{9,8},{10,11... | collective-permute-start | bytes 393224 | tf_op jit(solution)/shard_map/ppermute | solution.py:591
  64.0 1.3 %collective-permute-start.12 = (f32[256,128]{1,0:T(8,128)S(1)}, f32[256,128]{1,0:T(8,128)S(1)}, u32[]{:S(2)}, u32[]{:S(2)}) collective-permute-start(f32[256,128]{1,0:T(8,128)S(1)} %collective-permute-done.8.rest_1_), channel_id=1, source_target_pairs={{0,1},{1,0},{2,3},{3,2},{4,5},{5,4},{6,7},{7,6},{8,9},{9,8},{10,11... | collective-permute-start | bytes 393224 | tf_op jit(solution)/shard_map/ppermute | solution.py:591

commit v4 on v3

--- a/solution.py
+++ b/solution.py
@@ -89,7 +89,7 @@
     for rho in range(classes):
         cos, sin = phases(rho + classes * np.arange(steps), freqs, length)
         out.append(tiles_of(cos, -sin, band, 1))
-    return np.stack(out).astype(BF16)
+    return split(np.stack(out)).transpose(1, 0, 2, 3)
 
 
 def flip_table(band):
@@ -394,7 +394,7 @@
     low_parts, high_parts = rest[:members], rest[members : 2 * members]
     outs = rest[2 * members : 2 * members + many]
     held_ref, last_ref = rest[2 * members + many :]
-    steps = tables[0].shape[0]
+    steps = tables[0].shape[1]
     low, width = low_parts[0].shape
     band = held_ref.shape[1]
     wide = width // 2
@@ -426,7 +426,10 @@
             for re, im in planes[turn * cores : (turn + 1) * cores]:
                 blocks += [cos * re - sin * im, sin * re + cos * im] if turn else [re, im]
             stacked = jnp.concatenate(blocks, 0)
-            corr = corr + jnp.dot(tables[which][...], stacked, preferred_element_type=jnp.float32)
+            for level in range(2):
+                corr = corr + jnp.dot(
+                    tables[which][level], stacked, preferred_element_type=jnp.float32
+                )
         corr = corr * (scale * (1 - 2 * (side * rho % 2)).astype(jnp.float32))
         peak = corr[:, :WCOLS]
         power = corr[:, :WCOLS] * corr[:, :WCOLS]
@@ -451,7 +454,7 @@
 def columns(parts, tables, group_of, classes, band, scale, share, dtype):
     members = len(parts) // 2
     many = len(group_of)
-    steps = tables[0].shape[0]
+    steps = tables[0].shape[1]
     height = steps // (members // 2)
     width = parts[0].shape[1]
     roots = np.round(np.exp(2j * np.pi * np.arange(classes) / classes), 12)
@@ -581,7 +584,7 @@
             band,
             1.0 / (length * tsize),
             window / max(window, members),
-            jnp.float32,
+            jnp.bfloat16,
         )
         for s, one in zip(group, made):
             maps[s] = one

time: 66.8 us -> 63.3 us (0.948)
  waiting for transfers between devices: 15.3 us -> 8.09 us
  local copies, waits for them, and re-layouts: 3.71 us -> 5.63 us
  Pallas kernels: 30.5 us -> 32.2 us
    ppermute x3, waiting for transfers between devices: 8.76 us -> 3.72 us  [shards(): lax.ppermute(maps[s], 'row', [(i, i ^ s) for i in range(classes)])]
    ppermute x6, waiting for transfers between devices: 5.17 us -> 3.12 us  [shards(): got.append(lax.ppermute(parts[s], line, [(i, i ^ s) for i in range(count)]))]
    squeeze x1, local copies, waits for them, and re-layouts: 2.63 us -> 4.67 us  [shards(): lax.dynamic_index_in_dim(all_tables, rho, 0, False)]
    pallas_call x2, Pallas kernels: 4.96 us -> 6.66 us  [columns(): pl.pallas_call(functools.partial(column_kernel, group_of, scale, share),...]
  transfers between devices with their start and end apart: 15 -> 15, of which waited for: 6 -> 6; matrix products, arithmetic and copies ran while one was open for 5% -> 8% of each run, Pallas kernels for 35% -> 38%
where the time goes in v4:
time: 63.3 us; the launch traced here: 63.1 us
  Pallas kernels  32.2 us (51%)
  starting transfers between devices  15.6 us (25%)
  waiting for transfers between devices  8.09 us (13%)
  local copies, waits for them, and re-layouts  5.63 us (9%)
  between operations  0.99 us (2%)
    pallas_call x2, Pallas kernels, template_spectra(): pl.pallas_call(functools.partial(template_kernel, fresh), out_shape=out_s...  8.06 us
    pallas_call x1, Pallas kernels, window_rest(): pl.pallas_call(rest_kernel, out_shape=[jax.ShapeDtypeStruct((rows, ratio...  7.78 us
    pallas_call x2, Pallas kernels, columns(): pl.pallas_call(functools.partial(column_kernel, group_of, scale, share),...  6.66 us
    ppermute x6, starting transfers between devices, shards(): got.append(lax.ppermute(parts[s], line, [(i, i ^ s) for i in range(count)]))  6.29 us
    pallas_call x2, Pallas kernels, partials(): pl.pallas_call(functools.partial(partial_kernel, len(others), first), out...  4.89 us
    squeeze x1, local copies, waits for them, and re-layouts, shards(): lax.dynamic_index_in_dim(all_tables, rho, 0, False)  4.67 us
    ppermute x1, starting transfers between devices, shards(): others = [lax.ppermute(sent, line, opposite)]  4.55 us
    ppermute x3, starting transfers between devices, shards(): lax.ppermute(maps[s], 'row', [(i, i ^ s) for i in range(classes)])  4.32 us
  transfers between devices with their start and end apart: 15, of which 6 were waited for; matrix products, arithmetic and copies ran while one was open for 8% of the time, Pallas kernels for 38%

profile of v4, /device:TPU:0, one launch (start us, length us, event | category | flops | bytes accessed | tf_op | source)
XLA Modules:
  0.0 63.1 jit_solution(15583423391290391598)
XLA Ops:
  0.6 3.5 %window_first.1 = bf16[128,1024]{1,0:T(8,128)(2,1)} custom-call(bf16[2,2,512,2048]{3,2,1,0:T(8,128)(2,1)} %spec_ref.2, bf16[2,4,512,256]{3,2,1,0:T(8,128)(2,1)} %constant.150.clone.tables_ref.table_ref), custom_call_target="tpu_custom_call" | custom-call | flops 1073741824 | bytes 2097152 | tf_op jit(solution)/shard_map/window_first/pallas_call | solution.py:174
  4.2 4.6 %collective-permute-start = (bf16[128,1024]{1,0:T(8,128)(2,1)}, bf16[128,1024]{1,0:T(8,128)(2,1)S(1)}, u32[]{:S(2)}, u32[]{:S(2)}) collective-permute-start(bf16[128,1024]{1,0:T(8,128)(2,1)} %window_first.1), channel_id=1, source_target_pairs={{0,13},{1,12},{4,9},{5,8},{8,5},{9,4},{12,1},{13,0},{2,15},{3,14},... | collective-permute-start | bytes 786440 | tf_op jit(solution)/shard_map/ppermute | solution.py:545
  8.7 0.6 pad_add_fusion.place_ref
  9.3 7.8 %window_rest.1 = (bf16[128,1024]{1,0:T(8,128)(2,1)}, f32[256,1024]{1,0:T(8,128)}, bf16[2,128,384]{2,1,0:T(8,128)(2,1)}, bf16[2,144,384]{2,1,0:T(8,128)(2,1)}) custom-call(s32[3]{0:T(128)} %pad_add_fusion.place_ref, bf16[2,2,512,2048]{3,2,1,0:T(8,128)(2,1)} %spec_ref.2, bf16[2,4,512,256]{3,2,1,0:T(8,128)(2,1)} %constant.150.clone.tables_ref.table_ref, ...), custom_call_target="tpu_custom_call" | custom-call | flops 3221225472 | bytes 5242880 | tf_op jit(solution)/shard_map/window_rest/pallas_call | solution.py:225
  17.1 0.0 collective-permute-start.1
  17.2 0.9 %copy-done.7 = bf16[2,128,384]{2,1,0:T(8,128)(2,1)S(1)} copy-done((bf16[2,128,384]{2,1,0:T(8,128)(2,1)S(1)}, bf16[2,128,384]{2,1,0:T(8,128)(2,1)}, u32[]{:S(2)}) %copy-start.7) | copy-done | bytes 196632
  18.1 4.4 %templates.2 = (f32[4,1024,256]{2,1,0:T(8,128)S(1)}, bf16[8,384,384]{2,1,0:T(8,128)(2,1)S(1)}) custom-call(s32[8]{0:T(128)S(1)} %copy-done.8, bf16[8,384,384]{2,1,0:T(8,128)(2,1)S(1)} %copy-done.5, bf16[2,128,384]{2,1,0:T(8,128)(2,1)S(1)} %copy-done.7, bf16[4,768,256]{2,1,0:T(8,128)(2,1)S(1)} %copy-done.9), custom_call_target="tpu_custom_call" | custom-call | flops 2214592512 | bytes 6553600 | tf_op jit(solution)/shard_map/templates/pallas_call | solution.py:294
  22.6 2.3 %partials.2 = (bf16[128,512]{1,0:T(8,128)(2,1)S(1)}, bf16[128,512]{1,0:T(8,128)(2,1)S(1)}, bf16[128,512]{1,0:T(8,128)(2,1)S(1)}, bf16[128,512]{1,0:T(8,128)(2,1)S(1)}) custom-call(f32[256,1024]{1,0:T(8,128)S(1)} %copy-done.1, bf16[128,128]{1,0:T(8,128)(2,1)S(1)} %copy-done.3, f32[4,1024,256]{2,1,0:T(8,128)S(1)} %get-tuple-element.42.tspec_ref, ...), custom_call_target="tpu_custom_call" | custom-call | flops 1610612736 | bytes 2097152 | tf_op jit(solution)/shard_map/partials/pallas_call | solution.py:371
  24.9 0.7 %collective-permute-start.2 = (bf16[128,512]{1,0:T(8,128)(2,1)S(1)}, bf16[128,512]{1,0:T(8,128)(2,1)S(1)}, u32[]{:S(2)}, u32[]{:S(2)}) collective-permute-start(bf16[128,512]{1,0:T(8,128)(2,1)S(1)} %get-tuple-element.47), channel_id=1, source_target_pairs={{0,1},{1,0},{4,5},{5,4},{8,9},{9,8},{12,13},{13,12},{2,3},{3,2},{6... | collective-permute-start | bytes 393224 | tf_op jit(solution)/shard_map/ppermute | solution.py:567
  25.7 3.3 %collective-permute-start.3 = (bf16[128,512]{1,0:T(8,128)(2,1)S(1)}, bf16[128,512]{1,0:T(8,128)(2,1)S(1)}, u32[]{:S(2)}, u32[]{:S(2)}) collective-permute-start(bf16[128,512]{1,0:T(8,128)(2,1)S(1)} %get-tuple-element.48), channel_id=1, source_target_pairs={{0,4},{1,5},{4,0},{5,1},{8,12},{9,13},{12,8},{13,9},{2,6},{3,7},{6... | collective-permute-start | bytes 393224 | tf_op jit(solution)/shard_map/ppermute | solution.py:567
  29.0 0.1 collective-permute-start.4
  29.1 3.6 %templates.3.tspec_ref = f32[4,1152,256]{2,1,0:T(8,128)S(1)} custom-call(s32[8]{0:T(128)S(1)} %copy-done.8, bf16[8,384,384]{2,1,0:T(8,128)(2,1)S(1)} %get-tuple-element.44.bank_ref, bf16[2,144,384]{2,1,0:T(8,128)(2,1)S(1)} %copy-done.6, bf16[4,768,256]{2,1,0:T(8,128)(2,1)S(1)} %copy-done.9), custom_call_target="tpu_custom_call" | custom-call | flops 2491416576 | bytes 7077888 | tf_op jit(solution)/shard_map/templates/pallas_call | solution.py:294
  32.7 0.0 collective-permute-done.1.rest_0_
  32.7 0.6 collective-permute-done.3.rest_4_
  33.3 2.6 %partials.3 = (bf16[144,512]{1,0:T(8,128)(2,1)S(1)}, bf16[144,512]{1,0:T(8,128)(2,1)S(1)}, bf16[144,512]{1,0:T(8,128)(2,1)S(1)}, bf16[144,512]{1,0:T(8,128)(2,1)S(1)}) custom-call(f32[256,1024]{1,0:T(8,128)S(1)} %copy-done.1, bf16[144,256]{1,0:T(8,128)(2,1)S(1)} %copy-done.2, f32[4,1152,256]{2,1,0:T(8,128)S(1)} %templates.3.tspec_ref, ...), custom_call_target="tpu_custom_call" | custom-call | flops 1811939328 | bytes 2359296 | tf_op jit(solution)/shard_map/partials/pallas_call | solution.py:371
  36.1 0.1 collective-permute-start.5
  36.2 2.0 %collective-permute-start.6 = (bf16[144,512]{1,0:T(8,128)(2,1)S(1)}, bf16[144,512]{1,0:T(8,128)(2,1)S(1)}, u32[]{:S(2)}, u32[]{:S(2)}) collective-permute-start(bf16[144,512]{1,0:T(8,128)(2,1)S(1)} %get-tuple-element.56), channel_id=1, source_target_pairs={{0,4},{1,5},{4,0},{5,1},{8,12},{9,13},{12,8},{13,9},{2,6},{3,7},{6... | collective-permute-start | bytes 442376 | tf_op jit(solution)/shard_map/ppermute | solution.py:567
  38.2 0.1 collective-permute-start.7
  38.3 4.7 %dynamic-slice_bitcast_fusion = (bf16[2,512,1024]{2,1,0:T(8,128)(2,1)S(1)}, bf16[2,512,1024]{2,1,0:T(8,128)(2,1)S(1)}, bf16[2,512,1024]{2,1,0:T(8,128)(2,1)S(1)}, bf16[2,512,1024]{2,1,0:T(8,128)(2,1)S(1)}) fusion(bf16[4,2,512,1024]{3,2,1,0:T(8,128)(2,1)} %constant.156.clone, s32[]{:T(128)S(6)} %select_n.84, s32[]{:T(128)S(6)} %select_n.76, s32[]{:T(128)S(6)} %select_n.72, ...), kind=kLoop, calls=%fused_computation | loop fusion | bytes 16777232 | tf_op jit(solution)/shard_map/jit(dynamic_index_in_dim)/squeeze | solution.py:581
  43.0 0.0 collective-permute-done.4.rest_5_
  43.0 2.5 %collective-permute-done.7.rest_9_ = bf16[144,512]{1,0:T(8,128)(2,1)S(1)} collective-permute-done((bf16[144,512]{1,0:T(8,128)(2,1)S(1)}, bf16[144,512]{1,0:T(8,128)(2,1)S(1)}, u32[]{:S(2)}, u32[]{:S(2)}) %collective-permute-start.7) | collective-permute-done | bytes 147488 | tf_op jit(solution)/shard_map/ppermute | solution.py:567
  45.5 3.3 %columns.3 = (bf16[256,128]{1,0:T(8,128)(2,1)S(1)}, bf16[256,128]{1,0:T(8,128)(2,1)S(1)}) custom-call(f32[2,4]{1,0:T(2,128)S(1)} %copy-done.4, bf16[2,512,1024]{2,1,0:T(8,128)(2,1)S(1)} %get-tuple-element.65.rest_0_, bf16[2,512,1024]{2,1,0:T(8,128)(2,1)S(1)} %get-tuple-element.62.rest_1_, bf16[128,512]{1,0:T(8,128)(2,1)S(1)} %get-tuple-element.43.rest_2_, ...), custom_call_target="tpu_custom_call" | custom-call | flops 1073741824 | bytes 4194304 | tf_op jit(solution)/shard_map/columns/pallas_call | solution.py:462
  48.8 3.6 %collective-permute-start.9 = (bf16[256,128]{1,0:T(8,128)(2,1)S(1)}, bf16[256,128]{1,0:T(8,128)(2,1)S(1)}, u32[]{:S(2)}, u32[]{:S(2)}) collective-permute-start(bf16[256,128]{1,0:T(8,128)(2,1)S(1)} %get-tuple-element.60), channel_id=1, source_target_pairs={{0,8},{4,12},{8,0},{12,4},{1,9},{5,13},{9,1},{13,5},{2,10},{6,14},... | collective-permute-start | bytes 196616 | tf_op jit(solution)/shard_map/ppermute | solution.py:593
  52.4 0.5 collective-permute-start.10
  52.9 3.3 %columns.2 = (bf16[256,128]{1,0:T(8,128)(2,1)S(1)}, bf16[256,128]{1,0:T(8,128)(2,1)S(1)}) custom-call(f32[2,4]{1,0:T(2,128)S(1)} %copy-done.4, bf16[2,512,1024]{2,1,0:T(8,128)(2,1)S(1)} %get-tuple-element.64.rest_0_, bf16[2,512,1024]{2,1,0:T(8,128)(2,1)S(1)} %get-tuple-element.63.rest_1_, bf16[128,512]{1,0:T(8,128)(2,1)S(1)} %get-tuple-element.43.rest_2_, ...), custom_call_target="tpu_custom_call" | custom-call | flops 1073741824 | bytes 4194304 | tf_op jit(solution)/shard_map/columns/pallas_call | solution.py:462
  56.2 0.3 collective-permute-start.8
  56.5 0.2 collective-permute-done.9.rest_2_
  56.6 0.3 collective-permute-start.13
  57.0 1.6 %collective-permute-done.10.rest_3_ = bf16[256,128]{1,0:T(8,128)(2,1)S(1)} collective-permute-done((bf16[256,128]{1,0:T(8,128)(2,1)S(1)}, bf16[256,128]{1,0:T(8,128)(2,1)S(1)}, u32[]{:S(2)}, u32[]{:S(2)}) %collective-permute-start.10) | collective-permute-done | bytes 65568 | tf_op jit(solution)/shard_map/ppermute | solution.py:593
  58.5 2.0 %collective-permute-done.8.rest_1_ = bf16[256,128]{1,0:T(8,128)(2,1)S(1)} collective-permute-done((bf16[256,128]{1,0:T(8,128)(2,1)S(1)}, bf16[256,128]{1,0:T(8,128)(2,1)S(1)}, u32[]{:S(2)}, u32[]{:S(2)}) %collective-permute-start.8) | collective-permute-done | bytes 65568 | tf_op jit(solution)/shard_map/ppermute | solution.py:593
  60.6 1.2 %collective-permute-done.12.rest_5_ = bf16[256,128]{1,0:T(8,128)(2,1)S(1)} collective-permute-done((bf16[256,128]{1,0:T(8,128)(2,1)S(1)}, bf16[256,128]{1,0:T(8,128)(2,1)S(1)}, u32[]{:S(2)}, u32[]{:S(2)}) %collective-permute-start.12) | collective-permute-done | bytes 65568 | tf_op jit(solution)/shard_map/ppermute | solution.py:594
  61.8 1.3 %unpack.1 = (f32[2,1,512,128]{3,2,1,0:T(8,128)}, f32[2,1,512,128]{3,2,1,0:T(8,128)}) custom-call(bf16[256,128]{1,0:T(8,128)(2,1)S(1)} %get-tuple-element.58.rest_0_, bf16[256,128]{1,0:T(8,128)(2,1)S(1)} %collective-permute-done.8.rest_1_, bf16[256,128]{1,0:T(8,128)(2,1)S(1)} %collective-permute-done.9.rest_2_, ...), custom_call_target="tpu_custom_call" | custom-call | tf_op jit(solution)/shard_map/unpack/pallas_call | solution.py:509
  (29 shorter events, 0.1 us)
Async XLA Ops:
  4.2 18.4 %collective-permute-start = (bf16[128,1024]{1,0:T(8,128)(2,1)}, bf16[128,1024]{1,0:T(8,128)(2,1)S(1)}, u32[]{:S(2)}, u32[]{:S(2)}) collective-permute-start(bf16[128,1024]{1,0:T(8,128)(2,1)} %window_first.1), channel_id=1, source_target_pairs={{0,13},{1,12},{4,9},{5,8},{8,5},{9,4},{12,1},{13,0},{2,15},{3,14},... | collective-permute-start | bytes 786440 | tf_op jit(solution)/shard_map/ppermute | solution.py:545
  9.3 7.8 %copy-start.5 = (bf16[8,384,384]{2,1,0:T(8,128)(2,1)S(1)}, bf16[8,384,384]{2,1,0:T(8,128)(2,1)}, u32[]{:S(2)}) copy-start(bf16[8,384,384]{2,1,0:T(8,128)(2,1)} %bank_ref) | copy-start | bytes 7077892
  9.3 7.8 %copy-start.8 = (s32[8]{0:T(128)S(1)}, s32[8]{0:T(128)}, u32[]{:S(2)}) copy-start(s32[8]{0:T(128)} %index_ref.3) | copy-start | bytes 100
  9.3 7.8 %copy-start.9 = (bf16[4,768,256]{2,1,0:T(8,128)(2,1)S(1)}, bf16[4,768,256]{2,1,0:T(8,128)(2,1)}, u32[]{:S(2)}) copy-start(bf16[4,768,256]{2,1,0:T(8,128)(2,1)} %constant.153.clone.right_ref) | copy-start | bytes 4718596
  17.1 15.6 %collective-permute-start.1 = (bf16[128,1024]{1,0:T(8,128)(2,1)}, bf16[128,1024]{1,0:T(8,128)(2,1)S(1)}, u32[]{:S(2)}, u32[]{:S(2)}) collective-permute-start(bf16[128,1024]{1,0:T(8,128)(2,1)} %get-tuple-element.46), channel_id=1, source_target_pairs={{0,13},{1,12},{4,9},{5,8},{8,5},{9,4},{12,1},{13,0},{2,15},{3,14},... | collective-permute-start | bytes 786440 | tf_op jit(solution)/shard_map/ppermute | solution.py:548
  17.2 0.9 %copy-start.7 = (bf16[2,128,384]{2,1,0:T(8,128)(2,1)S(1)}, bf16[2,128,384]{2,1,0:T(8,128)(2,1)}, u32[]{:S(2)}) copy-start(bf16[2,128,384]{2,1,0:T(8,128)(2,1)} %get-tuple-element.39.left_ref) | copy-start | bytes 589828
  18.1 4.5 %copy-start = (bf16[2,4,256,256]{3,2,1,0:T(8,128)(2,1)S(1)}, bf16[2,4,256,256]{3,2,1,0:T(8,128)(2,1)}, u32[]{:S(2)}) copy-start(bf16[2,4,256,256]{3,2,1,0:T(8,128)(2,1)} %constant.151.clone.back_ref) | copy-start | bytes 3145732
  18.1 4.5 %copy-start.1 = (f32[256,1024]{1,0:T(8,128)S(1)}, f32[256,1024]{1,0:T(8,128)}, u32[]{:S(2)}) copy-start(f32[256,1024]{1,0:T(8,128)} %get-tuple-element.37.keep_ref) | copy-start | bytes 3145732
  18.1 4.5 %copy-start.3 = (bf16[128,128]{1,0:T(8,128)(2,1)S(1)}, bf16[128,128]{1,0:T(8,128)(2,1)}, u32[]{:S(2)}) copy-start(bf16[128,128]{1,0:T(8,128)(2,1)} %constant.154.clone.flip_ref) | copy-start | bytes 98308
  22.6 6.5 %copy-start.6 = (bf16[2,144,384]{2,1,0:T(8,128)(2,1)S(1)}, bf16[2,144,384]{2,1,0:T(8,128)(2,1)}, u32[]{:S(2)}) copy-start(bf16[2,144,384]{2,1,0:T(8,128)(2,1)} %get-tuple-element.45.left_ref) | copy-start | bytes 663556
  24.9 7.8 %collective-permute-start.2 = (bf16[128,512]{1,0:T(8,128)(2,1)S(1)}, bf16[128,512]{1,0:T(8,128)(2,1)S(1)}, u32[]{:S(2)}, u32[]{:S(2)}) collective-permute-start(bf16[128,512]{1,0:T(8,128)(2,1)S(1)} %get-tuple-element.47), channel_id=1, source_target_pairs={{0,1},{1,0},{4,5},{5,4},{8,9},{9,8},{12,13},{13,12},{2,3},{3,2},{6... | collective-permute-start | bytes 393224 | tf_op jit(solution)/shard_map/ppermute | solution.py:567
  25.7 7.7 %collective-permute-start.3 = (bf16[128,512]{1,0:T(8,128)(2,1)S(1)}, bf16[128,512]{1,0:T(8,128)(2,1)S(1)}, u32[]{:S(2)}, u32[]{:S(2)}) collective-permute-start(bf16[128,512]{1,0:T(8,128)(2,1)S(1)} %get-tuple-element.48), channel_id=1, source_target_pairs={{0,4},{1,5},{4,0},{5,1},{8,12},{9,13},{12,8},{13,9},{2,6},{3,7},{6... | collective-permute-start | bytes 393224 | tf_op jit(solution)/shard_map/ppermute | solution.py:567
  29.0 4.4 %copy-start.2 = (bf16[144,256]{1,0:T(8,128)(2,1)S(1)}, bf16[144,256]{1,0:T(8,128)(2,1)}, u32[]{:S(2)}) copy-start(bf16[144,256]{1,0:T(8,128)(2,1)} %constant.155.clone.flip_ref) | copy-start | bytes 221188
  29.0 14.0 %collective-permute-start.4 = (bf16[128,512]{1,0:T(8,128)(2,1)S(1)}, bf16[128,512]{1,0:T(8,128)(2,1)S(1)}, u32[]{:S(2)}, u32[]{:S(2)}) collective-permute-start(bf16[128,512]{1,0:T(8,128)(2,1)S(1)} %get-tuple-element.54), channel_id=1, source_target_pairs={{0,5},{1,4},{4,1},{5,0},{8,13},{9,12},{12,9},{13,8},{2,7},{3,6},{6... | collective-permute-start | bytes 393224 | tf_op jit(solution)/shard_map/ppermute | solution.py:567
  36.1 6.9 %collective-permute-start.5 = (bf16[144,512]{1,0:T(8,128)(2,1)S(1)}, bf16[144,512]{1,0:T(8,128)(2,1)S(1)}, u32[]{:S(2)}, u32[]{:S(2)}) collective-permute-start(bf16[144,512]{1,0:T(8,128)(2,1)S(1)} %get-tuple-element.55), channel_id=1, source_target_pairs={{0,1},{1,0},{4,5},{5,4},{8,9},{9,8},{12,13},{13,12},{2,3},{3,2},{6... | collective-permute-start | bytes 442376 | tf_op jit(solution)/shard_map/ppermute | solution.py:567
  36.2 6.8 %collective-permute-start.6 = (bf16[144,512]{1,0:T(8,128)(2,1)S(1)}, bf16[144,512]{1,0:T(8,128)(2,1)S(1)}, u32[]{:S(2)}, u32[]{:S(2)}) collective-permute-start(bf16[144,512]{1,0:T(8,128)(2,1)S(1)} %get-tuple-element.56), channel_id=1, source_target_pairs={{0,4},{1,5},{4,0},{5,1},{8,12},{9,13},{12,8},{13,9},{2,6},{3,7},{6... | collective-permute-start | bytes 442376 | tf_op jit(solution)/shard_map/ppermute | solution.py:567
  38.2 7.3 %collective-permute-start.7 = (bf16[144,512]{1,0:T(8,128)(2,1)S(1)}, bf16[144,512]{1,0:T(8,128)(2,1)S(1)}, u32[]{:S(2)}, u32[]{:S(2)}) collective-permute-start(bf16[144,512]{1,0:T(8,128)(2,1)S(1)} %get-tuple-element.57), channel_id=1, source_target_pairs={{0,5},{1,4},{4,1},{5,0},{8,13},{9,12},{12,9},{13,8},{2,7},{3,6},{6... | collective-permute-start | bytes 442376 | tf_op jit(solution)/shard_map/ppermute | solution.py:567
  38.3 7.2 %copy-start.4 = (f32[2,4]{1,0:T(2,128)S(1)}, f32[2,4]{1,0:T(2,128)}, u32[]{:S(2)}) copy-start(f32[2,4]{1,0:T(2,128)} %constant.157.clone.roots_ref) | copy-start | bytes 100
  48.8 7.8 %collective-permute-start.9 = (bf16[256,128]{1,0:T(8,128)(2,1)S(1)}, bf16[256,128]{1,0:T(8,128)(2,1)S(1)}, u32[]{:S(2)}, u32[]{:S(2)}) collective-permute-start(bf16[256,128]{1,0:T(8,128)(2,1)S(1)} %get-tuple-element.60), channel_id=1, source_target_pairs={{0,8},{4,12},{8,0},{12,4},{1,9},{5,13},{9,1},{13,5},{2,10},{6,14},... | collective-permute-start | bytes 196616 | tf_op jit(solution)/shard_map/ppermute | solution.py:593
  52.4 6.1 %collective-permute-start.10 = (bf16[256,128]{1,0:T(8,128)(2,1)S(1)}, bf16[256,128]{1,0:T(8,128)(2,1)S(1)}, u32[]{:S(2)}, u32[]{:S(2)}) collective-permute-start(bf16[256,128]{1,0:T(8,128)(2,1)S(1)} %get-tuple-element.61), channel_id=1, source_target_pairs={{0,12},{4,8},{8,4},{12,0},{1,13},{5,9},{9,5},{13,1},{2,14},{6,10},... | collective-permute-start | bytes 196616 | tf_op jit(solution)/shard_map/ppermute | solution.py:593
  56.2 4.3 %collective-permute-start.8 = (bf16[256,128]{1,0:T(8,128)(2,1)S(1)}, bf16[256,128]{1,0:T(8,128)(2,1)S(1)}, u32[]{:S(2)}, u32[]{:S(2)}) collective-permute-start(bf16[256,128]{1,0:T(8,128)(2,1)S(1)} %get-tuple-element.59), channel_id=1, source_target_pairs={{0,4},{4,0},{8,12},{12,8},{1,5},{5,1},{9,13},{13,9},{2,6},{6,2},{1... | collective-permute-start | bytes 196616 | tf_op jit(solution)/shard_map/ppermute | solution.py:593
  56.5 4.1 %collective-permute-start.11 = (bf16[256,128]{1,0:T(8,128)(2,1)S(1)}, bf16[256,128]{1,0:T(8,128)(2,1)S(1)}, u32[]{:S(2)}, u32[]{:S(2)}) collective-permute-start(bf16[256,128]{1,0:T(8,128)(2,1)S(1)} %get-tuple-element.58.rest_0_), channel_id=1, source_target_pairs={{0,1},{1,0},{2,3},{3,2},{4,5},{5,4},{6,7},{7,6},{8,9},{9,8},{10,11... | collective-permute-start | bytes 196616 | tf_op jit(solution)/shard_map/ppermute | solution.py:594
  56.6 3.9 %collective-permute-start.13 = (bf16[256,128]{1,0:T(8,128)(2,1)S(1)}, bf16[256,128]{1,0:T(8,128)(2,1)S(1)}, u32[]{:S(2)}, u32[]{:S(2)}) collective-permute-start(bf16[256,128]{1,0:T(8,128)(2,1)S(1)} %collective-permute-done.9.rest_2_), channel_id=1, source_target_pairs={{0,1},{1,0},{2,3},{3,2},{4,5},{5,4},{6,7},{7,6},{8,9},{9,8},{10,11... | collective-permute-start | bytes 196616 | tf_op jit(solution)/shard_map/ppermute | solution.py:594
  58.5 2.0 %collective-permute-start.14 = (bf16[256,128]{1,0:T(8,128)(2,1)S(1)}, bf16[256,128]{1,0:T(8,128)(2,1)S(1)}, u32[]{:S(2)}, u32[]{:S(2)}) collective-permute-start(bf16[256,128]{1,0:T(8,128)(2,1)S(1)} %collective-permute-done.10.rest_3_), channel_id=1, source_target_pairs={{0,1},{1,0},{2,3},{3,2},{4,5},{5,4},{6,7},{7,6},{8,9},{9,8},{10,11... | collective-permute-start | bytes 196616 | tf_op jit(solution)/shard_map/ppermute | solution.py:594
  60.5 1.3 %collective-permute-start.12 = (bf16[256,128]{1,0:T(8,128)(2,1)S(1)}, bf16[256,128]{1,0:T(8,128)(2,1)S(1)}, u32[]{:S(2)}, u32[]{:S(2)}) collective-permute-start(bf16[256,128]{1,0:T(8,128)(2,1)S(1)} %collective-permute-done.8.rest_1_), channel_id=1, source_target_pairs={{0,1},{1,0},{2,3},{3,2},{4,5},{5,4},{6,7},{7,6},{8,9},{9,8},{10,11... | collective-permute-start | bytes 196616 | tf_op jit(solution)/shard_map/ppermute | solution.py:594

commit v5 on v4

--- a/solution.py
+++ b/solution.py
@@ -82,14 +82,21 @@
     return split(table.reshape(win // lanes, 2 * lanes, 2 * WCOLS))
 
 
+def sorted_rows(count):
+    return np.concatenate([np.arange(0, count, 2), np.arange(1, count, 2)])
+
+
 def column_table(length, classes, cores, band):
     steps = length // classes
     freqs = np.arange(cores * band)
     out = []
     for rho in range(classes):
-        cos, sin = phases(rho + classes * np.arange(steps), freqs, length)
-        out.append(tiles_of(cos, -sin, band, 1))
-    return split(np.stack(out)).transpose(1, 0, 2, 3)
+        rows = rho + classes * np.arange(steps // 2)
+        for parity in range(2):
+            cos, sin = phases(rows, freqs[parity::2], length)
+            upper, lower = split(tiles_of(cos, -sin, band // 2, 1))
+            out.append(np.concatenate([upper, lower], 0))
+    return np.stack(out).reshape(classes, 2, steps, cores * band)
 
 
 def flip_table(band):
@@ -117,7 +124,7 @@
     return row, core, members, device % members, device // members
 
 
-def window_block(mirrored, spec, table, out_ref):
+def window_block(mirrored, spec, table, out_ref, order=None):
     rows, total = out_ref.shape
     ratio = table(None)
     width = total // ratio
@@ -142,9 +149,13 @@
         out_im = re[:, lanes:] + im[:, :lanes]
         if mirrored:
             out_im = -out_im
-        start = part * width
-        out_ref[:, start : start + lanes] = out_re.astype(out_ref.dtype)
-        out_ref[:, start + lanes : start + width] = out_im.astype(out_ref.dtype)
+        both = jnp.concatenate([out_re, out_im], 1)
+        if order is not None:
+            upper = both.astype(jnp.bfloat16)
+            lower = (both - upper.astype(jnp.float32)).astype(jnp.bfloat16)
+            both = jnp.dot(order, upper, preferred_element_type=jnp.float32)
+            both += jnp.dot(order, lower, preferred_element_type=jnp.float32)
+        out_ref[:, part * width : (part + 1) * width] = both.astype(out_ref.dtype)
 
 
 def first_kernel(spec_ref, tables_ref, out_ref, held_ref, table_ref, sem):
@@ -191,7 +202,7 @@
     )(spectra, tables)
 
 
-def rest_kernel(place_ref, spec_ref, table_ref, main_ref, more_ref, *outs):
+def rest_kernel(place_ref, spec_ref, table_ref, order_ref, main_ref, more_ref, *outs):
     sent_ref, keep_ref, low_ref, high_ref = outs
     step = pl.program_id(0)
     spec = lambda part, at: spec_ref[0, part, :, at]
@@ -207,7 +218,7 @@
 
     @pl.when(step > 0)
     def _():
-        window_block(False, spec, table, keep_ref)
+        window_block(False, spec, table, keep_ref, order_ref[...])
 
 
 def window_rest(spectra, tables, left, rows):
@@ -217,6 +228,7 @@
     band = 2 * rows
     tsize = left.shape[2]
     at = jnp.stack([side, core, device]).astype(jnp.int32)
+    order = jnp.asarray(np.eye(rows)[sorted_rows(rows)].astype(BF16))
 
     def spec_index(i, at):
         first = jnp.where(i == 0, 1, 0)
@@ -236,6 +248,7 @@
             in_specs=[
                 pl.BlockSpec((1, 2, rows, ratio * win), spec_index),
                 pl.BlockSpec((1, ratio, win, width), lambda i, at: (jnp.minimum(i, 1), 0, 0, 0)),
+                pl.BlockSpec((rows, rows), lambda i, at: (0, 0)),
                 pl.BlockSpec((2, band, tsize), lambda i, at: (0, at[2], 0)),
                 pl.BlockSpec((2, PAD, tsize), lambda i, at: (0, (at[2] + 1) * (band // PAD), 0)),
             ],
@@ -253,7 +266,7 @@
             transcendentals=0,
         ),
         name="window_rest",
-    )(at, spectra, tables, left, left)
+    )(at, spectra, tables, order, left, left)
 
 
 def template_kernel(fresh, index_ref, bank_ref, left_ref, right_ref, out_ref, *rest):
@@ -394,7 +407,7 @@
     low_parts, high_parts = rest[:members], rest[members : 2 * members]
     outs = rest[2 * members : 2 * members + many]
     held_ref, last_ref = rest[2 * members + many :]
-    steps = tables[0].shape[1]
+    _, steps, depth = tables[0].shape
     low, width = low_parts[0].shape
     band = held_ref.shape[1]
     wide = width // 2
@@ -403,13 +416,18 @@
         held_ref[member, :low] = low_parts[s][...]
         held_ref[member, low:] = high_parts[s][: band - low]
         last_ref[member] = high_parts[s][band - low :]
-    planes = []
+    planes = [[], []]
     for member in range(members):
         block = held_ref[member]
-        if member:
-            head = block[:PAD].astype(jnp.float32) + last_ref[member - 1].astype(jnp.float32)
-            block = jnp.concatenate([head.astype(jnp.bfloat16), block[PAD:]], 0)
-        planes.append((block[:, :wide], block[:, wide:]))
+        for parity in range(2):
+            at = parity * (low // 2)
+            piece = jnp.concatenate(
+                [block[at : at + low // 2], block[low + at : low + at + low // 2]], 0
+            )
+            if member and not parity:
+                head = piece[:PAD].astype(jnp.float32) + last_ref[member - 1].astype(jnp.float32)
+                piece = jnp.concatenate([head.astype(jnp.bfloat16), piece[PAD:]], 0)
+            planes[parity].append((piece[:, :wide], piece[:, wide:]))
     top = last_ref[members - 1][:1, :wide].astype(jnp.float32)
     group = WCOLS // members
     height = steps // (members // 2)
@@ -417,19 +435,19 @@
     kappa = (lane_group + (members - mine)) % members
     for which in range(many):
         rho = reverse_bits(lax.bitwise_xor(row, group_of[which]), bits(classes))
-        corr = (1 - 2 * (rho % 2)).astype(jnp.float32) * top
-        for turn in range(members // cores):
-            angle = rho * turn % classes
-            cos = roots_ref[0, angle].astype(jnp.bfloat16)
-            sin = roots_ref[1, angle].astype(jnp.bfloat16)
-            blocks = []
-            for re, im in planes[turn * cores : (turn + 1) * cores]:
-                blocks += [cos * re - sin * im, sin * re + cos * im] if turn else [re, im]
-            stacked = jnp.concatenate(blocks, 0)
-            for level in range(2):
-                corr = corr + jnp.dot(
-                    tables[which][level], stacked, preferred_element_type=jnp.float32
-                )
+        sums = [(1 - 2 * (rho % 2)).astype(jnp.float32) * top, 0.0]
+        for parity in range(2):
+            for turn in range(members // cores):
+                angle = rho * turn % classes
+                cos = roots_ref[0, angle].astype(jnp.bfloat16)
+                sin = roots_ref[1, angle].astype(jnp.bfloat16)
+                blocks = []
+                for re, im in planes[parity][turn * cores : (turn + 1) * cores]:
+                    blocks += [cos * re - sin * im, sin * re + cos * im] if turn else [re, im]
+                stacked = jnp.concatenate(blocks, 0)
+                got = jnp.dot(tables[which][parity], stacked, preferred_element_type=jnp.float32)
+                sums[parity] = sums[parity] + got[: steps // 2] + got[steps // 2 :]
+        corr = jnp.concatenate([sums[0] + sums[1], sums[0] - sums[1]], 0)
         corr = corr * (scale * (1 - 2 * (side * rho % 2)).astype(jnp.float32))
         peak = corr[:, :WCOLS]
         power = corr[:, :WCOLS] * corr[:, :WCOLS]
@@ -537,10 +555,14 @@
     )
     back = jnp.asarray(back_table(win, lanes))
     flip = flip_table(band)
+    order = sorted_rows(rows)
+    flips = [flip[:rows, rows:][order], np.concatenate([flip[rows:band][order], flip[band:]], 0)]
 
     opposite = [(i, count - 1 - i) for i in range(count)]
     cos, sin = phases(np.arange(length + PAD), np.arange(tsize), length)
-    left = jnp.asarray(np.stack([cos, -sin]).astype(BF16))
+    left = np.stack([cos, -sin]).astype(BF16)
+    chunked = left[:, :length].reshape(2, -1, rows, tsize)[:, :, sorted_rows(rows)]
+    left = jnp.asarray(np.concatenate([chunked.reshape(2, length, tsize), left[:, length:]], 1))
     sent = window_first(spectra, window_tables, rows)
     others = [lax.ppermute(sent, line, opposite)]
     spectra, bank, _ = lax.optimization_barrier((spectra, bank, sent))
@@ -556,7 +578,7 @@
             keep,
             others[1 - block :],
             block * rows,
-            jnp.asarray(flip[:rows, rows:] if block == 0 else flip[rows:]),
+            jnp.asarray(flips[block]),
             tspec,
             back,
             members,

time: 63.3 us -> 60.2 us (0.951)
  starting transfers between devices: 15.6 us -> 13.2 us
  waiting for transfers between devices: 8.09 us -> 10.4 us
  local copies, waits for them, and re-layouts: 5.63 us -> 3.54 us
  Pallas kernels: 32.2 us -> 31.1 us
    ppermute x6, waiting for transfers between devices: 3.12 us -> 5.9 us  [shards(): got.append(lax.ppermute(parts[s], line, [(i, i ^ s) for i in range(count)]))]
    squeeze x1, local copies, waits for them, and re-layouts: 4.67 us -> 2.45 us  [shards(): lax.dynamic_index_in_dim(all_tables, rho, 0, False)]
    ppermute x6, starting transfers between devices: 6.29 us -> 4.09 us  [shards(): got.append(lax.ppermute(parts[s], line, [(i, i ^ s) for i in range(count)]))]
    pallas_call x2, Pallas kernels: 6.66 us -> 4.5 us  [columns(): pl.pallas_call(functools.partial(column_kernel, group_of, scale, share),...]
    pallas_call x1, Pallas kernels: 7.78 us -> 8.85 us  [window_rest(): pl.pallas_call(rest_kernel, out_shape=[jax.ShapeDtypeStruct((rows, ratio...]
  transfers between devices with their start and end apart: 15 -> 15, of which waited for: 6 -> 7; matrix products, arithmetic and copies ran while one was open for 8% -> 5% of each run, Pallas kernels for 38% -> 40%
where the time goes in v5:
time: 60.2 us; the launch traced here: 60 us
  Pallas kernels  31.1 us (52%)
  starting transfers between devices  13.2 us (22%)
  waiting for transfers between devices  10.4 us (17%)
  local copies, waits for them, and re-layouts  3.54 us (6%)
  between operations  0.99 us (2%)
  other arithmetic  0.62 us (1%)
    pallas_call x1, Pallas kernels, window_rest(): pl.pallas_call(rest_kernel, out_shape=[jax.ShapeDtypeStruct((rows, ratio...  8.85 us
    pallas_call x2, Pallas kernels, template_spectra(): pl.pallas_call(functools.partial(template_kernel, fresh), out_shape=out_s...  8.07 us
    ppermute x6, waiting for transfers between devices, shards(): got.append(lax.ppermute(parts[s], line, [(i, i ^ s) for i in range(count)]))  5.9 us
    pallas_call x2, Pallas kernels, partials(): pl.pallas_call(functools.partial(partial_kernel, len(others), first), out...  4.89 us
    ppermute x1, starting transfers between devices, shards(): others = [lax.ppermute(sent, line, opposite)]  4.55 us
    pallas_call x2, Pallas kernels, columns(): pl.pallas_call(functools.partial(column_kernel, group_of, scale, share),...  4.5 us
    ppermute x6, starting transfers between devices, shards(): got.append(lax.ppermute(parts[s], line, [(i, i ^ s) for i in range(count)]))  4.09 us
    ppermute x3, starting transfers between devices, shards(): lax.ppermute(maps[s], 'row', [(i, i ^ s) for i in range(classes)])  3.99 us
  transfers between devices with their start and end apart: 15, of which 7 were waited for; matrix products, arithmetic and copies ran while one was open for 5% of the time, Pallas kernels for 40%

profile of v5, /device:TPU:0, one launch (start us, length us, event | category | flops | bytes accessed | tf_op | source)
XLA Modules:
  0.0 60.0 jit_solution(12153447755191042944)
XLA Ops:
  0.6 3.5 %window_first.1 = bf16[128,1024]{1,0:T(8,128)(2,1)} custom-call(bf16[2,2,512,2048]{3,2,1,0:T(8,128)(2,1)} %spec_ref.2, bf16[2,4,512,256]{3,2,1,0:T(8,128)(2,1)} %constant.152.clone.tables_ref.table_ref), custom_call_target="tpu_custom_call" | custom-call | flops 1073741824 | bytes 2097152 | tf_op jit(solution)/shard_map/window_first/pallas_call | solution.py:185
  4.2 4.6 %collective-permute-start = (bf16[128,1024]{1,0:T(8,128)(2,1)}, bf16[128,1024]{1,0:T(8,128)(2,1)S(1)}, u32[]{:S(2)}, u32[]{:S(2)}) collective-permute-start(bf16[128,1024]{1,0:T(8,128)(2,1)} %window_first.1), channel_id=1, source_target_pairs={{0,13},{1,12},{4,9},{5,8},{8,5},{9,4},{12,1},{13,0},{2,15},{3,14},... | collective-permute-start | bytes 786440 | tf_op jit(solution)/shard_map/ppermute | solution.py:567
  8.7 0.6 %pad_add_fusion.place_ref = s32[3]{0:T(128)} fusion(s32[1]{0:T(128)} %bitcast.2, s32[1]{0:T(128)} %bitcast.1, s32[1]{0:T(128)} %bitcast), kind=kLoop, calls=%fused_computation.4 | loop fusion | flops 6 | bytes 24 | tf_op jit(solution)/shard_map/stack | solution.py:230
  9.3 8.8 %window_rest.1 = (bf16[128,1024]{1,0:T(8,128)(2,1)}, f32[256,1024]{1,0:T(8,128)}, bf16[2,128,384]{2,1,0:T(8,128)(2,1)}, bf16[2,144,384]{2,1,0:T(8,128)(2,1)}) custom-call(s32[3]{0:T(128)} %pad_add_fusion.place_ref, bf16[2,2,512,2048]{3,2,1,0:T(8,128)(2,1)} %spec_ref.2, bf16[2,4,512,256]{3,2,1,0:T(8,128)(2,1)} %constant.152.clone.tables_ref.table_ref, ...), custom_call_target="tpu_custom_call" | custom-call | flops 3221225472 | bytes 5242880 | tf_op jit(solution)/shard_map/window_rest/pallas_call | solution.py:237
  18.2 0.0 copy-start.3
  18.2 0.1 collective-permute-start.1
  18.3 1.0 %copy-done.7 = bf16[2,128,384]{2,1,0:T(8,128)(2,1)S(1)} copy-done((bf16[2,128,384]{2,1,0:T(8,128)(2,1)S(1)}, bf16[2,128,384]{2,1,0:T(8,128)(2,1)}, u32[]{:S(2)}) %copy-start.7) | copy-done | bytes 196632
  19.4 4.4 %templates.2 = (f32[4,1024,256]{2,1,0:T(8,128)S(1)}, bf16[8,384,384]{2,1,0:T(8,128)(2,1)S(1)}) custom-call(s32[8]{0:T(128)S(1)} %copy-done.8, bf16[8,384,384]{2,1,0:T(8,128)(2,1)S(1)} %copy-done.5, bf16[2,128,384]{2,1,0:T(8,128)(2,1)S(1)} %copy-done.7, bf16[4,768,256]{2,1,0:T(8,128)(2,1)S(1)} %copy-done.9), custom_call_target="tpu_custom_call" | custom-call | flops 2214592512 | bytes 6553600 | tf_op jit(solution)/shard_map/templates/pallas_call | solution.py:307
  23.9 2.3 %partials.2 = (bf16[128,512]{1,0:T(8,128)(2,1)S(1)}, bf16[128,512]{1,0:T(8,128)(2,1)S(1)}, bf16[128,512]{1,0:T(8,128)(2,1)S(1)}, bf16[128,512]{1,0:T(8,128)(2,1)S(1)}) custom-call(f32[256,1024]{1,0:T(8,128)S(1)} %copy-done.1, bf16[128,128]{1,0:T(8,128)(2,1)S(1)} %copy-done.3, f32[4,1024,256]{2,1,0:T(8,128)S(1)} %get-tuple-element.42.tspec_ref, ...), custom_call_target="tpu_custom_call" | custom-call | flops 1610612736 | bytes 2097152 | tf_op jit(solution)/shard_map/partials/pallas_call | solution.py:384
  26.2 0.7 %collective-permute-start.2 = (bf16[128,512]{1,0:T(8,128)(2,1)S(1)}, bf16[128,512]{1,0:T(8,128)(2,1)S(1)}, u32[]{:S(2)}, u32[]{:S(2)}) collective-permute-start(bf16[128,512]{1,0:T(8,128)(2,1)S(1)} %get-tuple-element.47), channel_id=1, source_target_pairs={{0,1},{1,0},{4,5},{5,4},{8,9},{9,8},{12,13},{13,12},{2,3},{3,2},{6... | collective-permute-start | bytes 393224 | tf_op jit(solution)/shard_map/ppermute | solution.py:589
  26.9 1.4 %collective-permute-start.4 = (bf16[128,512]{1,0:T(8,128)(2,1)S(1)}, bf16[128,512]{1,0:T(8,128)(2,1)S(1)}, u32[]{:S(2)}, u32[]{:S(2)}) collective-permute-start(bf16[128,512]{1,0:T(8,128)(2,1)S(1)} %get-tuple-element.54), channel_id=1, source_target_pairs={{0,5},{1,4},{4,1},{5,0},{8,13},{9,12},{12,9},{13,8},{2,7},{3,6},{6... | collective-permute-start | bytes 393224 | tf_op jit(solution)/shard_map/ppermute | solution.py:589
  28.4 3.6 %templates.3.tspec_ref = f32[4,1152,256]{2,1,0:T(8,128)S(1)} custom-call(s32[8]{0:T(128)S(1)} %copy-done.8, bf16[8,384,384]{2,1,0:T(8,128)(2,1)S(1)} %get-tuple-element.44.bank_ref, bf16[2,144,384]{2,1,0:T(8,128)(2,1)S(1)} %copy-done.6, bf16[4,768,256]{2,1,0:T(8,128)(2,1)S(1)} %copy-done.9), custom_call_target="tpu_custom_call" | custom-call | flops 2491416576 | bytes 7077888 | tf_op jit(solution)/shard_map/templates/pallas_call | solution.py:307
  32.0 1.3 %collective-permute-done.3.rest_4_ = bf16[128,512]{1,0:T(8,128)(2,1)S(1)} collective-permute-done((bf16[128,512]{1,0:T(8,128)(2,1)S(1)}, bf16[128,512]{1,0:T(8,128)(2,1)S(1)}, u32[]{:S(2)}, u32[]{:S(2)}) %collective-permute-start.3) | collective-permute-done | bytes 131104 | tf_op jit(solution)/shard_map/ppermute | solution.py:589
  33.3 2.6 %partials.3 = (bf16[144,512]{1,0:T(8,128)(2,1)S(1)}, bf16[144,512]{1,0:T(8,128)(2,1)S(1)}, bf16[144,512]{1,0:T(8,128)(2,1)S(1)}, bf16[144,512]{1,0:T(8,128)(2,1)S(1)}) custom-call(f32[256,1024]{1,0:T(8,128)S(1)} %copy-done.1, bf16[144,256]{1,0:T(8,128)(2,1)S(1)} %copy-done.2, f32[4,1152,256]{2,1,0:T(8,128)S(1)} %templates.3.tspec_ref, ...), custom_call_target="tpu_custom_call" | custom-call | flops 1811939328 | bytes 2359296 | tf_op jit(solution)/shard_map/partials/pallas_call | solution.py:384
  36.1 0.1 collective-permute-start.5
  36.1 0.1 collective-permute-start.6
  36.2 1.8 %collective-permute-start.7 = (bf16[144,512]{1,0:T(8,128)(2,1)S(1)}, bf16[144,512]{1,0:T(8,128)(2,1)S(1)}, u32[]{:S(2)}, u32[]{:S(2)}) collective-permute-start(bf16[144,512]{1,0:T(8,128)(2,1)S(1)} %get-tuple-element.57), channel_id=1, source_target_pairs={{0,5},{1,4},{4,1},{5,0},{8,13},{9,12},{12,9},{13,8},{2,7},{3,6},{6... | collective-permute-start | bytes 442376 | tf_op jit(solution)/shard_map/ppermute | solution.py:589
  38.0 2.5 %dynamic-slice_bitcast_fusion = (bf16[2,512,512]{2,1,0:T(8,128)(2,1)S(1)}, bf16[2,512,512]{2,1,0:T(8,128)(2,1)S(1)}, bf16[2,512,512]{2,1,0:T(8,128)(2,1)S(1)}, bf16[2,512,512]{2,1,0:T(8,128)(2,1)S(1)}) fusion(bf16[4,2,512,512]{3,2,1,0:T(8,128)(2,1)} %constant.159.clone, s32[]{:T(128)S(6)} %select_n.84, s32[]{:T(128)S(6)} %select_n.76, s32[]{:T(128)S(6)} %select_n.72, ...), kind=kLoop, calls=%fused_computation | loop fusion | bytes 8388624 | tf_op jit(solution)/shard_map/jit(dynamic_index_in_dim)/squeeze | solution.py:603
  40.5 2.4 %collective-permute-done.6.rest_8_ = bf16[144,512]{1,0:T(8,128)(2,1)S(1)} collective-permute-done((bf16[144,512]{1,0:T(8,128)(2,1)S(1)}, bf16[144,512]{1,0:T(8,128)(2,1)S(1)}, u32[]{:S(2)}, u32[]{:S(2)}) %collective-permute-start.6) | collective-permute-done | bytes 147488 | tf_op jit(solution)/shard_map/ppermute | solution.py:589
  42.9 2.3 %collective-permute-done.7.rest_9_ = bf16[144,512]{1,0:T(8,128)(2,1)S(1)} collective-permute-done((bf16[144,512]{1,0:T(8,128)(2,1)S(1)}, bf16[144,512]{1,0:T(8,128)(2,1)S(1)}, u32[]{:S(2)}, u32[]{:S(2)}) %collective-permute-start.7) | collective-permute-done | bytes 147488 | tf_op jit(solution)/shard_map/ppermute | solution.py:589
  45.1 2.4 %columns.3 = (bf16[256,128]{1,0:T(8,128)(2,1)S(1)}, bf16[256,128]{1,0:T(8,128)(2,1)S(1)}) custom-call(f32[2,4]{1,0:T(2,128)S(1)} %copy-done.4, bf16[2,512,512]{2,1,0:T(8,128)(2,1)S(1)} %get-tuple-element.65.rest_0_, bf16[2,512,512]{2,1,0:T(8,128)(2,1)S(1)} %get-tuple-element.62.rest_1_, bf16[128,512]{1,0:T(8,128)(2,1)S(1)} %get-tuple-element.43.rest_2_, ...), custom_call_target="tpu_custom_call" | custom-call | flops 536870912 | bytes 2097152 | tf_op jit(solution)/shard_map/columns/pallas_call | solution.py:480
  47.5 2.3 %collective-permute-start.9 = (bf16[256,128]{1,0:T(8,128)(2,1)S(1)}, bf16[256,128]{1,0:T(8,128)(2,1)S(1)}, u32[]{:S(2)}, u32[]{:S(2)}) collective-permute-start(bf16[256,128]{1,0:T(8,128)(2,1)S(1)} %get-tuple-element.60), channel_id=1, source_target_pairs={{0,8},{4,12},{8,0},{12,4},{1,9},{5,13},{9,1},{13,5},{2,10},{6,14},... | collective-permute-start | bytes 196616 | tf_op jit(solution)/shard_map/ppermute | solution.py:615
  49.8 1.2 %collective-permute-start.10 = (bf16[256,128]{1,0:T(8,128)(2,1)S(1)}, bf16[256,128]{1,0:T(8,128)(2,1)S(1)}, u32[]{:S(2)}, u32[]{:S(2)}) collective-permute-start(bf16[256,128]{1,0:T(8,128)(2,1)S(1)} %get-tuple-element.61), channel_id=1, source_target_pairs={{0,12},{4,8},{8,4},{12,0},{1,13},{5,9},{9,5},{13,1},{2,14},{6,10},... | collective-permute-start | bytes 196616 | tf_op jit(solution)/shard_map/ppermute | solution.py:615
  50.9 2.1 %columns.2 = (bf16[256,128]{1,0:T(8,128)(2,1)S(1)}, bf16[256,128]{1,0:T(8,128)(2,1)S(1)}) custom-call(f32[2,4]{1,0:T(2,128)S(1)} %copy-done.4, bf16[2,512,512]{2,1,0:T(8,128)(2,1)S(1)} %get-tuple-element.64.rest_0_, bf16[2,512,512]{2,1,0:T(8,128)(2,1)S(1)} %get-tuple-element.63.rest_1_, bf16[128,512]{1,0:T(8,128)(2,1)S(1)} %get-tuple-element.43.rest_2_, ...), custom_call_target="tpu_custom_call" | custom-call | flops 536870912 | bytes 2097152 | tf_op jit(solution)/shard_map/columns/pallas_call | solution.py:480
  53.1 0.6 collective-permute-start.8
  53.6 2.6 %collective-permute-done.9.rest_2_ = bf16[256,128]{1,0:T(8,128)(2,1)S(1)} collective-permute-done((bf16[256,128]{1,0:T(8,128)(2,1)S(1)}, bf16[256,128]{1,0:T(8,128)(2,1)S(1)}, u32[]{:S(2)}, u32[]{:S(2)}) %collective-permute-start.9) | collective-permute-done | bytes 65568 | tf_op jit(solution)/shard_map/ppermute | solution.py:615
  56.2 0.5 collective-permute-start.14
  56.7 0.7 %collective-permute-done.8.rest_1_ = bf16[256,128]{1,0:T(8,128)(2,1)S(1)} collective-permute-done((bf16[256,128]{1,0:T(8,128)(2,1)S(1)}, bf16[256,128]{1,0:T(8,128)(2,1)S(1)}, u32[]{:S(2)}, u32[]{:S(2)}) %collective-permute-start.8) | collective-permute-done | bytes 65568 | tf_op jit(solution)/shard_map/ppermute | solution.py:615
  57.4 0.0 collective-permute-done.13.rest_6_
  57.4 0.2 collective-permute-done.14.rest_7_
  57.6 1.1 %collective-permute-done.12.rest_5_ = bf16[256,128]{1,0:T(8,128)(2,1)S(1)} collective-permute-done((bf16[256,128]{1,0:T(8,128)(2,1)S(1)}, bf16[256,128]{1,0:T(8,128)(2,1)S(1)}, u32[]{:S(2)}, u32[]{:S(2)}) %collective-permute-start.12) | collective-permute-done | bytes 65568 | tf_op jit(solution)/shard_map/ppermute | solution.py:616
  58.7 1.3 %unpack.1 = (f32[2,1,512,128]{3,2,1,0:T(8,128)}, f32[2,1,512,128]{3,2,1,0:T(8,128)}) custom-call(bf16[256,128]{1,0:T(8,128)(2,1)S(1)} %get-tuple-element.58.rest_0_, bf16[256,128]{1,0:T(8,128)(2,1)S(1)} %collective-permute-done.8.rest_1_, bf16[256,128]{1,0:T(8,128)(2,1)S(1)} %collective-permute-done.9.rest_2_, ...), custom_call_target="tpu_custom_call" | custom-call | tf_op jit(solution)/shard_map/unpack/pallas_call | solution.py:527
  (29 shorter events, 0.1 us)
Async XLA Ops:
  4.2 19.7 %collective-permute-start = (bf16[128,1024]{1,0:T(8,128)(2,1)}, bf16[128,1024]{1,0:T(8,128)(2,1)S(1)}, u32[]{:S(2)}, u32[]{:S(2)}) collective-permute-start(bf16[128,1024]{1,0:T(8,128)(2,1)} %window_first.1), channel_id=1, source_target_pairs={{0,13},{1,12},{4,9},{5,8},{8,5},{9,4},{12,1},{13,0},{2,15},{3,14},... | collective-permute-start | bytes 786440 | tf_op jit(solution)/shard_map/ppermute | solution.py:567
  9.3 9.0 %copy-start.5 = (bf16[8,384,384]{2,1,0:T(8,128)(2,1)S(1)}, bf16[8,384,384]{2,1,0:T(8,128)(2,1)}, u32[]{:S(2)}) copy-start(bf16[8,384,384]{2,1,0:T(8,128)(2,1)} %bank_ref) | copy-start | bytes 7077892
  9.3 9.0 %copy-start.8 = (s32[8]{0:T(128)S(1)}, s32[8]{0:T(128)}, u32[]{:S(2)}) copy-start(s32[8]{0:T(128)} %index_ref.3) | copy-start | bytes 100
  9.3 9.0 %copy-start.9 = (bf16[4,768,256]{2,1,0:T(8,128)(2,1)S(1)}, bf16[4,768,256]{2,1,0:T(8,128)(2,1)}, u32[]{:S(2)}) copy-start(bf16[4,768,256]{2,1,0:T(8,128)(2,1)} %constant.156.clone.right_ref) | copy-start | bytes 4718596
  18.2 5.7 %copy-start = (bf16[2,4,256,256]{3,2,1,0:T(8,128)(2,1)S(1)}, bf16[2,4,256,256]{3,2,1,0:T(8,128)(2,1)}, u32[]{:S(2)}) copy-start(bf16[2,4,256,256]{3,2,1,0:T(8,128)(2,1)} %constant.153.clone.back_ref) | copy-start | bytes 3145732
  18.2 5.7 %copy-start.1 = (f32[256,1024]{1,0:T(8,128)S(1)}, f32[256,1024]{1,0:T(8,128)}, u32[]{:S(2)}) copy-start(f32[256,1024]{1,0:T(8,128)} %get-tuple-element.37.keep_ref) | copy-start | bytes 3145732
  18.2 5.7 %copy-start.3 = (bf16[128,128]{1,0:T(8,128)(2,1)S(1)}, bf16[128,128]{1,0:T(8,128)(2,1)}, u32[]{:S(2)}) copy-start(bf16[128,128]{1,0:T(8,128)(2,1)} %constant.157.clone.flip_ref) | copy-start | bytes 98308
  18.2 13.8 %collective-permute-start.1 = (bf16[128,1024]{1,0:T(8,128)(2,1)}, bf16[128,1024]{1,0:T(8,128)(2,1)S(1)}, u32[]{:S(2)}, u32[]{:S(2)}) collective-permute-start(bf16[128,1024]{1,0:T(8,128)(2,1)} %get-tuple-element.46), channel_id=1, source_target_pairs={{0,13},{1,12},{4,9},{5,8},{8,5},{9,4},{12,1},{13,0},{2,15},{3,14},... | collective-permute-start | bytes 786440 | tf_op jit(solution)/shard_map/ppermute | solution.py:570
  18.3 1.1 %copy-start.7 = (bf16[2,128,384]{2,1,0:T(8,128)(2,1)S(1)}, bf16[2,128,384]{2,1,0:T(8,128)(2,1)}, u32[]{:S(2)}) copy-start(bf16[2,128,384]{2,1,0:T(8,128)(2,1)} %get-tuple-element.39.left_ref) | copy-start | bytes 589828
  23.8 4.5 %copy-start.6 = (bf16[2,144,384]{2,1,0:T(8,128)(2,1)S(1)}, bf16[2,144,384]{2,1,0:T(8,128)(2,1)}, u32[]{:S(2)}) copy-start(bf16[2,144,384]{2,1,0:T(8,128)(2,1)} %get-tuple-element.45.left_ref) | copy-start | bytes 663556
  26.2 5.8 %collective-permute-start.2 = (bf16[128,512]{1,0:T(8,128)(2,1)S(1)}, bf16[128,512]{1,0:T(8,128)(2,1)S(1)}, u32[]{:S(2)}, u32[]{:S(2)}) collective-permute-start(bf16[128,512]{1,0:T(8,128)(2,1)S(1)} %get-tuple-element.47), channel_id=1, source_target_pairs={{0,1},{1,0},{4,5},{5,4},{8,9},{9,8},{12,13},{13,12},{2,3},{3,2},{6... | collective-permute-start | bytes 393224 | tf_op jit(solution)/shard_map/ppermute | solution.py:589
  26.9 6.4 %collective-permute-start.3 = (bf16[128,512]{1,0:T(8,128)(2,1)S(1)}, bf16[128,512]{1,0:T(8,128)(2,1)S(1)}, u32[]{:S(2)}, u32[]{:S(2)}) collective-permute-start(bf16[128,512]{1,0:T(8,128)(2,1)S(1)} %get-tuple-element.48), channel_id=1, source_target_pairs={{0,4},{1,5},{4,0},{5,1},{8,12},{9,13},{12,8},{13,9},{2,6},{3,7},{6... | collective-permute-start | bytes 393224 | tf_op jit(solution)/shard_map/ppermute | solution.py:589
  26.9 6.4 %copy-start.2 = (bf16[144,256]{1,0:T(8,128)(2,1)S(1)}, bf16[144,256]{1,0:T(8,128)(2,1)}, u32[]{:S(2)}) copy-start(bf16[144,256]{1,0:T(8,128)(2,1)} %constant.158.clone.flip_ref) | copy-start | bytes 221188
  26.9 13.5 %collective-permute-start.4 = (bf16[128,512]{1,0:T(8,128)(2,1)S(1)}, bf16[128,512]{1,0:T(8,128)(2,1)S(1)}, u32[]{:S(2)}, u32[]{:S(2)}) collective-permute-start(bf16[128,512]{1,0:T(8,128)(2,1)S(1)} %get-tuple-element.54), channel_id=1, source_target_pairs={{0,5},{1,4},{4,1},{5,0},{8,13},{9,12},{12,9},{13,8},{2,7},{3,6},{6... | collective-permute-start | bytes 393224 | tf_op jit(solution)/shard_map/ppermute | solution.py:589
  36.1 4.4 %collective-permute-start.5 = (bf16[144,512]{1,0:T(8,128)(2,1)S(1)}, bf16[144,512]{1,0:T(8,128)(2,1)S(1)}, u32[]{:S(2)}, u32[]{:S(2)}) collective-permute-start(bf16[144,512]{1,0:T(8,128)(2,1)S(1)} %get-tuple-element.55), channel_id=1, source_target_pairs={{0,1},{1,0},{4,5},{5,4},{8,9},{9,8},{12,13},{13,12},{2,3},{3,2},{6... | collective-permute-start | bytes 442376 | tf_op jit(solution)/shard_map/ppermute | solution.py:589
  36.1 6.7 %collective-permute-start.6 = (bf16[144,512]{1,0:T(8,128)(2,1)S(1)}, bf16[144,512]{1,0:T(8,128)(2,1)S(1)}, u32[]{:S(2)}, u32[]{:S(2)}) collective-permute-start(bf16[144,512]{1,0:T(8,128)(2,1)S(1)} %get-tuple-element.56), channel_id=1, source_target_pairs={{0,4},{1,5},{4,0},{5,1},{8,12},{9,13},{12,8},{13,9},{2,6},{3,7},{6... | collective-permute-start | bytes 442376 | tf_op jit(solution)/shard_map/ppermute | solution.py:589
  36.2 8.9 %collective-permute-start.7 = (bf16[144,512]{1,0:T(8,128)(2,1)S(1)}, bf16[144,512]{1,0:T(8,128)(2,1)S(1)}, u32[]{:S(2)}, u32[]{:S(2)}) collective-permute-start(bf16[144,512]{1,0:T(8,128)(2,1)S(1)} %get-tuple-element.57), channel_id=1, source_target_pairs={{0,5},{1,4},{4,1},{5,0},{8,13},{9,12},{12,9},{13,8},{2,7},{3,6},{6... | collective-permute-start | bytes 442376 | tf_op jit(solution)/shard_map/ppermute | solution.py:589
  38.0 7.1 %copy-start.4 = (f32[2,4]{1,0:T(2,128)S(1)}, f32[2,4]{1,0:T(2,128)}, u32[]{:S(2)}) copy-start(f32[2,4]{1,0:T(2,128)} %constant.160.clone.roots_ref) | copy-start | bytes 100
  47.5 8.7 %collective-permute-start.9 = (bf16[256,128]{1,0:T(8,128)(2,1)S(1)}, bf16[256,128]{1,0:T(8,128)(2,1)S(1)}, u32[]{:S(2)}, u32[]{:S(2)}) collective-permute-start(bf16[256,128]{1,0:T(8,128)(2,1)S(1)} %get-tuple-element.60), channel_id=1, source_target_pairs={{0,8},{4,12},{8,0},{12,4},{1,9},{5,13},{9,1},{13,5},{2,10},{6,14},... | collective-permute-start | bytes 196616 | tf_op jit(solution)/shard_map/ppermute | solution.py:615
  49.8 6.4 %collective-permute-start.10 = (bf16[256,128]{1,0:T(8,128)(2,1)S(1)}, bf16[256,128]{1,0:T(8,128)(2,1)S(1)}, u32[]{:S(2)}, u32[]{:S(2)}) collective-permute-start(bf16[256,128]{1,0:T(8,128)(2,1)S(1)} %get-tuple-element.61), channel_id=1, source_target_pairs={{0,12},{4,8},{8,4},{12,0},{1,13},{5,9},{9,5},{13,1},{2,14},{6,10},... | collective-permute-start | bytes 196616 | tf_op jit(solution)/shard_map/ppermute | solution.py:615
  53.1 4.4 %collective-permute-start.8 = (bf16[256,128]{1,0:T(8,128)(2,1)S(1)}, bf16[256,128]{1,0:T(8,128)(2,1)S(1)}, u32[]{:S(2)}, u32[]{:S(2)}) collective-permute-start(bf16[256,128]{1,0:T(8,128)(2,1)S(1)} %get-tuple-element.59), channel_id=1, source_target_pairs={{0,4},{4,0},{8,12},{12,8},{1,5},{5,1},{9,13},{13,9},{2,6},{6,2},{1... | collective-permute-start | bytes 196616 | tf_op jit(solution)/shard_map/ppermute | solution.py:615
  53.6 3.8 %collective-permute-start.11 = (bf16[256,128]{1,0:T(8,128)(2,1)S(1)}, bf16[256,128]{1,0:T(8,128)(2,1)S(1)}, u32[]{:S(2)}, u32[]{:S(2)}) collective-permute-start(bf16[256,128]{1,0:T(8,128)(2,1)S(1)} %get-tuple-element.58.rest_0_), channel_id=1, source_target_pairs={{0,1},{1,0},{2,3},{3,2},{4,5},{5,4},{6,7},{7,6},{8,9},{9,8},{10,11... | collective-permute-start | bytes 196616 | tf_op jit(solution)/shard_map/ppermute | solution.py:616
  56.2 1.3 %collective-permute-start.13 = (bf16[256,128]{1,0:T(8,128)(2,1)S(1)}, bf16[256,128]{1,0:T(8,128)(2,1)S(1)}, u32[]{:S(2)}, u32[]{:S(2)}) collective-permute-start(bf16[256,128]{1,0:T(8,128)(2,1)S(1)} %collective-permute-done.9.rest_2_), channel_id=1, source_target_pairs={{0,1},{1,0},{2,3},{3,2},{4,5},{5,4},{6,7},{7,6},{8,9},{9,8},{10,11... | collective-permute-start | bytes 196616 | tf_op jit(solution)/shard_map/ppermute | solution.py:616
  56.2 1.4 %collective-permute-start.14 = (bf16[256,128]{1,0:T(8,128)(2,1)S(1)}, bf16[256,128]{1,0:T(8,128)(2,1)S(1)}, u32[]{:S(2)}, u32[]{:S(2)}) collective-permute-start(bf16[256,128]{1,0:T(8,128)(2,1)S(1)} %collective-permute-done.10.rest_3_), channel_id=1, source_target_pairs={{0,1},{1,0},{2,3},{3,2},{4,5},{5,4},{6,7},{7,6},{8,9},{9,8},{10,11... | collective-permute-start | bytes 196616 | tf_op jit(solution)/shard_map/ppermute | solution.py:616
  57.4 1.3 %collective-permute-start.12 = (bf16[256,128]{1,0:T(8,128)(2,1)S(1)}, bf16[256,128]{1,0:T(8,128)(2,1)S(1)}, u32[]{:S(2)}, u32[]{:S(2)}) collective-permute-start(bf16[256,128]{1,0:T(8,128)(2,1)S(1)} %collective-permute-done.8.rest_1_), channel_id=1, source_target_pairs={{0,1},{1,0},{2,3},{3,2},{4,5},{5,4},{6,7},{7,6},{8,9},{9,8},{10,11... | collective-permute-start | bytes 196616 | tf_op jit(solution)/shard_map/ppermute | solution.py:616

commit v6 on v5

--- a/solution.py
+++ b/solution.py
@@ -349,9 +349,9 @@
             lower.append((product - rounded.astype(jnp.float32)).astype(jnp.bfloat16))
         upper = jnp.concatenate(upper, 0)
         lower = jnp.concatenate(lower, 0)
-        got = jnp.dot(upper, back_ref[0, part], preferred_element_type=jnp.float32)
-        got += jnp.dot(lower, back_ref[0, part], preferred_element_type=jnp.float32)
-        got += jnp.dot(upper, back_ref[1, part], preferred_element_type=jnp.float32)
+        pieces = jnp.concatenate([upper, lower, upper], 1)
+        table = jnp.concatenate([back_ref[0, part], back_ref[0, part], back_ref[1, part]], 0)
+        got = jnp.dot(pieces, table, preferred_element_type=jnp.float32)
         total = got if total is None else total + got
     for o in range(window):
         part_ref[o] = total[o * rows : (o + 1) * rows]

time: 60.2 us -> 59.9 us (level)
  no operation moved by 1% of the time
where the time goes in v6:
time: 59.9 us; the launch traced here: 59.8 us
  Pallas kernels  30.9 us (52%)
  starting transfers between devices  13.2 us (22%)
  waiting for transfers between devices  10.4 us (17%)
  local copies, waits for them, and re-layouts  3.54 us (6%)
  between operations  0.99 us (2%)
  other arithmetic  0.62 us (1%)
    pallas_call x1, Pallas kernels, window_rest(): pl.pallas_call(rest_kernel, out_shape=[jax.ShapeDtypeStruct((rows, ratio...  8.85 us
    pallas_call x2, Pallas kernels, template_spectra(): pl.pallas_call(functools.partial(template_kernel, fresh), out_shape=out_s...  8.07 us
    ppermute x6, waiting for transfers between devices, shards(): got.append(lax.ppermute(parts[s], line, [(i, i ^ s) for i in range(count)]))  5.9 us
    pallas_call x2, Pallas kernels, partials(): pl.pallas_call(functools.partial(partial_kernel, len(others), first), out...  4.7 us
    ppermute x1, starting transfers between devices, shards(): others = [lax.ppermute(sent, line, opposite)]  4.55 us
    pallas_call x2, Pallas kernels, columns(): pl.pallas_call(functools.partial(column_kernel, group_of, scale, share),...  4.49 us
    ppermute x6, starting transfers between devices, shards(): got.append(lax.ppermute(parts[s], line, [(i, i ^ s) for i in range(count)]))  4.09 us
    ppermute x3, starting transfers between devices, shards(): lax.ppermute(maps[s], 'row', [(i, i ^ s) for i in range(classes)])  3.99 us
  transfers between devices with their start and end apart: 15, of which 7 were waited for; matrix products, arithmetic and copies ran while one was open for 5% of the time, Pallas kernels for 40%

profile of v6, /device:TPU:0, one launch (start us, length us, event | category | flops | bytes accessed | tf_op | source)
XLA Modules:
  0.0 59.8 jit_solution(12013444668759932671)
XLA Ops:
  0.6 3.5 %window_first.1 = bf16[128,1024]{1,0:T(8,128)(2,1)} custom-call(bf16[2,2,512,2048]{3,2,1,0:T(8,128)(2,1)} %spec_ref.2, bf16[2,4,512,256]{3,2,1,0:T(8,128)(2,1)} %constant.152.clone.tables_ref.table_ref), custom_call_target="tpu_custom_call" | custom-call | flops 1073741824 | bytes 2097152 | tf_op jit(solution)/shard_map/window_first/pallas_call | solution.py:185
  4.2 4.6 %collective-permute-start = (bf16[128,1024]{1,0:T(8,128)(2,1)}, bf16[128,1024]{1,0:T(8,128)(2,1)S(1)}, u32[]{:S(2)}, u32[]{:S(2)}) collective-permute-start(bf16[128,1024]{1,0:T(8,128)(2,1)} %window_first.1), channel_id=1, source_target_pairs={{0,13},{1,12},{4,9},{5,8},{8,5},{9,4},{12,1},{13,0},{2,15},{3,14},... | collective-permute-start | bytes 786440 | tf_op jit(solution)/shard_map/ppermute | solution.py:567
  8.7 0.6 %pad_add_fusion.place_ref = s32[3]{0:T(128)} fusion(s32[1]{0:T(128)} %bitcast.2, s32[1]{0:T(128)} %bitcast.1, s32[1]{0:T(128)} %bitcast), kind=kLoop, calls=%fused_computation.4 | loop fusion | flops 6 | bytes 24 | tf_op jit(solution)/shard_map/stack | solution.py:230
  9.3 8.8 %window_rest.1 = (bf16[128,1024]{1,0:T(8,128)(2,1)}, f32[256,1024]{1,0:T(8,128)}, bf16[2,128,384]{2,1,0:T(8,128)(2,1)}, bf16[2,144,384]{2,1,0:T(8,128)(2,1)}) custom-call(s32[3]{0:T(128)} %pad_add_fusion.place_ref, bf16[2,2,512,2048]{3,2,1,0:T(8,128)(2,1)} %spec_ref.2, bf16[2,4,512,256]{3,2,1,0:T(8,128)(2,1)} %constant.152.clone.tables_ref.table_ref, ...), custom_call_target="tpu_custom_call" | custom-call | flops 3221225472 | bytes 5242880 | tf_op jit(solution)/shard_map/window_rest/pallas_call | solution.py:237
  18.2 0.0 copy-start.3
  18.2 0.1 collective-permute-start.1
  18.3 1.0 %copy-done.7 = bf16[2,128,384]{2,1,0:T(8,128)(2,1)S(1)} copy-done((bf16[2,128,384]{2,1,0:T(8,128)(2,1)S(1)}, bf16[2,128,384]{2,1,0:T(8,128)(2,1)}, u32[]{:S(2)}) %copy-start.7) | copy-done | bytes 196632
  19.4 4.4 %templates.2 = (f32[4,1024,256]{2,1,0:T(8,128)S(1)}, bf16[8,384,384]{2,1,0:T(8,128)(2,1)S(1)}) custom-call(s32[8]{0:T(128)S(1)} %copy-done.8, bf16[8,384,384]{2,1,0:T(8,128)(2,1)S(1)} %copy-done.5, bf16[2,128,384]{2,1,0:T(8,128)(2,1)S(1)} %copy-done.7, bf16[4,768,256]{2,1,0:T(8,128)(2,1)S(1)} %copy-done.9), custom_call_target="tpu_custom_call" | custom-call | flops 2214592512 | bytes 6553600 | tf_op jit(solution)/shard_map/templates/pallas_call | solution.py:307
  23.9 2.2 %partials.2 = (bf16[128,512]{1,0:T(8,128)(2,1)S(1)}, bf16[128,512]{1,0:T(8,128)(2,1)S(1)}, bf16[128,512]{1,0:T(8,128)(2,1)S(1)}, bf16[128,512]{1,0:T(8,128)(2,1)S(1)}) custom-call(f32[256,1024]{1,0:T(8,128)S(1)} %copy-done.1, bf16[128,128]{1,0:T(8,128)(2,1)S(1)} %copy-done.3, f32[4,1024,256]{2,1,0:T(8,128)S(1)} %get-tuple-element.42.tspec_ref, ...), custom_call_target="tpu_custom_call" | custom-call | flops 1610612736 | bytes 2097152 | tf_op jit(solution)/shard_map/partials/pallas_call | solution.py:384
  26.1 0.7 %collective-permute-start.2 = (bf16[128,512]{1,0:T(8,128)(2,1)S(1)}, bf16[128,512]{1,0:T(8,128)(2,1)S(1)}, u32[]{:S(2)}, u32[]{:S(2)}) collective-permute-start(bf16[128,512]{1,0:T(8,128)(2,1)S(1)} %get-tuple-element.47), channel_id=1, source_target_pairs={{0,1},{1,0},{4,5},{5,4},{8,9},{9,8},{12,13},{13,12},{2,3},{3,2},{6... | collective-permute-start | bytes 393224 | tf_op jit(solution)/shard_map/ppermute | solution.py:589
  26.8 1.4 %collective-permute-start.4 = (bf16[128,512]{1,0:T(8,128)(2,1)S(1)}, bf16[128,512]{1,0:T(8,128)(2,1)S(1)}, u32[]{:S(2)}, u32[]{:S(2)}) collective-permute-start(bf16[128,512]{1,0:T(8,128)(2,1)S(1)} %get-tuple-element.54), channel_id=1, source_target_pairs={{0,5},{1,4},{4,1},{5,0},{8,13},{9,12},{12,9},{13,8},{2,7},{3,6},{6... | collective-permute-start | bytes 393224 | tf_op jit(solution)/shard_map/ppermute | solution.py:589
  28.2 3.6 %templates.3.tspec_ref = f32[4,1152,256]{2,1,0:T(8,128)S(1)} custom-call(s32[8]{0:T(128)S(1)} %copy-done.8, bf16[8,384,384]{2,1,0:T(8,128)(2,1)S(1)} %get-tuple-element.44.bank_ref, bf16[2,144,384]{2,1,0:T(8,128)(2,1)S(1)} %copy-done.6, bf16[4,768,256]{2,1,0:T(8,128)(2,1)S(1)} %copy-done.9), custom_call_target="tpu_custom_call" | custom-call | flops 2491416576 | bytes 7077888 | tf_op jit(solution)/shard_map/templates/pallas_call | solution.py:307
  31.9 1.3 %collective-permute-done.3.rest_4_ = bf16[128,512]{1,0:T(8,128)(2,1)S(1)} collective-permute-done((bf16[128,512]{1,0:T(8,128)(2,1)S(1)}, bf16[128,512]{1,0:T(8,128)(2,1)S(1)}, u32[]{:S(2)}, u32[]{:S(2)}) %collective-permute-start.3) | collective-permute-done | bytes 131104 | tf_op jit(solution)/shard_map/ppermute | solution.py:589
  33.2 2.5 %partials.3 = (bf16[144,512]{1,0:T(8,128)(2,1)S(1)}, bf16[144,512]{1,0:T(8,128)(2,1)S(1)}, bf16[144,512]{1,0:T(8,128)(2,1)S(1)}, bf16[144,512]{1,0:T(8,128)(2,1)S(1)}) custom-call(f32[256,1024]{1,0:T(8,128)S(1)} %copy-done.1, bf16[144,256]{1,0:T(8,128)(2,1)S(1)} %copy-done.2, f32[4,1152,256]{2,1,0:T(8,128)S(1)} %templates.3.tspec_ref, ...), custom_call_target="tpu_custom_call" | custom-call | flops 1811939328 | bytes 2359296 | tf_op jit(solution)/shard_map/partials/pallas_call | solution.py:384
  35.9 0.1 collective-permute-start.5
  35.9 0.1 collective-permute-start.6
  36.0 1.8 %collective-permute-start.7 = (bf16[144,512]{1,0:T(8,128)(2,1)S(1)}, bf16[144,512]{1,0:T(8,128)(2,1)S(1)}, u32[]{:S(2)}, u32[]{:S(2)}) collective-permute-start(bf16[144,512]{1,0:T(8,128)(2,1)S(1)} %get-tuple-element.57), channel_id=1, source_target_pairs={{0,5},{1,4},{4,1},{5,0},{8,13},{9,12},{12,9},{13,8},{2,7},{3,6},{6... | collective-permute-start | bytes 442376 | tf_op jit(solution)/shard_map/ppermute | solution.py:589
  37.8 2.5 %dynamic-slice_bitcast_fusion = (bf16[2,512,512]{2,1,0:T(8,128)(2,1)S(1)}, bf16[2,512,512]{2,1,0:T(8,128)(2,1)S(1)}, bf16[2,512,512]{2,1,0:T(8,128)(2,1)S(1)}, bf16[2,512,512]{2,1,0:T(8,128)(2,1)S(1)}) fusion(bf16[4,2,512,512]{3,2,1,0:T(8,128)(2,1)} %constant.159.clone, s32[]{:T(128)S(6)} %select_n.84, s32[]{:T(128)S(6)} %select_n.76, s32[]{:T(128)S(6)} %select_n.72, ...), kind=kLoop, calls=%fused_computation | loop fusion | bytes 8388624 | tf_op jit(solution)/shard_map/jit(dynamic_index_in_dim)/squeeze | solution.py:603
  40.3 2.4 %collective-permute-done.6.rest_8_ = bf16[144,512]{1,0:T(8,128)(2,1)S(1)} collective-permute-done((bf16[144,512]{1,0:T(8,128)(2,1)S(1)}, bf16[144,512]{1,0:T(8,128)(2,1)S(1)}, u32[]{:S(2)}, u32[]{:S(2)}) %collective-permute-start.6) | collective-permute-done | bytes 147488 | tf_op jit(solution)/shard_map/ppermute | solution.py:589
  42.7 2.3 %collective-permute-done.7.rest_9_ = bf16[144,512]{1,0:T(8,128)(2,1)S(1)} collective-permute-done((bf16[144,512]{1,0:T(8,128)(2,1)S(1)}, bf16[144,512]{1,0:T(8,128)(2,1)S(1)}, u32[]{:S(2)}, u32[]{:S(2)}) %collective-permute-start.7) | collective-permute-done | bytes 147488 | tf_op jit(solution)/shard_map/ppermute | solution.py:589
  44.9 2.4 %columns.3 = (bf16[256,128]{1,0:T(8,128)(2,1)S(1)}, bf16[256,128]{1,0:T(8,128)(2,1)S(1)}) custom-call(f32[2,4]{1,0:T(2,128)S(1)} %copy-done.4, bf16[2,512,512]{2,1,0:T(8,128)(2,1)S(1)} %get-tuple-element.65.rest_0_, bf16[2,512,512]{2,1,0:T(8,128)(2,1)S(1)} %get-tuple-element.62.rest_1_, bf16[128,512]{1,0:T(8,128)(2,1)S(1)} %get-tuple-element.43.rest_2_, ...), custom_call_target="tpu_custom_call" | custom-call | flops 536870912 | bytes 2097152 | tf_op jit(solution)/shard_map/columns/pallas_call | solution.py:480
  47.3 2.3 %collective-permute-start.9 = (bf16[256,128]{1,0:T(8,128)(2,1)S(1)}, bf16[256,128]{1,0:T(8,128)(2,1)S(1)}, u32[]{:S(2)}, u32[]{:S(2)}) collective-permute-start(bf16[256,128]{1,0:T(8,128)(2,1)S(1)} %get-tuple-element.60), channel_id=1, source_target_pairs={{0,8},{4,12},{8,0},{12,4},{1,9},{5,13},{9,1},{13,5},{2,10},{6,14},... | collective-permute-start | bytes 196616 | tf_op jit(solution)/shard_map/ppermute | solution.py:615
  49.6 1.2 %collective-permute-start.10 = (bf16[256,128]{1,0:T(8,128)(2,1)S(1)}, bf16[256,128]{1,0:T(8,128)(2,1)S(1)}, u32[]{:S(2)}, u32[]{:S(2)}) collective-permute-start(bf16[256,128]{1,0:T(8,128)(2,1)S(1)} %get-tuple-element.61), channel_id=1, source_target_pairs={{0,12},{4,8},{8,4},{12,0},{1,13},{5,9},{9,5},{13,1},{2,14},{6,10},... | collective-permute-start | bytes 196616 | tf_op jit(solution)/shard_map/ppermute | solution.py:615
  50.7 2.1 %columns.2 = (bf16[256,128]{1,0:T(8,128)(2,1)S(1)}, bf16[256,128]{1,0:T(8,128)(2,1)S(1)}) custom-call(f32[2,4]{1,0:T(2,128)S(1)} %copy-done.4, bf16[2,512,512]{2,1,0:T(8,128)(2,1)S(1)} %get-tuple-element.64.rest_0_, bf16[2,512,512]{2,1,0:T(8,128)(2,1)S(1)} %get-tuple-element.63.rest_1_, bf16[128,512]{1,0:T(8,128)(2,1)S(1)} %get-tuple-element.43.rest_2_, ...), custom_call_target="tpu_custom_call" | custom-call | flops 536870912 | bytes 2097152 | tf_op jit(solution)/shard_map/columns/pallas_call | solution.py:480
  52.9 0.6 collective-permute-start.8
  53.4 2.6 %collective-permute-done.9.rest_2_ = bf16[256,128]{1,0:T(8,128)(2,1)S(1)} collective-permute-done((bf16[256,128]{1,0:T(8,128)(2,1)S(1)}, bf16[256,128]{1,0:T(8,128)(2,1)S(1)}, u32[]{:S(2)}, u32[]{:S(2)}) %collective-permute-start.9) | collective-permute-done | bytes 65568 | tf_op jit(solution)/shard_map/ppermute | solution.py:615
  56.0 0.5 collective-permute-start.14
  56.5 0.7 %collective-permute-done.8.rest_1_ = bf16[256,128]{1,0:T(8,128)(2,1)S(1)} collective-permute-done((bf16[256,128]{1,0:T(8,128)(2,1)S(1)}, bf16[256,128]{1,0:T(8,128)(2,1)S(1)}, u32[]{:S(2)}, u32[]{:S(2)}) %collective-permute-start.8) | collective-permute-done | bytes 65568 | tf_op jit(solution)/shard_map/ppermute | solution.py:615
  57.2 0.0 collective-permute-done.13.rest_6_
  57.2 0.2 collective-permute-done.14.rest_7_
  57.4 1.1 %collective-permute-done.12.rest_5_ = bf16[256,128]{1,0:T(8,128)(2,1)S(1)} collective-permute-done((bf16[256,128]{1,0:T(8,128)(2,1)S(1)}, bf16[256,128]{1,0:T(8,128)(2,1)S(1)}, u32[]{:S(2)}, u32[]{:S(2)}) %collective-permute-start.12) | collective-permute-done | bytes 65568 | tf_op jit(solution)/shard_map/ppermute | solution.py:616
  58.5 1.3 %unpack.1 = (f32[2,1,512,128]{3,2,1,0:T(8,128)}, f32[2,1,512,128]{3,2,1,0:T(8,128)}) custom-call(bf16[256,128]{1,0:T(8,128)(2,1)S(1)} %get-tuple-element.58.rest_0_, bf16[256,128]{1,0:T(8,128)(2,1)S(1)} %collective-permute-done.8.rest_1_, bf16[256,128]{1,0:T(8,128)(2,1)S(1)} %collective-permute-done.9.rest_2_, ...), custom_call_target="tpu_custom_call" | custom-call | tf_op jit(solution)/shard_map/unpack/pallas_call | solution.py:527
  (29 shorter events, 0.1 us)
Async XLA Ops:
  4.2 19.7 %collective-permute-start = (bf16[128,1024]{1,0:T(8,128)(2,1)}, bf16[128,1024]{1,0:T(8,128)(2,1)S(1)}, u32[]{:S(2)}, u32[]{:S(2)}) collective-permute-start(bf16[128,1024]{1,0:T(8,128)(2,1)} %window_first.1), channel_id=1, source_target_pairs={{0,13},{1,12},{4,9},{5,8},{8,5},{9,4},{12,1},{13,0},{2,15},{3,14},... | collective-permute-start | bytes 786440 | tf_op jit(solution)/shard_map/ppermute | solution.py:567
  9.3 9.0 %copy-start.5 = (bf16[8,384,384]{2,1,0:T(8,128)(2,1)S(1)}, bf16[8,384,384]{2,1,0:T(8,128)(2,1)}, u32[]{:S(2)}) copy-start(bf16[8,384,384]{2,1,0:T(8,128)(2,1)} %bank_ref) | copy-start | bytes 7077892
  9.3 9.0 %copy-start.8 = (s32[8]{0:T(128)S(1)}, s32[8]{0:T(128)}, u32[]{:S(2)}) copy-start(s32[8]{0:T(128)} %index_ref.3) | copy-start | bytes 100
  9.3 9.0 %copy-start.9 = (bf16[4,768,256]{2,1,0:T(8,128)(2,1)S(1)}, bf16[4,768,256]{2,1,0:T(8,128)(2,1)}, u32[]{:S(2)}) copy-start(bf16[4,768,256]{2,1,0:T(8,128)(2,1)} %constant.156.clone.right_ref) | copy-start | bytes 4718596
  18.2 5.7 %copy-start = (bf16[2,4,256,256]{3,2,1,0:T(8,128)(2,1)S(1)}, bf16[2,4,256,256]{3,2,1,0:T(8,128)(2,1)}, u32[]{:S(2)}) copy-start(bf16[2,4,256,256]{3,2,1,0:T(8,128)(2,1)} %constant.153.clone.back_ref) | copy-start | bytes 3145732
  18.2 5.7 %copy-start.1 = (f32[256,1024]{1,0:T(8,128)S(1)}, f32[256,1024]{1,0:T(8,128)}, u32[]{:S(2)}) copy-start(f32[256,1024]{1,0:T(8,128)} %get-tuple-element.37.keep_ref) | copy-start | bytes 3145732
  18.2 5.7 %copy-start.3 = (bf16[128,128]{1,0:T(8,128)(2,1)S(1)}, bf16[128,128]{1,0:T(8,128)(2,1)}, u32[]{:S(2)}) copy-start(bf16[128,128]{1,0:T(8,128)(2,1)} %constant.157.clone.flip_ref) | copy-start | bytes 98308
  18.2 13.7 %collective-permute-start.1 = (bf16[128,1024]{1,0:T(8,128)(2,1)}, bf16[128,1024]{1,0:T(8,128)(2,1)S(1)}, u32[]{:S(2)}, u32[]{:S(2)}) collective-permute-start(bf16[128,1024]{1,0:T(8,128)(2,1)} %get-tuple-element.46), channel_id=1, source_target_pairs={{0,13},{1,12},{4,9},{5,8},{8,5},{9,4},{12,1},{13,0},{2,15},{3,14},... | collective-permute-start | bytes 786440 | tf_op jit(solution)/shard_map/ppermute | solution.py:570
  18.3 1.1 %copy-start.7 = (bf16[2,128,384]{2,1,0:T(8,128)(2,1)S(1)}, bf16[2,128,384]{2,1,0:T(8,128)(2,1)}, u32[]{:S(2)}) copy-start(bf16[2,128,384]{2,1,0:T(8,128)(2,1)} %get-tuple-element.39.left_ref) | copy-start | bytes 589828
  23.8 4.4 %copy-start.6 = (bf16[2,144,384]{2,1,0:T(8,128)(2,1)S(1)}, bf16[2,144,384]{2,1,0:T(8,128)(2,1)}, u32[]{:S(2)}) copy-start(bf16[2,144,384]{2,1,0:T(8,128)(2,1)} %get-tuple-element.45.left_ref) | copy-start | bytes 663556
  26.1 5.8 %collective-permute-start.2 = (bf16[128,512]{1,0:T(8,128)(2,1)S(1)}, bf16[128,512]{1,0:T(8,128)(2,1)S(1)}, u32[]{:S(2)}, u32[]{:S(2)}) collective-permute-start(bf16[128,512]{1,0:T(8,128)(2,1)S(1)} %get-tuple-element.47), channel_id=1, source_target_pairs={{0,1},{1,0},{4,5},{5,4},{8,9},{9,8},{12,13},{13,12},{2,3},{3,2},{6... | collective-permute-start | bytes 393224 | tf_op jit(solution)/shard_map/ppermute | solution.py:589
  26.8 6.4 %collective-permute-start.3 = (bf16[128,512]{1,0:T(8,128)(2,1)S(1)}, bf16[128,512]{1,0:T(8,128)(2,1)S(1)}, u32[]{:S(2)}, u32[]{:S(2)}) collective-permute-start(bf16[128,512]{1,0:T(8,128)(2,1)S(1)} %get-tuple-element.48), channel_id=1, source_target_pairs={{0,4},{1,5},{4,0},{5,1},{8,12},{9,13},{12,8},{13,9},{2,6},{3,7},{6... | collective-permute-start | bytes 393224 | tf_op jit(solution)/shard_map/ppermute | solution.py:589
  26.8 6.4 %copy-start.2 = (bf16[144,256]{1,0:T(8,128)(2,1)S(1)}, bf16[144,256]{1,0:T(8,128)(2,1)}, u32[]{:S(2)}) copy-start(bf16[144,256]{1,0:T(8,128)(2,1)} %constant.158.clone.flip_ref) | copy-start | bytes 221188
  26.8 13.4 %collective-permute-start.4 = (bf16[128,512]{1,0:T(8,128)(2,1)S(1)}, bf16[128,512]{1,0:T(8,128)(2,1)S(1)}, u32[]{:S(2)}, u32[]{:S(2)}) collective-permute-start(bf16[128,512]{1,0:T(8,128)(2,1)S(1)} %get-tuple-element.54), channel_id=1, source_target_pairs={{0,5},{1,4},{4,1},{5,0},{8,13},{9,12},{12,9},{13,8},{2,7},{3,6},{6... | collective-permute-start | bytes 393224 | tf_op jit(solution)/shard_map/ppermute | solution.py:589
  35.9 4.4 %collective-permute-start.5 = (bf16[144,512]{1,0:T(8,128)(2,1)S(1)}, bf16[144,512]{1,0:T(8,128)(2,1)S(1)}, u32[]{:S(2)}, u32[]{:S(2)}) collective-permute-start(bf16[144,512]{1,0:T(8,128)(2,1)S(1)} %get-tuple-element.55), channel_id=1, source_target_pairs={{0,1},{1,0},{4,5},{5,4},{8,9},{9,8},{12,13},{13,12},{2,3},{3,2},{6... | collective-permute-start | bytes 442376 | tf_op jit(solution)/shard_map/ppermute | solution.py:589
  35.9 6.7 %collective-permute-start.6 = (bf16[144,512]{1,0:T(8,128)(2,1)S(1)}, bf16[144,512]{1,0:T(8,128)(2,1)S(1)}, u32[]{:S(2)}, u32[]{:S(2)}) collective-permute-start(bf16[144,512]{1,0:T(8,128)(2,1)S(1)} %get-tuple-element.56), channel_id=1, source_target_pairs={{0,4},{1,5},{4,0},{5,1},{8,12},{9,13},{12,8},{13,9},{2,6},{3,7},{6... | collective-permute-start | bytes 442376 | tf_op jit(solution)/shard_map/ppermute | solution.py:589
  36.0 8.9 %collective-permute-start.7 = (bf16[144,512]{1,0:T(8,128)(2,1)S(1)}, bf16[144,512]{1,0:T(8,128)(2,1)S(1)}, u32[]{:S(2)}, u32[]{:S(2)}) collective-permute-start(bf16[144,512]{1,0:T(8,128)(2,1)S(1)} %get-tuple-element.57), channel_id=1, source_target_pairs={{0,5},{1,4},{4,1},{5,0},{8,13},{9,12},{12,9},{13,8},{2,7},{3,6},{6... | collective-permute-start | bytes 442376 | tf_op jit(solution)/shard_map/ppermute | solution.py:589
  37.8 7.1 %copy-start.4 = (f32[2,4]{1,0:T(2,128)S(1)}, f32[2,4]{1,0:T(2,128)}, u32[]{:S(2)}) copy-start(f32[2,4]{1,0:T(2,128)} %constant.160.clone.roots_ref) | copy-start | bytes 100
  47.3 8.7 %collective-permute-start.9 = (bf16[256,128]{1,0:T(8,128)(2,1)S(1)}, bf16[256,128]{1,0:T(8,128)(2,1)S(1)}, u32[]{:S(2)}, u32[]{:S(2)}) collective-permute-start(bf16[256,128]{1,0:T(8,128)(2,1)S(1)} %get-tuple-element.60), channel_id=1, source_target_pairs={{0,8},{4,12},{8,0},{12,4},{1,9},{5,13},{9,1},{13,5},{2,10},{6,14},... | collective-permute-start | bytes 196616 | tf_op jit(solution)/shard_map/ppermute | solution.py:615
  49.6 6.4 %collective-permute-start.10 = (bf16[256,128]{1,0:T(8,128)(2,1)S(1)}, bf16[256,128]{1,0:T(8,128)(2,1)S(1)}, u32[]{:S(2)}, u32[]{:S(2)}) collective-permute-start(bf16[256,128]{1,0:T(8,128)(2,1)S(1)} %get-tuple-element.61), channel_id=1, source_target_pairs={{0,12},{4,8},{8,4},{12,0},{1,13},{5,9},{9,5},{13,1},{2,14},{6,10},... | collective-permute-start | bytes 196616 | tf_op jit(solution)/shard_map/ppermute | solution.py:615
  52.9 4.4 %collective-permute-start.8 = (bf16[256,128]{1,0:T(8,128)(2,1)S(1)}, bf16[256,128]{1,0:T(8,128)(2,1)S(1)}, u32[]{:S(2)}, u32[]{:S(2)}) collective-permute-start(bf16[256,128]{1,0:T(8,128)(2,1)S(1)} %get-tuple-element.59), channel_id=1, source_target_pairs={{0,4},{4,0},{8,12},{12,8},{1,5},{5,1},{9,13},{13,9},{2,6},{6,2},{1... | collective-permute-start | bytes 196616 | tf_op jit(solution)/shard_map/ppermute | solution.py:615
  53.4 3.8 %collective-permute-start.11 = (bf16[256,128]{1,0:T(8,128)(2,1)S(1)}, bf16[256,128]{1,0:T(8,128)(2,1)S(1)}, u32[]{:S(2)}, u32[]{:S(2)}) collective-permute-start(bf16[256,128]{1,0:T(8,128)(2,1)S(1)} %get-tuple-element.58.rest_0_), channel_id=1, source_target_pairs={{0,1},{1,0},{2,3},{3,2},{4,5},{5,4},{6,7},{7,6},{8,9},{9,8},{10,11... | collective-permute-start | bytes 196616 | tf_op jit(solution)/shard_map/ppermute | solution.py:616
  56.0 1.3 %collective-permute-start.13 = (bf16[256,128]{1,0:T(8,128)(2,1)S(1)}, bf16[256,128]{1,0:T(8,128)(2,1)S(1)}, u32[]{:S(2)}, u32[]{:S(2)}) collective-permute-start(bf16[256,128]{1,0:T(8,128)(2,1)S(1)} %collective-permute-done.9.rest_2_), channel_id=1, source_target_pairs={{0,1},{1,0},{2,3},{3,2},{4,5},{5,4},{6,7},{7,6},{8,9},{9,8},{10,11... | collective-permute-start | bytes 196616 | tf_op jit(solution)/shard_map/ppermute | solution.py:616
  56.0 1.4 %collective-permute-start.14 = (bf16[256,128]{1,0:T(8,128)(2,1)S(1)}, bf16[256,128]{1,0:T(8,128)(2,1)S(1)}, u32[]{:S(2)}, u32[]{:S(2)}) collective-permute-start(bf16[256,128]{1,0:T(8,128)(2,1)S(1)} %collective-permute-done.10.rest_3_), channel_id=1, source_target_pairs={{0,1},{1,0},{2,3},{3,2},{4,5},{5,4},{6,7},{7,6},{8,9},{9,8},{10,11... | collective-permute-start | bytes 196616 | tf_op jit(solution)/shard_map/ppermute | solution.py:616
  57.2 1.3 %collective-permute-start.12 = (bf16[256,128]{1,0:T(8,128)(2,1)S(1)}, bf16[256,128]{1,0:T(8,128)(2,1)S(1)}, u32[]{:S(2)}, u32[]{:S(2)}) collective-permute-start(bf16[256,128]{1,0:T(8,128)(2,1)S(1)} %collective-permute-done.8.rest_1_), channel_id=1, source_target_pairs={{0,1},{1,0},{2,3},{3,2},{4,5},{5,4},{6,7},{7,6},{8,9},{9,8},{10,11... | collective-permute-start | bytes 196616 | tf_op jit(solution)/shard_map/ppermute | solution.py:616

commit v7 on v6

--- a/solution.py
+++ b/solution.py
@@ -437,16 +437,17 @@
         rho = reverse_bits(lax.bitwise_xor(row, group_of[which]), bits(classes))
         sums = [(1 - 2 * (rho % 2)).astype(jnp.float32) * top, 0.0]
         for parity in range(2):
+            blocks = []
             for turn in range(members // cores):
                 angle = rho * turn % classes
                 cos = roots_ref[0, angle].astype(jnp.bfloat16)
                 sin = roots_ref[1, angle].astype(jnp.bfloat16)
-                blocks = []
                 for re, im in planes[parity][turn * cores : (turn + 1) * cores]:
                     blocks += [cos * re - sin * im, sin * re + cos * im] if turn else [re, im]
-                stacked = jnp.concatenate(blocks, 0)
-                got = jnp.dot(tables[which][parity], stacked, preferred_element_type=jnp.float32)
-                sums[parity] = sums[parity] + got[: steps // 2] + got[steps // 2 :]
+            table = jnp.concatenate([tables[which][parity]] * (members // cores), 1)
+            stacked = jnp.concatenate(blocks, 0)
+            got = jnp.dot(table, stacked, preferred_element_type=jnp.float32)
+            sums[parity] = sums[parity] + got[: steps // 2] + got[steps // 2 :]
         corr = jnp.concatenate([sums[0] + sums[1], sums[0] - sums[1]], 0)
         corr = corr * (scale * (1 - 2 * (side * rho % 2)).astype(jnp.float32))
         peak = corr[:, :WCOLS]

time: 59.9 us -> 59.9 us (level)
  no operation moved by 1% of the time
where the time goes in v7:
time: 59.9 us; the launch traced here: 59.8 us
  Pallas kernels  30.9 us (52%)
  starting transfers between devices  13.2 us (22%)
  waiting for transfers between devices  10.4 us (17%)
  local copies, waits for them, and re-layouts  3.54 us (6%)
  between operations  0.99 us (2%)
  other arithmetic  0.62 us (1%)
    pallas_call x1, Pallas kernels, window_rest(): pl.pallas_call(rest_kernel, out_shape=[jax.ShapeDtypeStruct((rows, ratio...  8.85 us
    pallas_call x2, Pallas kernels, template_spectra(): pl.pallas_call(functools.partial(template_kernel, fresh), out_shape=out_s...  8.07 us
    ppermute x6, waiting for transfers between devices, shards(): got.append(lax.ppermute(parts[s], line, [(i, i ^ s) for i in range(count)]))  5.9 us
    pallas_call x2, Pallas kernels, partials(): pl.pallas_call(functools.partial(partial_kernel, len(others), first), out...  4.7 us
    ppermute x1, starting transfers between devices, shards(): others = [lax.ppermute(sent, line, opposite)]  4.55 us
    pallas_call x2, Pallas kernels, columns(): pl.pallas_call(functools.partial(column_kernel, group_of, scale, share),...  4.49 us
    ppermute x6, starting transfers between devices, shards(): got.append(lax.ppermute(parts[s], line, [(i, i ^ s) for i in range(count)]))  4.09 us
    ppermute x3, starting transfers between devices, shards(): lax.ppermute(maps[s], 'row', [(i, i ^ s) for i in range(classes)])  3.99 us
  transfers between devices with their start and end apart: 15, of which 7 were waited for; matrix products, arithmetic and copies ran while one was open for 5% of the time, Pallas kernels for 40%

profile of v7, /device:TPU:0, one launch (start us, length us, event | category | flops | bytes accessed | tf_op | source)
XLA Modules:
  0.0 59.8 jit_solution(8049576042183280631)
XLA Ops:
  0.6 3.5 %window_first.1 = bf16[128,1024]{1,0:T(8,128)(2,1)} custom-call(bf16[2,2,512,2048]{3,2,1,0:T(8,128)(2,1)} %spec_ref.2, bf16[2,4,512,256]{3,2,1,0:T(8,128)(2,1)} %constant.152.clone.tables_ref.table_ref), custom_call_target="tpu_custom_call" | custom-call | flops 1073741824 | bytes 2097152 | tf_op jit(solution)/shard_map/window_first/pallas_call | solution.py:185
  4.2 4.6 %collective-permute-start = (bf16[128,1024]{1,0:T(8,128)(2,1)}, bf16[128,1024]{1,0:T(8,128)(2,1)S(1)}, u32[]{:S(2)}, u32[]{:S(2)}) collective-permute-start(bf16[128,1024]{1,0:T(8,128)(2,1)} %window_first.1), channel_id=1, source_target_pairs={{0,13},{1,12},{4,9},{5,8},{8,5},{9,4},{12,1},{13,0},{2,15},{3,14},... | collective-permute-start | bytes 786440 | tf_op jit(solution)/shard_map/ppermute | solution.py:568
  8.7 0.6 %pad_add_fusion.place_ref = s32[3]{0:T(128)} fusion(s32[1]{0:T(128)} %bitcast.2, s32[1]{0:T(128)} %bitcast.1, s32[1]{0:T(128)} %bitcast), kind=kLoop, calls=%fused_computation.4 | loop fusion | flops 6 | bytes 24 | tf_op jit(solution)/shard_map/stack | solution.py:230
  9.3 8.8 %window_rest.1 = (bf16[128,1024]{1,0:T(8,128)(2,1)}, f32[256,1024]{1,0:T(8,128)}, bf16[2,128,384]{2,1,0:T(8,128)(2,1)}, bf16[2,144,384]{2,1,0:T(8,128)(2,1)}) custom-call(s32[3]{0:T(128)} %pad_add_fusion.place_ref, bf16[2,2,512,2048]{3,2,1,0:T(8,128)(2,1)} %spec_ref.2, bf16[2,4,512,256]{3,2,1,0:T(8,128)(2,1)} %constant.152.clone.tables_ref.table_ref, ...), custom_call_target="tpu_custom_call" | custom-call | flops 3221225472 | bytes 5242880 | tf_op jit(solution)/shard_map/window_rest/pallas_call | solution.py:237
  18.2 0.0 copy-start.3
  18.2 0.1 collective-permute-start.1
  18.3 1.0 %copy-done.7 = bf16[2,128,384]{2,1,0:T(8,128)(2,1)S(1)} copy-done((bf16[2,128,384]{2,1,0:T(8,128)(2,1)S(1)}, bf16[2,128,384]{2,1,0:T(8,128)(2,1)}, u32[]{:S(2)}) %copy-start.7) | copy-done | bytes 196632
  19.4 4.4 %templates.2 = (f32[4,1024,256]{2,1,0:T(8,128)S(1)}, bf16[8,384,384]{2,1,0:T(8,128)(2,1)S(1)}) custom-call(s32[8]{0:T(128)S(1)} %copy-done.8, bf16[8,384,384]{2,1,0:T(8,128)(2,1)S(1)} %copy-done.5, bf16[2,128,384]{2,1,0:T(8,128)(2,1)S(1)} %copy-done.7, bf16[4,768,256]{2,1,0:T(8,128)(2,1)S(1)} %copy-done.9), custom_call_target="tpu_custom_call" | custom-call | flops 2214592512 | bytes 6553600 | tf_op jit(solution)/shard_map/templates/pallas_call | solution.py:307
  23.9 2.2 %partials.2 = (bf16[128,512]{1,0:T(8,128)(2,1)S(1)}, bf16[128,512]{1,0:T(8,128)(2,1)S(1)}, bf16[128,512]{1,0:T(8,128)(2,1)S(1)}, bf16[128,512]{1,0:T(8,128)(2,1)S(1)}) custom-call(f32[256,1024]{1,0:T(8,128)S(1)} %copy-done.1, bf16[128,128]{1,0:T(8,128)(2,1)S(1)} %copy-done.3, f32[4,1024,256]{2,1,0:T(8,128)S(1)} %get-tuple-element.42.tspec_ref, ...), custom_call_target="tpu_custom_call" | custom-call | flops 1610612736 | bytes 2097152 | tf_op jit(solution)/shard_map/partials/pallas_call | solution.py:384
  26.1 0.7 %collective-permute-start.2 = (bf16[128,512]{1,0:T(8,128)(2,1)S(1)}, bf16[128,512]{1,0:T(8,128)(2,1)S(1)}, u32[]{:S(2)}, u32[]{:S(2)}) collective-permute-start(bf16[128,512]{1,0:T(8,128)(2,1)S(1)} %get-tuple-element.47), channel_id=1, source_target_pairs={{0,1},{1,0},{4,5},{5,4},{8,9},{9,8},{12,13},{13,12},{2,3},{3,2},{6... | collective-permute-start | bytes 393224 | tf_op jit(solution)/shard_map/ppermute | solution.py:590
  26.8 1.4 %collective-permute-start.4 = (bf16[128,512]{1,0:T(8,128)(2,1)S(1)}, bf16[128,512]{1,0:T(8,128)(2,1)S(1)}, u32[]{:S(2)}, u32[]{:S(2)}) collective-permute-start(bf16[128,512]{1,0:T(8,128)(2,1)S(1)} %get-tuple-element.54), channel_id=1, source_target_pairs={{0,5},{1,4},{4,1},{5,0},{8,13},{9,12},{12,9},{13,8},{2,7},{3,6},{6... | collective-permute-start | bytes 393224 | tf_op jit(solution)/shard_map/ppermute | solution.py:590
  28.2 3.6 %templates.3.tspec_ref = f32[4,1152,256]{2,1,0:T(8,128)S(1)} custom-call(s32[8]{0:T(128)S(1)} %copy-done.8, bf16[8,384,384]{2,1,0:T(8,128)(2,1)S(1)} %get-tuple-element.44.bank_ref, bf16[2,144,384]{2,1,0:T(8,128)(2,1)S(1)} %copy-done.6, bf16[4,768,256]{2,1,0:T(8,128)(2,1)S(1)} %copy-done.9), custom_call_target="tpu_custom_call" | custom-call | flops 2491416576 | bytes 7077888 | tf_op jit(solution)/shard_map/templates/pallas_call | solution.py:307
  31.9 1.3 %collective-permute-done.3.rest_4_ = bf16[128,512]{1,0:T(8,128)(2,1)S(1)} collective-permute-done((bf16[128,512]{1,0:T(8,128)(2,1)S(1)}, bf16[128,512]{1,0:T(8,128)(2,1)S(1)}, u32[]{:S(2)}, u32[]{:S(2)}) %collective-permute-start.3) | collective-permute-done | bytes 131104 | tf_op jit(solution)/shard_map/ppermute | solution.py:590
  33.2 2.5 %partials.3 = (bf16[144,512]{1,0:T(8,128)(2,1)S(1)}, bf16[144,512]{1,0:T(8,128)(2,1)S(1)}, bf16[144,512]{1,0:T(8,128)(2,1)S(1)}, bf16[144,512]{1,0:T(8,128)(2,1)S(1)}) custom-call(f32[256,1024]{1,0:T(8,128)S(1)} %copy-done.1, bf16[144,256]{1,0:T(8,128)(2,1)S(1)} %copy-done.2, f32[4,1152,256]{2,1,0:T(8,128)S(1)} %templates.3.tspec_ref, ...), custom_call_target="tpu_custom_call" | custom-call | flops 1811939328 | bytes 2359296 | tf_op jit(solution)/shard_map/partials/pallas_call | solution.py:384
  35.9 0.1 collective-permute-start.5
  35.9 0.1 collective-permute-start.6
  36.0 1.8 %collective-permute-start.7 = (bf16[144,512]{1,0:T(8,128)(2,1)S(1)}, bf16[144,512]{1,0:T(8,128)(2,1)S(1)}, u32[]{:S(2)}, u32[]{:S(2)}) collective-permute-start(bf16[144,512]{1,0:T(8,128)(2,1)S(1)} %get-tuple-element.57), channel_id=1, source_target_pairs={{0,5},{1,4},{4,1},{5,0},{8,13},{9,12},{12,9},{13,8},{2,7},{3,6},{6... | collective-permute-start | bytes 442376 | tf_op jit(solution)/shard_map/ppermute | solution.py:590
  37.8 2.5 %dynamic-slice_bitcast_fusion = (bf16[2,512,512]{2,1,0:T(8,128)(2,1)S(1)}, bf16[2,512,512]{2,1,0:T(8,128)(2,1)S(1)}, bf16[2,512,512]{2,1,0:T(8,128)(2,1)S(1)}, bf16[2,512,512]{2,1,0:T(8,128)(2,1)S(1)}) fusion(bf16[4,2,512,512]{3,2,1,0:T(8,128)(2,1)} %constant.159.clone, s32[]{:T(128)S(6)} %select_n.84, s32[]{:T(128)S(6)} %select_n.76, s32[]{:T(128)S(6)} %select_n.72, ...), kind=kLoop, calls=%fused_computation | loop fusion | bytes 8388624 | tf_op jit(solution)/shard_map/jit(dynamic_index_in_dim)/squeeze | solution.py:604
  40.3 2.4 %collective-permute-done.6.rest_8_ = bf16[144,512]{1,0:T(8,128)(2,1)S(1)} collective-permute-done((bf16[144,512]{1,0:T(8,128)(2,1)S(1)}, bf16[144,512]{1,0:T(8,128)(2,1)S(1)}, u32[]{:S(2)}, u32[]{:S(2)}) %collective-permute-start.6) | collective-permute-done | bytes 147488 | tf_op jit(solution)/shard_map/ppermute | solution.py:590
  42.7 2.3 %collective-permute-done.7.rest_9_ = bf16[144,512]{1,0:T(8,128)(2,1)S(1)} collective-permute-done((bf16[144,512]{1,0:T(8,128)(2,1)S(1)}, bf16[144,512]{1,0:T(8,128)(2,1)S(1)}, u32[]{:S(2)}, u32[]{:S(2)}) %collective-permute-start.7) | collective-permute-done | bytes 147488 | tf_op jit(solution)/shard_map/ppermute | solution.py:590
  44.9 2.4 %columns.3 = (bf16[256,128]{1,0:T(8,128)(2,1)S(1)}, bf16[256,128]{1,0:T(8,128)(2,1)S(1)}) custom-call(f32[2,4]{1,0:T(2,128)S(1)} %copy-done.4, bf16[2,512,512]{2,1,0:T(8,128)(2,1)S(1)} %get-tuple-element.65.rest_0_, bf16[2,512,512]{2,1,0:T(8,128)(2,1)S(1)} %get-tuple-element.62.rest_1_, bf16[128,512]{1,0:T(8,128)(2,1)S(1)} %get-tuple-element.43.rest_2_, ...), custom_call_target="tpu_custom_call" | custom-call | flops 536870912 | bytes 2097152 | tf_op jit(solution)/shard_map/columns/pallas_call | solution.py:481
  47.3 2.3 %collective-permute-start.9 = (bf16[256,128]{1,0:T(8,128)(2,1)S(1)}, bf16[256,128]{1,0:T(8,128)(2,1)S(1)}, u32[]{:S(2)}, u32[]{:S(2)}) collective-permute-start(bf16[256,128]{1,0:T(8,128)(2,1)S(1)} %get-tuple-element.60), channel_id=1, source_target_pairs={{0,8},{4,12},{8,0},{12,4},{1,9},{5,13},{9,1},{13,5},{2,10},{6,14},... | collective-permute-start | bytes 196616 | tf_op jit(solution)/shard_map/ppermute | solution.py:616
  49.6 1.2 %collective-permute-start.10 = (bf16[256,128]{1,0:T(8,128)(2,1)S(1)}, bf16[256,128]{1,0:T(8,128)(2,1)S(1)}, u32[]{:S(2)}, u32[]{:S(2)}) collective-permute-start(bf16[256,128]{1,0:T(8,128)(2,1)S(1)} %get-tuple-element.61), channel_id=1, source_target_pairs={{0,12},{4,8},{8,4},{12,0},{1,13},{5,9},{9,5},{13,1},{2,14},{6,10},... | collective-permute-start | bytes 196616 | tf_op jit(solution)/shard_map/ppermute | solution.py:616
  50.7 2.1 %columns.2 = (bf16[256,128]{1,0:T(8,128)(2,1)S(1)}, bf16[256,128]{1,0:T(8,128)(2,1)S(1)}) custom-call(f32[2,4]{1,0:T(2,128)S(1)} %copy-done.4, bf16[2,512,512]{2,1,0:T(8,128)(2,1)S(1)} %get-tuple-element.64.rest_0_, bf16[2,512,512]{2,1,0:T(8,128)(2,1)S(1)} %get-tuple-element.63.rest_1_, bf16[128,512]{1,0:T(8,128)(2,1)S(1)} %get-tuple-element.43.rest_2_, ...), custom_call_target="tpu_custom_call" | custom-call | flops 536870912 | bytes 2097152 | tf_op jit(solution)/shard_map/columns/pallas_call | solution.py:481
  52.9 0.6 collective-permute-start.8
  53.4 2.6 %collective-permute-done.9.rest_2_ = bf16[256,128]{1,0:T(8,128)(2,1)S(1)} collective-permute-done((bf16[256,128]{1,0:T(8,128)(2,1)S(1)}, bf16[256,128]{1,0:T(8,128)(2,1)S(1)}, u32[]{:S(2)}, u32[]{:S(2)}) %collective-permute-start.9) | collective-permute-done | bytes 65568 | tf_op jit(solution)/shard_map/ppermute | solution.py:616
  56.0 0.5 collective-permute-start.14
  56.5 0.7 %collective-permute-done.8.rest_1_ = bf16[256,128]{1,0:T(8,128)(2,1)S(1)} collective-permute-done((bf16[256,128]{1,0:T(8,128)(2,1)S(1)}, bf16[256,128]{1,0:T(8,128)(2,1)S(1)}, u32[]{:S(2)}, u32[]{:S(2)}) %collective-permute-start.8) | collective-permute-done | bytes 65568 | tf_op jit(solution)/shard_map/ppermute | solution.py:616
  57.2 0.0 collective-permute-done.13.rest_6_
  57.2 0.2 collective-permute-done.14.rest_7_
  57.4 1.1 %collective-permute-done.12.rest_5_ = bf16[256,128]{1,0:T(8,128)(2,1)S(1)} collective-permute-done((bf16[256,128]{1,0:T(8,128)(2,1)S(1)}, bf16[256,128]{1,0:T(8,128)(2,1)S(1)}, u32[]{:S(2)}, u32[]{:S(2)}) %collective-permute-start.12) | collective-permute-done | bytes 65568 | tf_op jit(solution)/shard_map/ppermute | solution.py:617
  58.5 1.3 %unpack.1 = (f32[2,1,512,128]{3,2,1,0:T(8,128)}, f32[2,1,512,128]{3,2,1,0:T(8,128)}) custom-call(bf16[256,128]{1,0:T(8,128)(2,1)S(1)} %get-tuple-element.58.rest_0_, bf16[256,128]{1,0:T(8,128)(2,1)S(1)} %collective-permute-done.8.rest_1_, bf16[256,128]{1,0:T(8,128)(2,1)S(1)} %collective-permute-done.9.rest_2_, ...), custom_call_target="tpu_custom_call" | custom-call | tf_op jit(solution)/shard_map/unpack/pallas_call | solution.py:528
  (29 shorter events, 0.1 us)
Async XLA Ops:
  4.2 19.7 %collective-permute-start = (bf16[128,1024]{1,0:T(8,128)(2,1)}, bf16[128,1024]{1,0:T(8,128)(2,1)S(1)}, u32[]{:S(2)}, u32[]{:S(2)}) collective-permute-start(bf16[128,1024]{1,0:T(8,128)(2,1)} %window_first.1), channel_id=1, source_target_pairs={{0,13},{1,12},{4,9},{5,8},{8,5},{9,4},{12,1},{13,0},{2,15},{3,14},... | collective-permute-start | bytes 786440 | tf_op jit(solution)/shard_map/ppermute | solution.py:568
  9.3 9.0 %copy-start.5 = (bf16[8,384,384]{2,1,0:T(8,128)(2,1)S(1)}, bf16[8,384,384]{2,1,0:T(8,128)(2,1)}, u32[]{:S(2)}) copy-start(bf16[8,384,384]{2,1,0:T(8,128)(2,1)} %bank_ref) | copy-start | bytes 7077892
  9.3 9.0 %copy-start.8 = (s32[8]{0:T(128)S(1)}, s32[8]{0:T(128)}, u32[]{:S(2)}) copy-start(s32[8]{0:T(128)} %index_ref.3) | copy-start | bytes 100
  9.3 9.0 %copy-start.9 = (bf16[4,768,256]{2,1,0:T(8,128)(2,1)S(1)}, bf16[4,768,256]{2,1,0:T(8,128)(2,1)}, u32[]{:S(2)}) copy-start(bf16[4,768,256]{2,1,0:T(8,128)(2,1)} %constant.156.clone.right_ref) | copy-start | bytes 4718596
  18.2 5.7 %copy-start = (bf16[2,4,256,256]{3,2,1,0:T(8,128)(2,1)S(1)}, bf16[2,4,256,256]{3,2,1,0:T(8,128)(2,1)}, u32[]{:S(2)}) copy-start(bf16[2,4,256,256]{3,2,1,0:T(8,128)(2,1)} %constant.153.clone.back_ref) | copy-start | bytes 3145732
  18.2 5.7 %copy-start.1 = (f32[256,1024]{1,0:T(8,128)S(1)}, f32[256,1024]{1,0:T(8,128)}, u32[]{:S(2)}) copy-start(f32[256,1024]{1,0:T(8,128)} %get-tuple-element.37.keep_ref) | copy-start | bytes 3145732
  18.2 5.7 %copy-start.3 = (bf16[128,128]{1,0:T(8,128)(2,1)S(1)}, bf16[128,128]{1,0:T(8,128)(2,1)}, u32[]{:S(2)}) copy-start(bf16[128,128]{1,0:T(8,128)(2,1)} %constant.157.clone.flip_ref) | copy-start | bytes 98308
  18.2 13.7 %collective-permute-start.1 = (bf16[128,1024]{1,0:T(8,128)(2,1)}, bf16[128,1024]{1,0:T(8,128)(2,1)S(1)}, u32[]{:S(2)}, u32[]{:S(2)}) collective-permute-start(bf16[128,1024]{1,0:T(8,128)(2,1)} %get-tuple-element.46), channel_id=1, source_target_pairs={{0,13},{1,12},{4,9},{5,8},{8,5},{9,4},{12,1},{13,0},{2,15},{3,14},... | collective-permute-start | bytes 786440 | tf_op jit(solution)/shard_map/ppermute | solution.py:571
  18.3 1.1 %copy-start.7 = (bf16[2,128,384]{2,1,0:T(8,128)(2,1)S(1)}, bf16[2,128,384]{2,1,0:T(8,128)(2,1)}, u32[]{:S(2)}) copy-start(bf16[2,128,384]{2,1,0:T(8,128)(2,1)} %get-tuple-element.39.left_ref) | copy-start | bytes 589828
  23.8 4.4 %copy-start.6 = (bf16[2,144,384]{2,1,0:T(8,128)(2,1)S(1)}, bf16[2,144,384]{2,1,0:T(8,128)(2,1)}, u32[]{:S(2)}) copy-start(bf16[2,144,384]{2,1,0:T(8,128)(2,1)} %get-tuple-element.45.left_ref) | copy-start | bytes 663556
  26.1 5.8 %collective-permute-start.2 = (bf16[128,512]{1,0:T(8,128)(2,1)S(1)}, bf16[128,512]{1,0:T(8,128)(2,1)S(1)}, u32[]{:S(2)}, u32[]{:S(2)}) collective-permute-start(bf16[128,512]{1,0:T(8,128)(2,1)S(1)} %get-tuple-element.47), channel_id=1, source_target_pairs={{0,1},{1,0},{4,5},{5,4},{8,9},{9,8},{12,13},{13,12},{2,3},{3,2},{6... | collective-permute-start | bytes 393224 | tf_op jit(solution)/shard_map/ppermute | solution.py:590
  26.8 6.4 %collective-permute-start.3 = (bf16[128,512]{1,0:T(8,128)(2,1)S(1)}, bf16[128,512]{1,0:T(8,128)(2,1)S(1)}, u32[]{:S(2)}, u32[]{:S(2)}) collective-permute-start(bf16[128,512]{1,0:T(8,128)(2,1)S(1)} %get-tuple-element.48), channel_id=1, source_target_pairs={{0,4},{1,5},{4,0},{5,1},{8,12},{9,13},{12,8},{13,9},{2,6},{3,7},{6... | collective-permute-start | bytes 393224 | tf_op jit(solution)/shard_map/ppermute | solution.py:590
  26.8 6.4 %copy-start.2 = (bf16[144,256]{1,0:T(8,128)(2,1)S(1)}, bf16[144,256]{1,0:T(8,128)(2,1)}, u32[]{:S(2)}) copy-start(bf16[144,256]{1,0:T(8,128)(2,1)} %constant.158.clone.flip_ref) | copy-start | bytes 221188
  26.8 13.4 %collective-permute-start.4 = (bf16[128,512]{1,0:T(8,128)(2,1)S(1)}, bf16[128,512]{1,0:T(8,128)(2,1)S(1)}, u32[]{:S(2)}, u32[]{:S(2)}) collective-permute-start(bf16[128,512]{1,0:T(8,128)(2,1)S(1)} %get-tuple-element.54), channel_id=1, source_target_pairs={{0,5},{1,4},{4,1},{5,0},{8,13},{9,12},{12,9},{13,8},{2,7},{3,6},{6... | collective-permute-start | bytes 393224 | tf_op jit(solution)/shard_map/ppermute | solution.py:590
  35.9 4.4 %collective-permute-start.5 = (bf16[144,512]{1,0:T(8,128)(2,1)S(1)}, bf16[144,512]{1,0:T(8,128)(2,1)S(1)}, u32[]{:S(2)}, u32[]{:S(2)}) collective-permute-start(bf16[144,512]{1,0:T(8,128)(2,1)S(1)} %get-tuple-element.55), channel_id=1, source_target_pairs={{0,1},{1,0},{4,5},{5,4},{8,9},{9,8},{12,13},{13,12},{2,3},{3,2},{6... | collective-permute-start | bytes 442376 | tf_op jit(solution)/shard_map/ppermute | solution.py:590
  35.9 6.7 %collective-permute-start.6 = (bf16[144,512]{1,0:T(8,128)(2,1)S(1)}, bf16[144,512]{1,0:T(8,128)(2,1)S(1)}, u32[]{:S(2)}, u32[]{:S(2)}) collective-permute-start(bf16[144,512]{1,0:T(8,128)(2,1)S(1)} %get-tuple-element.56), channel_id=1, source_target_pairs={{0,4},{1,5},{4,0},{5,1},{8,12},{9,13},{12,8},{13,9},{2,6},{3,7},{6... | collective-permute-start | bytes 442376 | tf_op jit(solution)/shard_map/ppermute | solution.py:590
  36.0 8.9 %collective-permute-start.7 = (bf16[144,512]{1,0:T(8,128)(2,1)S(1)}, bf16[144,512]{1,0:T(8,128)(2,1)S(1)}, u32[]{:S(2)}, u32[]{:S(2)}) collective-permute-start(bf16[144,512]{1,0:T(8,128)(2,1)S(1)} %get-tuple-element.57), channel_id=1, source_target_pairs={{0,5},{1,4},{4,1},{5,0},{8,13},{9,12},{12,9},{13,8},{2,7},{3,6},{6... | collective-permute-start | bytes 442376 | tf_op jit(solution)/shard_map/ppermute | solution.py:590
  37.8 7.1 %copy-start.4 = (f32[2,4]{1,0:T(2,128)S(1)}, f32[2,4]{1,0:T(2,128)}, u32[]{:S(2)}) copy-start(f32[2,4]{1,0:T(2,128)} %constant.160.clone.roots_ref) | copy-start | bytes 100
  47.3 8.7 %collective-permute-start.9 = (bf16[256,128]{1,0:T(8,128)(2,1)S(1)}, bf16[256,128]{1,0:T(8,128)(2,1)S(1)}, u32[]{:S(2)}, u32[]{:S(2)}) collective-permute-start(bf16[256,128]{1,0:T(8,128)(2,1)S(1)} %get-tuple-element.60), channel_id=1, source_target_pairs={{0,8},{4,12},{8,0},{12,4},{1,9},{5,13},{9,1},{13,5},{2,10},{6,14},... | collective-permute-start | bytes 196616 | tf_op jit(solution)/shard_map/ppermute | solution.py:616
  49.6 6.4 %collective-permute-start.10 = (bf16[256,128]{1,0:T(8,128)(2,1)S(1)}, bf16[256,128]{1,0:T(8,128)(2,1)S(1)}, u32[]{:S(2)}, u32[]{:S(2)}) collective-permute-start(bf16[256,128]{1,0:T(8,128)(2,1)S(1)} %get-tuple-element.61), channel_id=1, source_target_pairs={{0,12},{4,8},{8,4},{12,0},{1,13},{5,9},{9,5},{13,1},{2,14},{6,10},... | collective-permute-start | bytes 196616 | tf_op jit(solution)/shard_map/ppermute | solution.py:616
  52.9 4.4 %collective-permute-start.8 = (bf16[256,128]{1,0:T(8,128)(2,1)S(1)}, bf16[256,128]{1,0:T(8,128)(2,1)S(1)}, u32[]{:S(2)}, u32[]{:S(2)}) collective-permute-start(bf16[256,128]{1,0:T(8,128)(2,1)S(1)} %get-tuple-element.59), channel_id=1, source_target_pairs={{0,4},{4,0},{8,12},{12,8},{1,5},{5,1},{9,13},{13,9},{2,6},{6,2},{1... | collective-permute-start | bytes 196616 | tf_op jit(solution)/shard_map/ppermute | solution.py:616
  53.4 3.8 %collective-permute-start.11 = (bf16[256,128]{1,0:T(8,128)(2,1)S(1)}, bf16[256,128]{1,0:T(8,128)(2,1)S(1)}, u32[]{:S(2)}, u32[]{:S(2)}) collective-permute-start(bf16[256,128]{1,0:T(8,128)(2,1)S(1)} %get-tuple-element.58.rest_0_), channel_id=1, source_target_pairs={{0,1},{1,0},{2,3},{3,2},{4,5},{5,4},{6,7},{7,6},{8,9},{9,8},{10,11... | collective-permute-start | bytes 196616 | tf_op jit(solution)/shard_map/ppermute | solution.py:617
  56.0 1.3 %collective-permute-start.13 = (bf16[256,128]{1,0:T(8,128)(2,1)S(1)}, bf16[256,128]{1,0:T(8,128)(2,1)S(1)}, u32[]{:S(2)}, u32[]{:S(2)}) collective-permute-start(bf16[256,128]{1,0:T(8,128)(2,1)S(1)} %collective-permute-done.9.rest_2_), channel_id=1, source_target_pairs={{0,1},{1,0},{2,3},{3,2},{4,5},{5,4},{6,7},{7,6},{8,9},{9,8},{10,11... | collective-permute-start | bytes 196616 | tf_op jit(solution)/shard_map/ppermute | solution.py:617
  56.0 1.4 %collective-permute-start.14 = (bf16[256,128]{1,0:T(8,128)(2,1)S(1)}, bf16[256,128]{1,0:T(8,128)(2,1)S(1)}, u32[]{:S(2)}, u32[]{:S(2)}) collective-permute-start(bf16[256,128]{1,0:T(8,128)(2,1)S(1)} %collective-permute-done.10.rest_3_), channel_id=1, source_target_pairs={{0,1},{1,0},{2,3},{3,2},{4,5},{5,4},{6,7},{7,6},{8,9},{9,8},{10,11... | collective-permute-start | bytes 196616 | tf_op jit(solution)/shard_map/ppermute | solution.py:617
  57.2 1.3 %collective-permute-start.12 = (bf16[256,128]{1,0:T(8,128)(2,1)S(1)}, bf16[256,128]{1,0:T(8,128)(2,1)S(1)}, u32[]{:S(2)}, u32[]{:S(2)}) collective-permute-start(bf16[256,128]{1,0:T(8,128)(2,1)S(1)} %collective-permute-done.8.rest_1_), channel_id=1, source_target_pairs={{0,1},{1,0},{2,3},{3,2},{4,5},{5,4},{6,7},{7,6},{8,9},{9,8},{10,11... | collective-permute-start | bytes 196616 | tf_op jit(solution)/shard_map/ppermute | solution.py:617
